TPU v7x, 32 devices: a whole 2x2x4 slice. The times are simulated.
32 devices in a mesh: groups: 2 (over x), section: 16 (over z, y, core).
Axes of the slice: x: 2, y: 2, z: 4, core: 2. Of those that a mesh axis runs over, the one named last changes fastest.
Arguments:
- micro: bfloat16 [32, 192, 1024], P(('groups', 'section')), parts along dimension 0, may hold values from -6 to 6
- segment: int32 [32, 192], P(('groups', 'section')), parts along dimension 0, may hold values from 0 to 3, as said below
- gain: bfloat16 [16, 1024], P('section'), may hold values from 0.099609375 to 1.8984375
- w_query: bfloat16 [16, 1024, 2048], P('section'), may hold values from -0.1875 to 0.1875
- w_key: bfloat16 [16, 1024, 1024], P('section'), may hold values from -0.1875 to 0.1875
- w_value: bfloat16 [16, 1024, 1024], P('section'), may hold values from -0.1875 to 0.1875
- w_out: bfloat16 [16, 2048, 1024], P('section'), may hold values from -0.125 to 0.125
Outputs:
- result: bfloat16 [32, 192, 1024], P(('groups', 'section')), parts along dimension 0
There are 2 independent parts, one for each index of `groups`. A program takes and returns all parts, laid end to end along the dimension named above; an argument that names none is the same for every part. Nothing has to cross between parts.
Inputs may be any that keep to these rules, and one draw needn't show every extreme that they name: `segment`: in each micro-batch the ids never fall, each of the 4 pairs holds 24 to 96 consecutive tokens, and one pair holds exactly 96.
All inputs are finite; a program needn't handle non-finite values.
Results may differ from a plain program's by a relative error of at most 0.013.
Values may be sent and summed in bfloat16 or wider, within the bound.
No kernel may reach another device: no remote copies, remote signals or barrier semaphores. Data moves between devices by JAX's collectives and lax.ppermute only.
A program may use at most 128 MiB of HBM per device.

v0:
```python
import jax
import jax.numpy as jnp
from jax import lax
from jax.sharding import PartitionSpec as P

HEADS = 16
KV_HEADS = 8
HD = 128
TICKS = 4


def passed_along(array, axis, by):
    length = lax.axis_size(axis)
    return lax.ppermute(array, axis, [(i, (i + by) % length) for i in range(length)])


def positions(pair_ids):
    length = pair_ids.shape[0]
    matched = pair_ids[:, None] == pair_ids[None, :]
    row_index = lax.broadcasted_iota(jnp.int32, (length, length), 0)
    column = lax.broadcasted_iota(jnp.int32, (length, length), 1)
    earlier = matched & (column < row_index)
    places = jnp.sum(earlier.astype(jnp.float32), axis=1)
    allowed = matched & (column <= row_index)
    return (places, allowed)


def rotate(values, places):
    middle = values.shape[2] // 2
    ladder = jnp.arange(middle, dtype=jnp.float32)
    spacing = 1000000.0 ** (-2.0 * ladder / (2 * middle))
    angles = places[:, None, None] * spacing[None, None, :]
    cosine = jnp.cos(angles)
    sine_part = jnp.sin(angles)
    front_part = values[:, :, :middle]
    second = values[:, :, middle:]
    return jnp.concatenate(
        [front_part * cosine - second * sine_part, second * cosine + front_part * sine_part], axis=2
    )


def project(stream, pair_ids, gain_row, wq_layer, wk_layer, wv_layer):
    length = stream.shape[0]
    stream_f = stream.astype(jnp.float32)
    scale = lax.rsqrt(jnp.mean(stream_f * stream_f, axis=1, keepdims=True) + 1e-05)
    normed = (stream_f * scale * gain_row.astype(jnp.float32)[None, :]).astype(jnp.bfloat16)
    places, allowed = positions(pair_ids)
    queries = rotate(
        jnp.dot(normed, wq_layer, preferred_element_type=jnp.float32).reshape(length, HEADS, HD),
        places,
    ).astype(jnp.bfloat16)
    key_rows = rotate(
        jnp.dot(normed, wk_layer, preferred_element_type=jnp.float32).reshape(length, KV_HEADS, HD),
        places,
    ).astype(jnp.bfloat16)
    value_rows = (
        jnp.dot(normed, wv_layer, preferred_element_type=jnp.float32)
        .reshape(length, KV_HEADS, HD)
        .astype(jnp.bfloat16)
    )
    grouped = queries.reshape(length, KV_HEADS, HEADS // KV_HEADS, HD)
    return (grouped, key_rows, value_rows, allowed)


def respond(stream, grouped, key_rows, value_rows, allowed, wo_layer, start, stop):
    scores = jnp.einsum("ikgd,jkd->kgij", grouped, key_rows, preferred_element_type=jnp.float32)
    scores = scores * HD ** (-0.5)
    expo = jnp.where(allowed[None, None], jnp.exp(scores), jnp.zeros_like(scores))
    totals = jnp.sum(expo, axis=3, keepdims=True)
    shares = (expo / totals).astype(jnp.bfloat16)
    mixed = jnp.einsum(
        "kgij,jkd->ikgd", shares, value_rows, preferred_element_type=jnp.float32
    ).astype(jnp.bfloat16)
    mixed = mixed.reshape(stop - start, HEADS * HD)
    update = jnp.dot(mixed, wo_layer, preferred_element_type=jnp.float32)
    return (stream.astype(jnp.float32) + update).astype(jnp.bfloat16)


def body(micro, segment, gain, w_query, w_key, w_value, w_out):
    stream = micro[0]
    pair_ids = segment[0]
    gain_row = gain[0]
    wq_layer = w_query[0]
    wk_layer = w_key[0]
    wv_layer = w_value[0]
    wo_layer = w_out[0]
    length = stream.shape[0]
    for tick_index in range(TICKS):
        grouped, key_rows, value_rows, allowed = project(
            stream, pair_ids, gain_row, wq_layer, wk_layer, wv_layer
        )
        final = tick_index == TICKS - 1
        stream = respond(stream, grouped, key_rows, value_rows, allowed, wo_layer, 0, length)
        if not final:
            stream, pair_ids = passed_along((stream, pair_ids), "section", 1)
    return stream[None]


def solution(mesh):
    in_specs = (
        P(("groups", "section"), None, None),
        P(("groups", "section"), None),
        P("section", None),
        P("section", None, None),
        P("section", None, None),
        P("section", None, None),
        P("section", None, None),
    )
    out_specs = P(("groups", "section"), None, None)
    return jax.shard_map(body, mesh=mesh, in_specs=in_specs, out_specs=out_specs, check_vma=False)
```

profile of v0, /device:TPU:0, one launch (start us, length us, event | category | flops | bytes accessed | tf_op | source)
XLA Modules:
  0.0 134.6 jit_solution(12451186994389322092)
XLA Ops:
  3.0 6.5 %copy.50 = bf16[2048,1024]{1,0:T(8,128)(2,1)} copy(bf16[2048,1024]{0,1:T(8,128)(2,1)} %bitcast.257) | data formatting | bytes 8388608 | tf_op jit(solution)/shard_map/dot_general | solution.py:49
  9.6 4.0 %copy.49 = bf16[1024,1024]{1,0:T(8,128)(2,1)} copy(bf16[1024,1024]{0,1:T(8,128)(2,1)} %bitcast.258) | data formatting | bytes 4194304 | tf_op jit(solution)/shard_map/dot_general | solution.py:53
  13.6 3.8 %fusion.166 = f32[192,16,128]{2,0,1:T(8,128)S(1)} fusion(bf16[16,128,1024]{2,1,0:T(8,128)(2,1)} %bitcast.249, bf16[1,192,1024]{2,1,0:T(8,128)(2,1)S(1)} %copy-done.8, f32[1024]{0:T(1024)S(1)} %bitcast.267, f32[192]{0:T(256)S(1)} %add_rsqrt_fusion.3), kind=kOutput, calls=%fused_computation.175 | convolution fusion | flops 806092800 | bytes 6165248 | tf_op jit(solution)/shard_map/dot_general | solution.py:49
  18.4 2.6 %collective-permute-start.3 = (s32[192]{0:T(256)S(1)}, s32[192]{0:T(256)S(1)}, u32[]{:S(2)}, u32[]{:S(2)}) collective-permute-start(s32[192]{0:T(256)S(1)} %collective-permute-done.1), channel_id=1, source_target_pairs={{0,1},{1,2},{2,3},{3,4},{4,5},{5,6},{6,7},{7,8},{8,9},{9,10},{10,1... | collective-permute-start | bytes 2312 | tf_op jit(solution)/shard_map/ppermute | solution.py:14
  21.0 3.6 %collective-permute-done.3 = s32[192]{0:T(256)S(1)} collective-permute-done((s32[192]{0:T(256)S(1)}, s32[192]{0:T(256)S(1)}, u32[]{:S(2)}, u32[]{:S(2)}) %collective-permute-start.3) | collective-permute-done | bytes 800 | tf_op jit(solution)/shard_map/ppermute | solution.py:14
  24.8 5.6 %collective-permute-done.5 = s32[192]{0:T(256)S(1)} collective-permute-done((s32[192]{0:T(256)S(1)}, s32[192]{0:T(256)S(1)}, u32[]{:S(2)}, u32[]{:S(2)}) %collective-permute-start.5) | collective-permute-done | bytes 800 | tf_op jit(solution)/shard_map/ppermute | solution.py:14
  30.5 2.1 %multiply_cosine_fusion = (f32[192,64]{1,0:T(8,128)S(1)}, f32[192,64]{1,0:T(8,128)S(1)}, f32[192,64]{1,0:T(8,128)}, f32[192,64]{1,0:T(8,128)}, f32[192,64]{1,0:T...) fusion(f32[192]{0:T(256)S(1)} %convert_reduce_fusion, f32[64]{0:T(128)S(1)} %multiply_power_fusion, ...), kind=kLoop, calls=%fused_computation.145 | loop fusion | flops 49152 | bytes 396544 | tf_op jit(solution)/shard_map/cos | solution.py:33
  33.5 2.9 %fusion.8 = (f32[8,2,192]{2,1,0:T(2,128)S(1)}, f32[8,192,192,2]{2,1,3,0:T(8,128)}) fusion(pred[192,192]{0,1:T(8,128)(4,1)S(1)} %compare_and_fusion.7, bf16[192,8,2,64]{3,0,2,1:T(8,128)(2,1)S(1)} %bitcast.260, bf16[192,8,2,64]{3,0,2,1:T(8,128)(2,1)S(1)} %bitcast.259, bf16[192,8,64]{2,0,1:T(8,128)(2,1)S(1)} %get-tuple-element.20, ...), kind=kOutput, calls=%fused_computation.16 | convolution fusion | flops 155120640 | bytes 3588096 | tf_op jit(solution)/shard_map/ikgd,jkd->kgij/dot_general | solution.py:66
  36.5 4.2 %fusion.32 = bf16[192,8,2,128]{3,0,2,1:T(8,128)(2,1)} fusion(f32[8,192,192,2]{2,1,3,0:T(8,128)} %get-tuple-element.36, f32[8,2,192]{2,1,0:T(2,128)S(1)} %get-tuple-element.35, pred[192,192]{0,1:T(8,128)(4,1)S(1)} %compare_and_fusion.7, bf16[1,192,1024]{2,1,0:T(8,128)(2,1)S(1)} %copy-done.8, f32[1024]{0:T(1024)S(1)} %bitcast.269, ...), kind=kOutput, calls=%fused_computation.48 | convolution fusion | flops 557383680 | bytes 5690112 | tf_op jit(solution)/shard_map/kgij,jkd->ikgd/dot_general | solution.py:71
  40.6 1.9 %copy.23 = bf16[192,8,2,128]{3,2,1,0:T(2,128)(2,1)S(1)} copy(bf16[192,8,2,128]{3,0,2,1:T(8,128)(2,1)} %fusion.32) | data formatting | bytes 1572864 | tf_op jit(solution)/shard_map/convert_element_type | solution.py:73
  42.6 1.5 %reshape.486 = bf16[192,2048]{1,0:T(8,128)(2,1)} reshape(bf16[192,8,2,128]{3,2,1,0:T(2,128)(2,1)S(1)} %copy.23) | data formatting | bytes 1572864 | tf_op jit(solution)/shard_map/reshape | solution.py:74
  44.1 3.6 %fusion.57 = bf16[192,1024]{1,0:T(8,128)(2,1)S(1)} fusion(bf16[192,2048]{1,0:T(8,128)(2,1)} %reshape.486, bf16[1,2048,1024]{2,1,0:T(8,128)(2,1)} %param.13, bf16[1,192,1024]{2,1,0:T(8,128)(2,1)S(1)} %copy-done.8), kind=kOutput, calls=%fused_computation.59 | convolution fusion | flops 805896192 | bytes 5767168 | tf_op jit(solution)/shard_map/dot_general | solution.py:75
  48.0 9.8 %collective-permute-done = bf16[192,1024]{1,0:T(8,128)(2,1)S(1)} collective-permute-done((bf16[192,1024]{1,0:T(8,128)(2,1)S(1)}, bf16[192,1024]{1,0:T(8,128)(2,1)S(1)}, u32[]{:S(2)}, u32[]{:S(2)}) %collective-permute-start) | collective-permute-done | bytes 393248 | tf_op jit(solution)/shard_map/ppermute | solution.py:14
  60.1 1.5 %fusion.136 = f32[192,16,128]{2,0,1:T(8,128)S(1)} fusion(bf16[16,128,1024]{2,1,0:T(8,128)(2,1)S(1)} %bitcast.250, bf16[192,1024]{1,0:T(8,128)(2,1)S(1)} %collective-permute-done, f32[1024]{0:T(1024)S(1)} %bitcast.271, f32[192]{0:T(256)S(1)} %add_rsqrt_fusion.2), kind=kOutput, calls=%fused_computation.152 | convolution fusion | flops 806092800 | bytes 6165248 | tf_op jit(solution)/shard_map/dot_general | solution.py:49
  62.3 2.9 %fusion.9 = (f32[8,2,192]{2,1,0:T(2,128)S(1)}, f32[8,192,192,2]{2,1,3,0:T(8,128)}) fusion(pred[192,192]{0,1:T(8,128)(4,1)S(1)} %compare_and_fusion.5, bf16[192,8,2,64]{3,0,2,1:T(8,128)(2,1)S(1)} %bitcast.262, bf16[192,8,2,64]{3,0,2,1:T(8,128)(2,1)S(1)} %bitcast.261, bf16[192,8,64]{2,0,1:T(8,128)(2,1)S(1)} %get-tuple-element.18, ...), kind=kOutput, calls=%fused_computation.17 | convolution fusion | flops 155120640 | bytes 3588096 | tf_op jit(solution)/shard_map/ikgd,jkd->kgij/dot_general | solution.py:66
  65.2 4.2 %fusion.33 = bf16[192,8,2,128]{3,0,2,1:T(8,128)(2,1)} fusion(f32[8,192,192,2]{2,1,3,0:T(8,128)} %get-tuple-element.38, f32[8,2,192]{2,1,0:T(2,128)S(1)} %get-tuple-element.37, pred[192,192]{0,1:T(8,128)(4,1)S(1)} %compare_and_fusion.5, bf16[192,1024]{1,0:T(8,128)(2,1)S(1)} %collective-permute-done, f32[1024]{0:T(1024)S(1)} %bitcast.272, ...), kind=kOutput, calls=%fused_computation.49 | convolution fusion | flops 557383680 | bytes 5690112 | tf_op jit(solution)/shard_map/kgij,jkd->ikgd/dot_general | solution.py:71
  69.4 1.9 %copy.27 = bf16[192,8,2,128]{3,2,1,0:T(2,128)(2,1)S(1)} copy(bf16[192,8,2,128]{3,0,2,1:T(8,128)(2,1)} %fusion.33) | data formatting | bytes 1572864 | tf_op jit(solution)/shard_map/convert_element_type | solution.py:73
  71.3 1.5 %reshape.487 = bf16[192,2048]{1,0:T(8,128)(2,1)} reshape(bf16[192,8,2,128]{3,2,1,0:T(2,128)(2,1)S(1)} %copy.27) | data formatting | bytes 1572864 | tf_op jit(solution)/shard_map/reshape | solution.py:74
  72.8 3.6 %fusion.54 = bf16[192,1024]{1,0:T(8,128)(2,1)S(1)} fusion(bf16[192,2048]{1,0:T(8,128)(2,1)} %reshape.487, bf16[1,2048,1024]{2,1,0:T(8,128)(2,1)} %param.13, bf16[192,1024]{1,0:T(8,128)(2,1)S(1)} %collective-permute-done), kind=kOutput, calls=%fused_computation.58 | convolution fusion | flops 805896192 | bytes 5767168 | tf_op jit(solution)/shard_map/dot_general | solution.py:75
  76.8 9.8 %collective-permute-done.2 = bf16[192,1024]{1,0:T(8,128)(2,1)S(1)} collective-permute-done((bf16[192,1024]{1,0:T(8,128)(2,1)S(1)}, bf16[192,1024]{1,0:T(8,128)(2,1)S(1)}, u32[]{:S(2)}, u32[]{:S(2)}) %collective-permute-start.2) | collective-permute-done | bytes 393248 | tf_op jit(solution)/shard_map/ppermute | solution.py:14
  88.9 1.5 %fusion.142 = f32[192,16,128]{2,0,1:T(8,128)S(1)} fusion(bf16[16,128,1024]{2,1,0:T(8,128)(2,1)S(1)} %bitcast.251, bf16[192,1024]{1,0:T(8,128)(2,1)S(1)} %collective-permute-done.2, f32[192]{0:T(256)S(1)} %add_rsqrt_fusion.1, f32[1024]{0:T(1024)S(1)} %bitcast.274), kind=kOutput, calls=%fused_computation.154 | convolution fusion | flops 806092800 | bytes 6165248 | tf_op jit(solution)/shard_map/dot_general | solution.py:49
  91.1 2.9 %fusion.10 = (f32[8,2,192]{2,1,0:T(2,128)S(1)}, f32[8,192,192,2]{2,1,3,0:T(8,128)}) fusion(pred[192,192]{0,1:T(8,128)(4,1)S(1)} %compare_and_fusion.3, bf16[192,8,2,64]{3,0,2,1:T(8,128)(2,1)S(1)} %bitcast.264, bf16[192,8,2,64]{3,0,2,1:T(8,128)(2,1)S(1)} %bitcast.263, bf16[192,8,64]{2,0,1:T(8,128)(2,1)S(1)} %get-tuple-element.16, ...), kind=kOutput, calls=%fused_computation.18 | convolution fusion | flops 155120640 | bytes 3588096 | tf_op jit(solution)/shard_map/ikgd,jkd->kgij/dot_general | solution.py:66
  94.0 4.2 %fusion.34 = bf16[192,8,2,128]{3,0,2,1:T(8,128)(2,1)} fusion(f32[8,192,192,2]{2,1,3,0:T(8,128)} %get-tuple-element.40, f32[8,2,192]{2,1,0:T(2,128)S(1)} %get-tuple-element.39, pred[192,192]{0,1:T(8,128)(4,1)S(1)} %compare_and_fusion.3, bf16[192,1024]{1,0:T(8,128)(2,1)S(1)} %collective-permute-done.2, f32[192]{0:T(256)S(1)} %add_rsqrt_fusion.1, ...), kind=kOutput, calls=%fused_computation.50 | convolution fusion | flops 557383680 | bytes 5690112 | tf_op jit(solution)/shard_map/kgij,jkd->ikgd/dot_general | solution.py:71
  98.2 1.9 %copy.31 = bf16[192,8,2,128]{3,2,1,0:T(2,128)(2,1)S(1)} copy(bf16[192,8,2,128]{3,0,2,1:T(8,128)(2,1)} %fusion.34) | data formatting | bytes 1572864 | tf_op jit(solution)/shard_map/convert_element_type | solution.py:73
  100.1 1.5 %reshape.488 = bf16[192,2048]{1,0:T(8,128)(2,1)} reshape(bf16[192,8,2,128]{3,2,1,0:T(2,128)(2,1)S(1)} %copy.31) | data formatting | bytes 1572864 | tf_op jit(solution)/shard_map/reshape | solution.py:74
  101.6 3.6 %fusion.51 = bf16[192,1024]{1,0:T(8,128)(2,1)S(1)} fusion(bf16[192,2048]{1,0:T(8,128)(2,1)} %reshape.488, bf16[1,2048,1024]{2,1,0:T(8,128)(2,1)} %param.13, bf16[192,1024]{1,0:T(8,128)(2,1)S(1)} %collective-permute-done.2), kind=kOutput, calls=%fused_computation.57 | convolution fusion | flops 805896192 | bytes 5767168 | tf_op jit(solution)/shard_map/dot_general | solution.py:75
  105.6 9.8 %collective-permute-done.4 = bf16[192,1024]{1,0:T(8,128)(2,1)S(1)} collective-permute-done((bf16[192,1024]{1,0:T(8,128)(2,1)S(1)}, bf16[192,1024]{1,0:T(8,128)(2,1)S(1)}, u32[]{:S(2)}, u32[]{:S(2)}) %collective-permute-start.4) | collective-permute-done | bytes 393248 | tf_op jit(solution)/shard_map/ppermute | solution.py:14
  117.8 1.5 %fusion.148 = f32[192,16,128]{2,0,1:T(8,128)S(1)} fusion(bf16[16,128,1024]{2,1,0:T(8,128)(2,1)S(1)} %bitcast.252, bf16[192,1024]{1,0:T(8,128)(2,1)S(1)} %collective-permute-done.4, f32[192]{0:T(256)S(1)} %add_rsqrt_fusion, f32[1024]{0:T(1024)S(1)} %bitcast.277), kind=kOutput, calls=%fused_computation.156 | convolution fusion | flops 806092800 | bytes 6165248 | tf_op jit(solution)/shard_map/dot_general | solution.py:49
  119.9 2.9 %fusion.11 = (f32[8,2,192]{2,1,0:T(2,128)S(1)}, f32[8,192,192,2]{2,1,3,0:T(8,128)}) fusion(pred[192,192]{0,1:T(8,128)(4,1)S(1)} %compare_and_fusion.1, bf16[192,8,2,64]{3,0,2,1:T(8,128)(2,1)S(1)} %bitcast.266, bf16[192,8,2,64]{3,0,2,1:T(8,128)(2,1)S(1)} %bitcast.265, bf16[192,8,64]{2,0,1:T(8,128)(2,1)S(1)} %get-tuple-element.14, ...), kind=kOutput, calls=%fused_computation.19 | convolution fusion | flops 155120640 | bytes 3588096 | tf_op jit(solution)/shard_map/ikgd,jkd->kgij/dot_general | solution.py:66
  122.8 4.1 %fusion.35 = bf16[192,8,2,128]{3,0,2,1:T(8,128)(2,1)} fusion(f32[8,192,192,2]{2,1,3,0:T(8,128)} %get-tuple-element.42, f32[8,2,192]{2,1,0:T(2,128)S(1)} %get-tuple-element.41, pred[192,192]{0,1:T(8,128)(4,1)S(1)} %compare_and_fusion.1, bf16[192,1024]{1,0:T(8,128)(2,1)S(1)} %collective-permute-done.4, f32[192]{0:T(256)S(1)} %add_rsqrt_fusion, ...), kind=kOutput, calls=%fused_computation.51 | convolution fusion | flops 557383680 | bytes 5690112 | tf_op jit(solution)/shard_map/kgij,jkd->ikgd/dot_general | solution.py:71
  127.0 1.9 %copy.35 = bf16[192,8,2,128]{3,2,1,0:T(2,128)(2,1)S(1)} copy(bf16[192,8,2,128]{3,0,2,1:T(8,128)(2,1)} %fusion.35) | data formatting | bytes 1572864 | tf_op jit(solution)/shard_map/convert_element_type | solution.py:73
  130.4 4.2 %fusion.84 = bf16[1,192,1024]{2,1,0:T(8,128)(2,1)} fusion(bf16[192,2048]{1,0:T(8,128)(2,1)} %reshape.489, bf16[1,2048,1024]{2,1,0:T(8,128)(2,1)} %param.13, bf16[192,1024]{1,0:T(8,128)(2,1)S(1)} %collective-permute-done.4), kind=kOutput, calls=%fused_computation.68 | convolution fusion | flops 805896192 | bytes 5767168 | tf_op jit(solution)/shard_map/dot_general | solution.py:75
  (63 shorter events, 16.8 us)
Async XLA Ops:
  0.0 36.5 %copy-start = (bf16[1,1024,1024]{2,1,0:T(8,128)(2,1)S(1)}, bf16[1,1024,1024]{2,1,0:T(8,128)(2,1)}, u32[]{:S(2)}) copy-start(bf16[1,1024,1024]{2,1,0:T(8,128)(2,1)} %param.12) | copy-start | bytes 6291460
  0.0 18.4 %collective-permute-start.1 = (s32[192]{0:T(256)}, s32[192]{0:T(256)S(1)}, u32[]{:S(2)}, u32[]{:S(2)}) collective-permute-start(s32[192]{0:T(256)} %bitcast.279), channel_id=1, source_target_pairs={{0,1},{1,2},{2,3},{3,4},{4,5},{5,6},{6,7},{7,8},{8,9},{9,10},{10,1... | collective-permute-start | bytes 2312 | tf_op jit(solution)/shard_map/ppermute | solution.py:14
  3.0 6.5 %copy-start.8 = (bf16[1,192,1024]{2,1,0:T(8,128)(2,1)S(1)}, bf16[1,192,1024]{2,1,0:T(8,128)(2,1)}, u32[]{:S(2)}) copy-start(bf16[1,192,1024]{2,1,0:T(8,128)(2,1)} %param.7) | copy-start | bytes 1179652
  13.6 3.9 %copy-start.4 = (bf16[1024,1024]{1,0:T(8,128)(2,1)S(1)}, bf16[1024,1024]{1,0:T(8,128)(2,1)}, u32[]{:S(2)}) copy-start(bf16[1024,1024]{1,0:T(8,128)(2,1)} %copy.49) | copy-start | bytes 6291460
  18.4 6.3 %collective-permute-start.3 = (s32[192]{0:T(256)S(1)}, s32[192]{0:T(256)S(1)}, u32[]{:S(2)}, u32[]{:S(2)}) collective-permute-start(s32[192]{0:T(256)S(1)} %collective-permute-done.1), channel_id=1, source_target_pairs={{0,1},{1,2},{2,3},{3,4},{4,5},{5,6},{6,7},{7,8},{8,9},{9,10},{10,1... | collective-permute-start | bytes 2312 | tf_op jit(solution)/shard_map/ppermute | solution.py:14
  24.7 5.7 %collective-permute-start.5 = (s32[192]{0:T(256)S(1)}, s32[192]{0:T(256)S(1)}, u32[]{:S(2)}, u32[]{:S(2)}) collective-permute-start(s32[192]{0:T(256)S(1)} %collective-permute-done.3), channel_id=1, source_target_pairs={{0,1},{1,2},{2,3},{3,4},{4,5},{5,6},{6,7},{7,8},{8,9},{9,10},{10,1... | collective-permute-start | bytes 2312 | tf_op jit(solution)/shard_map/ppermute | solution.py:14
  44.1 13.9 %copy-start.5 = (bf16[1024,1024]{1,0:T(8,128)(2,1)S(1)}, bf16[1024,1024]{1,0:T(8,128)(2,1)}, u32[]{:S(2)}) copy-start(bf16[1024,1024]{1,0:T(8,128)(2,1)} %copy.49) | copy-start | bytes 6291460
  47.6 11.2 %copy-start.11 = (f32[192,64]{1,0:T(8,128)S(1)}, f32[192,64]{1,0:T(8,128)}, u32[]{:S(2)}) copy-start(f32[192,64]{1,0:T(8,128)} %get-tuple-element.29) | copy-start | bytes 147460
  47.6 11.2 %copy-start.12 = (f32[192,64]{1,0:T(8,128)S(1)}, f32[192,64]{1,0:T(8,128)}, u32[]{:S(2)}) copy-start(f32[192,64]{1,0:T(8,128)} %get-tuple-element.30) | copy-start | bytes 147460
  47.6 10.1 %collective-permute-start = (bf16[192,1024]{1,0:T(8,128)(2,1)S(1)}, bf16[192,1024]{1,0:T(8,128)(2,1)S(1)}, u32[]{:S(2)}, u32[]{:S(2)}) collective-permute-start(bf16[192,1024]{1,0:T(8,128)(2,1)S(1)} %fusion.57), channel_id=1, source_target_pairs={{0,1},{1,2},{2,3},{3,4},{4,5},{5,6},{6,7},{7,8},{8,9},{9,10},{10,1... | collective-permute-start | bytes 1179656 | tf_op jit(solution)/shard_map/ppermute | solution.py:14
  58.0 2.2 %copy-start.1 = (bf16[2048,1024]{1,0:T(8,128)(2,1)S(1)}, bf16[2048,1024]{1,0:T(8,128)(2,1)}, u32[]{:S(2)}) copy-start(bf16[2048,1024]{1,0:T(8,128)(2,1)} %copy.50) | copy-start | bytes 12582916
  72.8 13.9 %copy-start.6 = (bf16[1024,1024]{1,0:T(8,128)(2,1)S(1)}, bf16[1024,1024]{1,0:T(8,128)(2,1)}, u32[]{:S(2)}) copy-start(bf16[1024,1024]{1,0:T(8,128)(2,1)} %copy.49) | copy-start | bytes 6291460
  76.4 11.3 %copy-start.9 = (f32[192,64]{1,0:T(8,128)S(1)}, f32[192,64]{1,0:T(8,128)}, u32[]{:S(2)}) copy-start(f32[192,64]{1,0:T(8,128)} %get-tuple-element.31) | copy-start | bytes 147460
  76.4 11.3 %copy-start.10 = (f32[192,64]{1,0:T(8,128)S(1)}, f32[192,64]{1,0:T(8,128)}, u32[]{:S(2)}) copy-start(f32[192,64]{1,0:T(8,128)} %get-tuple-element.32) | copy-start | bytes 147460
  76.4 10.2 %collective-permute-start.2 = (bf16[192,1024]{1,0:T(8,128)(2,1)S(1)}, bf16[192,1024]{1,0:T(8,128)(2,1)S(1)}, u32[]{:S(2)}, u32[]{:S(2)}) collective-permute-start(bf16[192,1024]{1,0:T(8,128)(2,1)S(1)} %fusion.54), channel_id=1, source_target_pairs={{0,1},{1,2},{2,3},{3,4},{4,5},{5,6},{6,7},{7,8},{8,9},{9,10},{10,1... | collective-permute-start | bytes 1179656 | tf_op jit(solution)/shard_map/ppermute | solution.py:14
  86.8 2.2 %copy-start.2 = (bf16[2048,1024]{1,0:T(8,128)(2,1)S(1)}, bf16[2048,1024]{1,0:T(8,128)(2,1)}, u32[]{:S(2)}) copy-start(bf16[2048,1024]{1,0:T(8,128)(2,1)} %copy.50) | copy-start | bytes 12582916
  101.6 13.9 %copy-start.7 = (bf16[1024,1024]{1,0:T(8,128)(2,1)S(1)}, bf16[1024,1024]{1,0:T(8,128)(2,1)}, u32[]{:S(2)}) copy-start(bf16[1024,1024]{1,0:T(8,128)(2,1)} %copy.49) | copy-start | bytes 6291460
  105.2 10.2 %collective-permute-start.4 = (bf16[192,1024]{1,0:T(8,128)(2,1)S(1)}, bf16[192,1024]{1,0:T(8,128)(2,1)S(1)}, u32[]{:S(2)}, u32[]{:S(2)}) collective-permute-start(bf16[192,1024]{1,0:T(8,128)(2,1)S(1)} %fusion.51), channel_id=1, source_target_pairs={{0,1},{1,2},{2,3},{3,4},{4,5},{5,6},{6,7},{7,8},{8,9},{9,10},{10,1... | collective-permute-start | bytes 1179656 | tf_op jit(solution)/shard_map/ppermute | solution.py:14
  115.6 2.2 %copy-start.3 = (bf16[2048,1024]{1,0:T(8,128)(2,1)S(1)}, bf16[2048,1024]{1,0:T(8,128)(2,1)}, u32[]{:S(2)}) copy-start(bf16[2048,1024]{1,0:T(8,128)(2,1)} %copy.50) | copy-start | bytes 12582916
where the time goes:
time: 135 us
  matrix products  55.1 us (41%)
  waiting for transfers between devices  38.5 us (29%)
  local copies, waits for them, and re-layouts  26.9 us (20%)
  other arithmetic  9.85 us (7%)
  starting transfers between devices  3.85 us (3%)
    ppermute x6, waiting for transfers between devices, passed_along(): lax.ppermute(array, axis, [(i, (i + by) % length) for i in range(length)])  38.5 us
    dot_general x4, matrix products, respond(): jnp.einsum('kgij,jkd->ikgd', shares, value_rows, preferred_element_type=j...  16.6 us
    dot_general x4, matrix products, respond(): update = jnp.dot(mixed, wo_layer, preferred_element_type=jnp.float32)  14.8 us
    dot_general x4, matrix products, respond(): jnp.einsum('ikgd,jkd->kgij', grouped, key_rows, preferred_element_type=jn...  11.8 us
    dot_general x4, matrix products, project(): jnp.dot(normed, wq_layer, preferred_element_type=jnp.float32)  8.4 us
    convert_element_type x4, local copies, waits for them, and re-layouts, respond(): mixed = jnp.einsum('kgij,jkd->ikgd', shares, value_rows, preferred_elemen...  7.77 us
    dot_general x1, local copies, waits for them, and re-layouts, project(): jnp.dot(normed, wq_layer, preferred_element_type=jnp.float32)  6.45 us
    reshape x4, local copies, waits for them, and re-layouts, respond(): mixed = mixed.reshape(stop - start, HEADS * HD)  5.91 us
  transfers between devices with their start and end apart: 6, of which 5 were waited for; matrix products, arithmetic and copies ran while one was open for 14% of the time, Pallas kernels for 0%

commit v1 on v0

v1 whole, which is shorter than its diff:
```python
import functools

import jax
import jax.numpy as jnp
import numpy as np
from jax import lax
from jax.experimental import pallas as pl
from jax.experimental.pallas import tpu as pltpu
from jax.sharding import PartitionSpec as P

HEADS = 16
KV_HEADS = 8
HD = 128
TICKS = 4
MAX_LEN = 96
SPLITS = (0, 96, 192)
HIDDEN = -1e30
BF16 = jnp.bfloat16
F32 = jnp.float32


def rope_table():
    middle = HD // 2
    spacing = 1000000.0 ** (-2.0 * np.arange(middle) / HD)
    angles = np.arange(MAX_LEN)[:, None] * spacing[None, :]
    cosine, sine = np.cos(angles), np.sin(angles)
    whole = np.concatenate([cosine, cosine, -sine, sine], axis=1).astype(np.float32)
    high = whole.astype(jnp.bfloat16)
    low = (whole - high.astype(np.float32)).astype(jnp.bfloat16)
    return np.concatenate([high, low], axis=0)


def tables_of(ids_row, table):
    length = ids_row.shape[1]
    across = jnp.broadcast_to(ids_row, (length, length))
    down = across.T
    row_index = lax.broadcasted_iota(jnp.int32, (length, length), 0)
    column = lax.broadcasted_iota(jnp.int32, (length, length), 1)
    matched = across == down
    places = jnp.sum(jnp.where(matched & (column < row_index), 1.0, 0.0), axis=1, keepdims=True)
    bias = jnp.where(matched & (column <= row_index), 0.0, HIDDEN)
    slots = lax.broadcasted_iota(jnp.int32, (length, 2 * MAX_LEN), 1)
    slots = jnp.where(slots >= MAX_LEN, slots - MAX_LEN, slots).astype(F32)
    one_hot = jnp.where(slots == places, 1.0, 0.0).astype(BF16)
    factors = jnp.dot(one_hot, table, preferred_element_type=F32)
    return factors, bias


def rotated(values, cosine, sine):
    return values * cosine + pltpu.roll(values, HD // 2, 1) * sine


def layer_rows(rows, keys, x_ref, gain_ref, weights, wait, cos_ref, bias_ref, k_ref, v_ref, mixed_ref, out_ref):
    low, high = rows
    first, last = keys
    size = high - low
    wq_ref, wk_ref, wv_ref, wo_ref = weights
    x = x_ref[...].astype(F32)
    scale = lax.rsqrt(jnp.mean(x * x, axis=1, keepdims=True) + 1e-05)
    normed = (x * scale * gain_ref[...].astype(F32)).astype(BF16)
    cosine = cos_ref[low:high, :HD]
    sine = cos_ref[low:high, HD:]
    factor = HD ** (-0.5) * np.log2(np.e)
    cosine_q = cosine * factor
    sine_q = sine * factor
    bias = bias_ref[low:high, first:last]
    width = 2 * HD
    for part in range(KV_HEADS // 2):
        lanes = slice(part * width, (part + 1) * width)
        wait("k", part)
        got = jnp.dot(normed, wk_ref[:, lanes], preferred_element_type=F32)
        for half in range(2):
            turned = rotated(got[:, half * HD : (half + 1) * HD], cosine, sine)
            k_ref[low:high, part * width + half * HD : part * width + (half + 1) * HD] = turned.astype(BF16)
    for part in range(KV_HEADS // 2):
        lanes = slice(part * width, (part + 1) * width)
        wait("v", part)
        v_ref[low:high, lanes] = jnp.dot(normed, wv_ref[:, lanes], preferred_element_type=F32).astype(BF16)
    ones = jnp.ones((last - first, HD), BF16)

    def query(group):
        wait("q", group)
        got = jnp.dot(normed, wq_ref[:, group * width : (group + 1) * width], preferred_element_type=F32)
        upper = rotated(got[:, :HD], cosine_q, sine_q)
        lower = rotated(got[:, HD:], cosine_q, sine_q)
        return jnp.concatenate([upper, lower], axis=0).astype(BF16)

    def attend(group, queries):
        key_rows = k_ref[first:last, group * HD : (group + 1) * HD]
        value_rows = v_ref[first:last, group * HD : (group + 1) * HD]
        scores = lax.dot_general(queries, key_rows, (((1,), (1,)), ((), ())), preferred_element_type=F32)
        scores = scores.reshape(2, size, last - first) + bias[None]
        most = jnp.max(scores, axis=2, keepdims=True)
        expo = jnp.exp2(scores - most).astype(BF16).reshape(2 * size, last - first)
        got = jnp.dot(expo, jnp.concatenate([value_rows, ones], axis=1), preferred_element_type=F32)
        mixed = (got[:, :HD] / got[:, HD:]).astype(BF16)
        mixed_ref[:, group * width : group * width + HD] = mixed[:size]
        mixed_ref[:, group * width + HD : (group + 1) * width] = mixed[size:]

    queries = query(0)
    for group in range(KV_HEADS):
        following = query(group + 1) if group + 1 < KV_HEADS else None
        attend(group, queries)
        queries = following
    for part in range(out_ref.shape[1] // width):
        lanes = slice(part * width, (part + 1) * width)
        wait("o", part)
        update = jnp.dot(mixed_ref[...], wo_ref[:, lanes], preferred_element_type=F32)
        out_ref[:, lanes] = (x_ref[:, lanes].astype(F32) + update).astype(BF16)


def opening_kernel(
    rows, keys, x_hbm, ids_ref, gain_ref, table_ref, wq_hbm, wk_hbm, wv_hbm, wo_hbm,
    out_ref, k_out, v_out, wq_ref, wk_ref, wv_ref, wo_ref, cos_ref, bias_ref,
    x_ref, mixed_ref, x_sem, sems,
):
    low, high = rows
    width = 2 * HD
    copies = {}
    load_x = pltpu.make_async_copy(x_hbm.at[0, low:high], x_ref, x_sem)
    load_x.start()
    plan = (("k", wk_hbm, wk_ref), ("v", wv_hbm, wv_ref), ("q", wq_hbm, wq_ref), ("o", wo_hbm, wo_ref))
    for name, source, target in plan:
        for part in range(target.shape[1] // width):
            lanes = slice(part * width, (part + 1) * width)
            copy = pltpu.make_async_copy(source.at[0, :, lanes], target.at[:, lanes], sems.at[len(copies)])
            copies[name, part] = copy
            copy.start()
    factors, bias = tables_of(ids_ref[...].astype(F32), table_ref[...])
    cos_ref[...] = factors
    bias_ref[...] = bias
    load_x.wait()
    layer_rows(
        rows, keys, x_ref, gain_ref, (wq_ref, wk_ref, wv_ref, wo_ref),
        lambda name, part: copies[name, part].wait(),
        cos_ref, bias_ref, k_out, v_out, mixed_ref, out_ref,
    )


def tables_kernel(ids_ref, table_ref, *outs):
    table = table_ref[...]
    for tick_index in range(TICKS - 1):
        factors, bias = tables_of(ids_ref[tick_index : tick_index + 1, :].astype(F32), table)
        outs[2 * tick_index][...] = factors
        outs[2 * tick_index + 1][...] = bias


def chunk_kernel(rows, keys, earlier, keep, x_ref, gain_ref, wq_ref, wk_ref, wv_ref, wo_ref, cos_ref, bias_ref, *refs):
    given, refs = refs[:earlier], refs[earlier:]
    out_ref, refs = refs[0], refs[1:]
    k_ref, v_ref, mixed_ref = refs[-3:]
    if earlier:
        k_ref[: rows[0]] = given[0][...]
        v_ref[: rows[0]] = given[1][...]
    layer_rows(
        rows, keys, x_ref, gain_ref, (wq_ref, wk_ref, wv_ref, wo_ref), lambda name, part: None,
        cos_ref, bias_ref, k_ref, v_ref, mixed_ref, out_ref,
    )
    if keep:
        refs[0][...] = k_ref[...]
        refs[1][...] = v_ref[...]


VMEM = pl.BlockSpec(memory_space=pltpu.VMEM)
ANY = pl.BlockSpec(memory_space=pl.ANY)


def kept(shape, dtype):
    return pltpu.VMEM(shape, dtype)


def held(array):
    return pltpu.with_memory_space_constraint(array, pltpu.VMEM)


def keys_of(rows):
    return (max(0, rows[0] - MAX_LEN + 1) // 16 * 16, rows[1])


def passed_along(array, by):
    length = lax.axis_size("section")
    return lax.ppermute(array, "section", [(i, (i + by) % length) for i in range(length)])


def body(micro, segment, gain, w_query, w_key, w_value, w_out):
    length, model = micro.shape[1], micro.shape[2]
    table = jnp.asarray(rope_table())
    later_ids = jnp.concatenate([passed_along(segment, by) for by in range(1, TICKS)], axis=0)
    limits = pltpu.CompilerParams(vmem_limit_bytes=40 * 1024 * 1024)
    kv_width = KV_HEADS * HD
    q_width = HEADS * HD
    pieces = list(zip(SPLITS[:-1], SPLITS[1:]))

    rows = pieces[0]
    size = rows[1] - rows[0]
    first = pl.pallas_call(
        functools.partial(opening_kernel, rows, keys_of(rows)),
        out_shape=(
            kept((size, model), BF16),
            kept((size, kv_width), BF16),
            kept((size, kv_width), BF16),
            kept((model, q_width), BF16),
            kept((model, kv_width), BF16),
            kept((model, kv_width), BF16),
            kept((q_width, model), BF16),
            kept((length, 2 * HD), F32),
            kept((length, length), F32),
        ),
        in_specs=[ANY, VMEM, VMEM, VMEM, ANY, ANY, ANY, ANY],
        out_specs=(VMEM,) * 9,
        scratch_shapes=[
            pltpu.VMEM((size, model), BF16),
            pltpu.VMEM((size, q_width), BF16),
            pltpu.SemaphoreType.DMA,
            pltpu.SemaphoreType.DMA((2 * (kv_width // (2 * HD)) + q_width // (2 * HD) + model // (2 * HD),)),
        ],
        compiler_params=limits,
        name="opening",
    )(micro, segment, gain, table, w_query, w_key, w_value, w_out)
    out, k_rows, v_rows = first[:3]
    weights = first[3:7]
    tables = [first[7:9]]

    def run(tick_index, piece, x, earlier):
        rows = pieces[piece]
        size = rows[1] - rows[0]
        keep = piece + 1 < len(pieces)
        shapes = [kept((size, model), BF16)]
        if keep:
            shapes += [kept((rows[1], kv_width), BF16)] * 2
        got = pl.pallas_call(
            functools.partial(chunk_kernel, rows, keys_of(rows), len(earlier), keep),
            out_shape=tuple(shapes),
            in_specs=[VMEM] * (8 + len(earlier)),
            out_specs=(VMEM,) * len(shapes),
            scratch_shapes=[
                pltpu.VMEM((rows[1], kv_width), BF16),
                pltpu.VMEM((rows[1], kv_width), BF16),
                pltpu.VMEM((size, q_width), BF16),
            ],
            compiler_params=limits,
            name="rows_%d_%d" % (tick_index, piece),
        )(held(x), gain, *map(held, weights), *map(held, tables[tick_index]), *map(held, earlier))
        return got[0], tuple(got[1:])

    streams = []
    for tick_index in range(TICKS):
        outs = []
        earlier = ()
        for piece in range(len(pieces)):
            if tick_index == 0 and piece == 0:
                got, earlier = out, (k_rows, v_rows)
            else:
                if tick_index == 0:
                    x = micro[0, pieces[piece][0] : pieces[piece][1]]
                else:
                    x = streams[piece]
                got, earlier = run(tick_index, piece, x, earlier)
            if tick_index < TICKS - 1:
                got = passed_along(got, 1)
            outs.append(got)
        if tick_index == 0:
            flat = pl.pallas_call(
                tables_kernel,
                out_shape=(kept((length, 2 * HD), F32), kept((length, length), F32)) * (TICKS - 1),
                in_specs=[VMEM, VMEM],
                out_specs=(VMEM,) * (2 * (TICKS - 1)),
                compiler_params=limits,
                name="tables",
            )(later_ids, table)
            tables += [flat[2 * i : 2 * i + 2] for i in range(TICKS - 1)]
        streams = outs
    return jnp.concatenate(streams, axis=0)[None]


def solution(mesh):
    in_specs = (
        P(("groups", "section"), None, None),
        P(("groups", "section"), None),
        P("section", None),
        P("section", None, None),
        P("section", None, None),
        P("section", None, None),
        P("section", None, None),
    )
    out_specs = P(("groups", "section"), None, None)
    return jax.shard_map(body, mesh=mesh, in_specs=in_specs, out_specs=out_specs, check_vma=False)
```

time: 135 us -> 62.7 us (0.46)
  matrix products: 55.1 us -> 0 us
  Pallas kernels: 0 us -> 39.1 us
  waiting for transfers between devices: 38.5 us -> 12.6 us
  local copies, waits for them, and re-layouts: 26.9 us -> 3.28 us
  other arithmetic: 9.85 us -> 0.78 us
  starting transfers between devices: 3.85 us -> 6.58 us
    dot_general x20 -> x0, matrix products: 55.1 us -> none  [the longest x4 16.6 us: respond(): jnp.einsum('kgij,jkd->ikgd', shares, value_rows, preferred_element_type=j...]
    pallas_call x0 -> x9, Pallas kernels: none -> 39.1 us  [the longest x7 29.4 us: run(): pl.pallas_call(functools.partial(chunk_kernel, rows, keys_of(rows), len(e...]
    ppermute x6 -> x9, waiting for transfers between devices: 38.5 us -> 12.6 us  [passed_along(): lax.ppermute(array, 'section', [(i, (i + by) % length) for i in range(len...]
    dot_general x2 -> x0, local copies, waits for them, and re-layouts: 10.5 us -> none  [the longest x1 6.45 us: project(): jnp.dot(normed, wq_layer, preferred_element_type=jnp.float32)]
    convert_element_type x4 -> x0, local copies, waits for them, and re-layouts: 7.77 us -> none  [respond(): mixed = jnp.einsum('kgij,jkd->ikgd', shares, value_rows, preferred_elemen...]
    reshape x4 -> x0, local copies, waits for them, and re-layouts: 5.91 us -> none  [respond(): mixed = mixed.reshape(stop - start, HEADS * HD)]
    another operation x8 -> x0, other arithmetic: 3.98 us -> none
    ppermute x6 -> x9, starting transfers between devices: 3.85 us -> 6.58 us  [passed_along(): lax.ppermute(array, 'section', [(i, (i + by) % length) for i in range(len...]
  transfers between devices with their start and end apart: 6 -> 9, of which waited for: 5 -> 6; matrix products, arithmetic and copies ran while one was open for 14% -> 0% of each run, Pallas kernels for 0% -> 41%
where the time goes in v1:
time: 62.7 us; the launch traced here: 62.5 us
  Pallas kernels  39.1 us (62%)
  waiting for transfers between devices  12.6 us (20%)
  starting transfers between devices  6.58 us (10%)
  local copies, waits for them, and re-layouts  3.28 us (5%)
  other arithmetic  0.78 us (1%)
    pallas_call x7, Pallas kernels, run(): pl.pallas_call(functools.partial(chunk_kernel, rows, keys_of(rows), len(e...  29.4 us
    ppermute x9, waiting for transfers between devices, passed_along(): lax.ppermute(array, 'section', [(i, (i + by) % length) for i in range(len...  12.6 us
    pallas_call x1, Pallas kernels, body(): pl.pallas_call(functools.partial(opening_kernel, rows, keys_of(rows)), ou...  9.24 us
    ppermute x9, starting transfers between devices, passed_along(): lax.ppermute(array, 'section', [(i, (i + by) % length) for i in range(len...  6.58 us
    unnamed x12, local copies, waits for them, and re-layouts  3.27 us
  transfers between devices with their start and end apart: 9, of which 6 were waited for; matrix products, arithmetic and copies ran while one was open for 0% of the time, Pallas kernels for 41%

profile of v1, /device:TPU:0, one launch (start us, length us, event | category | flops | bytes accessed | tf_op | source)
XLA Modules:
  0.0 62.5 jit_solution(17903822518912200731)
XLA Ops:
  0.0 1.0 %copy-done = bf16[1,192,1024]{2,1,0:T(8,128)(2,1)S(1)} copy-done((bf16[1,192,1024]{2,1,0:T(8,128)(2,1)S(1)}, bf16[1,192,1024]{2,1,0:T(8,128)(2,1)}, u32[]{:S(2)}) %copy-start) | copy-done | bytes 393240
  1.0 0.9 %copy-done.1 = bf16[192,256]{1,0:T(8,128)(2,1)S(1)} copy-done((bf16[192,256]{1,0:T(8,128)(2,1)S(1)}, bf16[192,256]{1,0:T(8,128)(2,1)}, u32[]{:S(2)}) %copy-start.1) | copy-done | bytes 98328
  1.9 0.7 %copy-done.3 = bf16[1,1024]{1,0:T(2,128)(2,1)S(1)} copy-done((bf16[1,1024]{1,0:T(2,128)(2,1)S(1)}, bf16[1,1024]{1,0:T(2,128)(2,1)}, u32[]{:S(2)}) %copy-start.3) | copy-done | bytes 2072
  2.6 0.7 %copy-done.5 = s32[1,192]{1,0:T(1,128)S(1)} copy-done((s32[1,192]{1,0:T(1,128)S(1)}, s32[1,192]{1,0:T(1,128)}, u32[]{:S(2)}) %copy-start.5) | copy-done | bytes 792
  3.3 9.2 %opening.1 = (bf16[96,1024]{1,0:T(8,128)(2,1)S(1)}, bf16[96,1024]{1,0:T(8,128)(2,1)S(1)}, bf16[96,1024]{1,0:T(8,128)(2,1)S(1)}, bf16[1024,2048]{1,0:T(8,128)(2,1...) custom-call(bf16[1,192,1024]{2,1,0:T(8,128)(2,1)S(1)} %copy-done, ...), custom_call_target="tpu_custom_call" | custom-call | tf_op jit(solution)/shard_map/opening/pallas_call | solution.py:196
  12.5 0.5 collective-permute-start
  13.0 0.0 copy-start.2
  13.0 0.0 copy-start.4
  13.0 4.3 %rows_0_1.1 = bf16[96,1024]{1,0:T(8,128)(2,1)S(1)} custom-call(bf16[96,1024]{1,0:T(8,128)(2,1)S(1)} %slice_bitcast_fusion.x_ref, bf16[1,1024]{1,0:T(2,128)(2,1)S(1)} %copy-done.3, bf16[1024,2048]{1,0:T(8,128)(2,1)S(1)} %get-tuple-element.30.wq_ref, bf16[1024,1024]{1,0:T(8,128)(2,1)S(1)} %get-tuple-element.31.wk_ref, ...), custom_call_target="tpu_custom_call" | custom-call | tf_op jit(solution)/shard_map/rows_0_1/pallas_call | solution.py:231
  17.3 2.7 %collective-permute-start.6 = (bf16[96,1024]{1,0:T(8,128)(2,1)S(1)}, bf16[96,1024]{1,0:T(8,128)(2,1)S(1)}, u32[]{:S(2)}, u32[]{:S(2)}) collective-permute-start(bf16[96,1024]{1,0:T(8,128)(2,1)S(1)} %rows_0_1.1), channel_id=1, source_target_pairs={{0,1},{1,2},{2,3},{3,4},{4,5},{5,6},{6,7},{7,8},{8,9},{9,10},{10,1... | collective-permute-start | bytes 589832 | tf_op jit(solution)/shard_map/ppermute | solution.py:182
  20.0 1.2 %collective-permute-start.3 = (s32[1,192]{1,0:T(1,128)S(1)}, s32[1,192]{1,0:T(1,128)S(1)}, u32[]{:S(2)}, u32[]{:S(2)}) collective-permute-start(s32[1,192]{1,0:T(1,128)S(1)} %copy-done.5), channel_id=1, source_target_pairs={{0,3},{1,4},{2,5},{3,6},{4,7},{5,8},{6,9},{7,10},{8,11},{9,12},{10... | collective-permute-start | bytes 2312 | tf_op jit(solution)/shard_map/ppermute | solution.py:182
  21.2 1.5 %collective-permute-start.2 = (s32[1,192]{1,0:T(1,128)S(1)}, s32[1,192]{1,0:T(1,128)S(1)}, u32[]{:S(2)}, u32[]{:S(2)}) collective-permute-start(s32[1,192]{1,0:T(1,128)S(1)} %copy-done.5), channel_id=1, source_target_pairs={{0,2},{1,3},{2,4},{3,5},{4,6},{5,7},{6,8},{7,9},{8,10},{9,11},{10,... | collective-permute-start | bytes 2312 | tf_op jit(solution)/shard_map/ppermute | solution.py:182
  22.7 0.2 collective-permute-start.1
  22.9 1.9 %collective-permute-done.3 = s32[1,192]{1,0:T(1,128)S(1)} collective-permute-done((s32[1,192]{1,0:T(1,128)S(1)}, s32[1,192]{1,0:T(1,128)S(1)}, u32[]{:S(2)}, u32[]{:S(2)}) %collective-permute-start.3) | collective-permute-done | bytes 800 | tf_op jit(solution)/shard_map/ppermute | solution.py:182
  24.8 2.7 %collective-permute-done.2 = s32[1,192]{1,0:T(1,128)S(1)} collective-permute-done((s32[1,192]{1,0:T(1,128)S(1)}, s32[1,192]{1,0:T(1,128)S(1)}, u32[]{:S(2)}, u32[]{:S(2)}) %collective-permute-start.2) | collective-permute-done | bytes 800 | tf_op jit(solution)/shard_map/ppermute | solution.py:182
  27.5 0.9 %collective-permute-done.1 = s32[1,192]{1,0:T(1,128)S(1)} collective-permute-done((s32[1,192]{1,0:T(1,128)S(1)}, s32[1,192]{1,0:T(1,128)S(1)}, u32[]{:S(2)}, u32[]{:S(2)}) %collective-permute-start.1) | collective-permute-done | bytes 800 | tf_op jit(solution)/shard_map/ppermute | solution.py:182
  28.4 0.5 tables.1
  28.9 4.1 %rows_1_0.1 = (bf16[96,1024]{1,0:T(8,128)(2,1)S(1)}, bf16[96,1024]{1,0:T(8,128)(2,1)S(1)}, bf16[96,1024]{1,0:T(8,128)(2,1)S(1)}) custom-call(bf16[96,1024]{1,0:T(8,128)(2,1)S(1)} %collective-permute-done.x_ref, bf16[1,1024]{1,0:T(2,128)(2,1)S(1)} %copy-done.4, bf16[1024,2048]{1,0:T(8,128)(2,1)S(1)} %get-tuple-element.30.wq_ref, ...), custom_call_target="tpu_custom_call" | custom-call | tf_op jit(solution)/shard_map/rows_1_0/pallas_call | solution.py:231
  33.1 0.1 collective-permute-start.4
  33.1 0.0 collective-permute-done.6.x_ref
  33.1 4.3 %rows_1_1.1 = bf16[96,1024]{1,0:T(8,128)(2,1)S(1)} custom-call(bf16[96,1024]{1,0:T(8,128)(2,1)S(1)} %collective-permute-done.6.x_ref, bf16[1,1024]{1,0:T(2,128)(2,1)S(1)} %copy-done.4, bf16[1024,2048]{1,0:T(8,128)(2,1)S(1)} %get-tuple-element.30.wq_ref, bf16[1024,1024]{1,0:T(8,128)(2,1)S(1)} %get-tuple-element.31.wk_ref, ...), custom_call_target="tpu_custom_call" | custom-call | tf_op jit(solution)/shard_map/rows_1_1/pallas_call | solution.py:231
  37.4 0.1 collective-permute-start.7
  37.5 3.4 %collective-permute-done.4.x_ref = bf16[96,1024]{1,0:T(8,128)(2,1)S(1)} collective-permute-done((bf16[96,1024]{1,0:T(8,128)(2,1)S(1)}, bf16[96,1024]{1,0:T(8,128)(2,1)S(1)}, u32[]{:S(2)}, u32[]{:S(2)}) %collective-permute-start.4) | collective-permute-done | bytes 196640 | tf_op jit(solution)/shard_map/ppermute | solution.py:182
  40.9 4.1 %rows_2_0.1 = (bf16[96,1024]{1,0:T(8,128)(2,1)S(1)}, bf16[96,1024]{1,0:T(8,128)(2,1)S(1)}, bf16[96,1024]{1,0:T(8,128)(2,1)S(1)}) custom-call(bf16[96,1024]{1,0:T(8,128)(2,1)S(1)} %collective-permute-done.4.x_ref, bf16[1,1024]{1,0:T(2,128)(2,1)S(1)} %copy-done.4, bf16[1024,2048]{1,0:T(8,128)(2,1)S(1)} %get-tuple-element.30.wq_ref, ...), custom_call_target="tpu_custom_call" | custom-call | tf_op jit(solution)/shard_map/rows_2_0/pallas_call | solution.py:231
  45.0 0.3 collective-permute-start.5
  45.3 4.3 %rows_2_1.1 = bf16[96,1024]{1,0:T(8,128)(2,1)S(1)} custom-call(bf16[96,1024]{1,0:T(8,128)(2,1)S(1)} %collective-permute-done.7.x_ref, bf16[1,1024]{1,0:T(2,128)(2,1)S(1)} %copy-done.4, bf16[1024,2048]{1,0:T(8,128)(2,1)S(1)} %get-tuple-element.30.wq_ref, bf16[1024,1024]{1,0:T(8,128)(2,1)S(1)} %get-tuple-element.31.wk_ref, ...), custom_call_target="tpu_custom_call" | custom-call | tf_op jit(solution)/shard_map/rows_2_1/pallas_call | solution.py:231
  49.6 0.1 collective-permute-start.8
  49.6 3.4 %collective-permute-done.5.x_ref = bf16[96,1024]{1,0:T(8,128)(2,1)S(1)} collective-permute-done((bf16[96,1024]{1,0:T(8,128)(2,1)S(1)}, bf16[96,1024]{1,0:T(8,128)(2,1)S(1)}, u32[]{:S(2)}, u32[]{:S(2)}) %collective-permute-start.5) | collective-permute-done | bytes 196640 | tf_op jit(solution)/shard_map/ppermute | solution.py:182
  53.1 4.1 %rows_3_0.1 = (bf16[96,1024]{1,0:T(8,128)(2,1)S(1)}, bf16[96,1024]{1,0:T(8,128)(2,1)S(1)}, bf16[96,1024]{1,0:T(8,128)(2,1)S(1)}) custom-call(bf16[96,1024]{1,0:T(8,128)(2,1)S(1)} %collective-permute-done.5.x_ref, bf16[1,1024]{1,0:T(2,128)(2,1)S(1)} %copy-done.4, bf16[1024,2048]{1,0:T(8,128)(2,1)S(1)} %get-tuple-element.30.wq_ref, ...), custom_call_target="tpu_custom_call" | custom-call | tf_op jit(solution)/shard_map/rows_3_0/pallas_call | solution.py:231
  57.2 0.2 collective-permute-done.8.x_ref
  57.4 4.3 %rows_3_1.1 = bf16[96,1024]{1,0:T(8,128)(2,1)S(1)} custom-call(bf16[96,1024]{1,0:T(8,128)(2,1)S(1)} %collective-permute-done.8.x_ref, bf16[1,1024]{1,0:T(2,128)(2,1)S(1)} %copy-done.4, bf16[1024,2048]{1,0:T(8,128)(2,1)S(1)} %get-tuple-element.30.wq_ref, bf16[1024,1024]{1,0:T(8,128)(2,1)S(1)} %get-tuple-element.31.wk_ref, ...), custom_call_target="tpu_custom_call" | custom-call | tf_op jit(solution)/shard_map/rows_3_1/pallas_call | solution.py:231
  61.7 0.8 %maximum_bitcast_fusion = bf16[1,192,1024]{2,1,0:T(8,128)(2,1)} fusion(bf16[96,1024]{1,0:T(8,128)(2,1)S(1)} %rows_3_1.1, bf16[96,1024]{1,0:T(8,128)(2,1)S(1)} %get-tuple-element.42), kind=kLoop, calls=%fused_computation | loop fusion | flops 786432 | bytes 786432 | tf_op jit(solution)/shard_map/broadcast_in_dim | solution.py:273
  (10 shorter events, 0.0 us)
Async XLA Ops:
  0.0 1.0 %copy-start = (bf16[1,192,1024]{2,1,0:T(8,128)(2,1)S(1)}, bf16[1,192,1024]{2,1,0:T(8,128)(2,1)}, u32[]{:S(2)}) copy-start(bf16[1,192,1024]{2,1,0:T(8,128)(2,1)} %x_hbm.1) | copy-start | bytes 1179652
  1.0 0.9 %copy-start.1 = (bf16[192,256]{1,0:T(8,128)(2,1)S(1)}, bf16[192,256]{1,0:T(8,128)(2,1)}, u32[]{:S(2)}) copy-start(bf16[192,256]{1,0:T(8,128)(2,1)} %constant.2.clone.table_ref) | copy-start | bytes 294916
  1.9 0.7 %copy-start.3 = (bf16[1,1024]{1,0:T(2,128)(2,1)S(1)}, bf16[1,1024]{1,0:T(2,128)(2,1)}, u32[]{:S(2)}) copy-start(bf16[1,1024]{1,0:T(2,128)(2,1)} %gain_ref.15) | copy-start | bytes 6148
  2.6 0.7 %copy-start.5 = (s32[1,192]{1,0:T(1,128)S(1)}, s32[1,192]{1,0:T(1,128)}, u32[]{:S(2)}) copy-start(s32[1,192]{1,0:T(1,128)} %ids_ref.1) | copy-start | bytes 2308
  12.5 16.4 %collective-permute-start = (bf16[96,1024]{1,0:T(8,128)(2,1)S(1)}, bf16[96,1024]{1,0:T(8,128)(2,1)S(1)}, u32[]{:S(2)}, u32[]{:S(2)}) collective-permute-start(bf16[96,1024]{1,0:T(8,128)(2,1)S(1)} %get-tuple-element.29), channel_id=1, source_target_pairs={{0,1},{1,2},{2,3},{3,4},{4,5},{5,6},{6,7},{7,8},{8,9},{9,10},{10,1... | collective-permute-start | bytes 589832 | tf_op jit(solution)/shard_map/ppermute | solution.py:182
  13.0 15.4 %copy-start.2 = (bf16[192,256]{1,0:T(8,128)(2,1)S(1)}, bf16[192,256]{1,0:T(8,128)(2,1)}, u32[]{:S(2)}) copy-start(bf16[192,256]{1,0:T(8,128)(2,1)} %constant.2.clone.table_ref) | copy-start | bytes 294916
  13.0 15.9 %copy-start.4 = (bf16[1,1024]{1,0:T(2,128)(2,1)S(1)}, bf16[1,1024]{1,0:T(2,128)(2,1)}, u32[]{:S(2)}) copy-start(bf16[1,1024]{1,0:T(2,128)(2,1)} %gain_ref.15) | copy-start | bytes 6148
  17.3 15.8 %collective-permute-start.6 = (bf16[96,1024]{1,0:T(8,128)(2,1)S(1)}, bf16[96,1024]{1,0:T(8,128)(2,1)S(1)}, u32[]{:S(2)}, u32[]{:S(2)}) collective-permute-start(bf16[96,1024]{1,0:T(8,128)(2,1)S(1)} %rows_0_1.1), channel_id=1, source_target_pairs={{0,1},{1,2},{2,3},{3,4},{4,5},{5,6},{6,7},{7,8},{8,9},{9,10},{10,1... | collective-permute-start | bytes 589832 | tf_op jit(solution)/shard_map/ppermute | solution.py:182
  20.0 4.8 %collective-permute-start.3 = (s32[1,192]{1,0:T(1,128)S(1)}, s32[1,192]{1,0:T(1,128)S(1)}, u32[]{:S(2)}, u32[]{:S(2)}) collective-permute-start(s32[1,192]{1,0:T(1,128)S(1)} %copy-done.5), channel_id=1, source_target_pairs={{0,3},{1,4},{2,5},{3,6},{4,7},{5,8},{6,9},{7,10},{8,11},{9,12},{10... | collective-permute-start | bytes 2312 | tf_op jit(solution)/shard_map/ppermute | solution.py:182
  21.2 6.3 %collective-permute-start.2 = (s32[1,192]{1,0:T(1,128)S(1)}, s32[1,192]{1,0:T(1,128)S(1)}, u32[]{:S(2)}, u32[]{:S(2)}) collective-permute-start(s32[1,192]{1,0:T(1,128)S(1)} %copy-done.5), channel_id=1, source_target_pairs={{0,2},{1,3},{2,4},{3,5},{4,6},{5,7},{6,8},{7,9},{8,10},{9,11},{10,... | collective-permute-start | bytes 2312 | tf_op jit(solution)/shard_map/ppermute | solution.py:182
  22.7 5.7 %collective-permute-start.1 = (s32[1,192]{1,0:T(1,128)S(1)}, s32[1,192]{1,0:T(1,128)S(1)}, u32[]{:S(2)}, u32[]{:S(2)}) collective-permute-start(s32[1,192]{1,0:T(1,128)S(1)} %copy-done.5), channel_id=1, source_target_pairs={{0,1},{1,2},{2,3},{3,4},{4,5},{5,6},{6,7},{7,8},{8,9},{9,10},{10,1... | collective-permute-start | bytes 2312 | tf_op jit(solution)/shard_map/ppermute | solution.py:182
  33.1 7.8 %collective-permute-start.4 = (bf16[96,1024]{1,0:T(8,128)(2,1)S(1)}, bf16[96,1024]{1,0:T(8,128)(2,1)S(1)}, u32[]{:S(2)}, u32[]{:S(2)}) collective-permute-start(bf16[96,1024]{1,0:T(8,128)(2,1)S(1)} %get-tuple-element.36), channel_id=1, source_target_pairs={{0,1},{1,2},{2,3},{3,4},{4,5},{5,6},{6,7},{7,8},{8,9},{9,10},{10,1... | collective-permute-start | bytes 589832 | tf_op jit(solution)/shard_map/ppermute | solution.py:182
  37.4 7.9 %collective-permute-start.7 = (bf16[96,1024]{1,0:T(8,128)(2,1)S(1)}, bf16[96,1024]{1,0:T(8,128)(2,1)S(1)}, u32[]{:S(2)}, u32[]{:S(2)}) collective-permute-start(bf16[96,1024]{1,0:T(8,128)(2,1)S(1)} %rows_1_1.1), channel_id=1, source_target_pairs={{0,1},{1,2},{2,3},{3,4},{4,5},{5,6},{6,7},{7,8},{8,9},{9,10},{10,1... | collective-permute-start | bytes 589832 | tf_op jit(solution)/shard_map/ppermute | solution.py:182
  45.0 8.1 %collective-permute-start.5 = (bf16[96,1024]{1,0:T(8,128)(2,1)S(1)}, bf16[96,1024]{1,0:T(8,128)(2,1)S(1)}, u32[]{:S(2)}, u32[]{:S(2)}) collective-permute-start(bf16[96,1024]{1,0:T(8,128)(2,1)S(1)} %get-tuple-element.39), channel_id=1, source_target_pairs={{0,1},{1,2},{2,3},{3,4},{4,5},{5,6},{6,7},{7,8},{8,9},{9,10},{10,1... | collective-permute-start | bytes 589832 | tf_op jit(solution)/shard_map/ppermute | solution.py:182
  49.6 7.8 %collective-permute-start.8 = (bf16[96,1024]{1,0:T(8,128)(2,1)S(1)}, bf16[96,1024]{1,0:T(8,128)(2,1)S(1)}, u32[]{:S(2)}, u32[]{:S(2)}) collective-permute-start(bf16[96,1024]{1,0:T(8,128)(2,1)S(1)} %rows_2_1.1), channel_id=1, source_target_pairs={{0,1},{1,2},{2,3},{3,4},{4,5},{5,6},{6,7},{7,8},{8,9},{9,10},{10,1... | collective-permute-start | bytes 589832 | tf_op jit(solution)/shard_map/ppermute | solution.py:182

commit v2 on v0

v2 whole, which is shorter than its diff:
```python
import functools

import jax
import jax.numpy as jnp
import numpy as np
from jax import lax
from jax.experimental import pallas as pl
from jax.experimental.pallas import tpu as pltpu
from jax.sharding import PartitionSpec as P

HEADS = 16
KV_HEADS = 8
HD = 128
TICKS = 4
MAX_LEN = 96
CUTS = (0, 512, 1024)
EXTRA = 16
LIFT = 16.0
HIDDEN = -1e30
PAIR = 2 * HD
Q_WIDTH = HEADS * HD
KV_WIDTH = KV_HEADS * HD
BF16 = jnp.bfloat16
F32 = jnp.float32


def rope_table():
    middle = HD // 2
    spacing = 1000000.0 ** (-2.0 * np.arange(middle) / HD)
    angles = np.arange(MAX_LEN)[:, None] * spacing[None, :]
    cosine, sine = np.cos(angles), np.sin(angles)
    whole = np.concatenate([cosine, cosine, -sine, sine], axis=1).astype(np.float32)
    high = whole.astype(jnp.bfloat16).astype(np.float32)
    low = (whole - high).astype(jnp.bfloat16).astype(np.float32)
    return np.concatenate([high, low], axis=0)


def tables_of(ids_row, table):
    length = ids_row.shape[1]
    across = jnp.broadcast_to(ids_row, (length, length))
    down = across.T
    row_index = lax.broadcasted_iota(jnp.int32, (length, length), 0)
    column = lax.broadcasted_iota(jnp.int32, (length, length), 1)
    matched = across == down
    places = jnp.sum(jnp.where(matched & (column < row_index), 1.0, 0.0), axis=1, keepdims=True)
    bias = jnp.where(matched & (column <= row_index), 0.0, HIDDEN)
    slots = lax.broadcasted_iota(jnp.int32, (length, 2 * MAX_LEN), 1)
    slots = jnp.where(slots >= MAX_LEN, slots - MAX_LEN, slots).astype(F32)
    one_hot = jnp.where(slots == places, 1.0, 0.0).astype(BF16)
    factors = jnp.dot(one_hot, table, preferred_element_type=F32)
    return factors, bias


def rotated(values, cosine, sine):
    return values * cosine + pltpu.roll(values, HD // 2, 1) * sine


def squares(x):
    total = x[:, :HD] * x[:, :HD]
    for start in range(HD, x.shape[1], HD):
        part = x[:, start : start + HD]
        total = total + part * part
    return total


def tiles_of():
    tiles = [("k", start, start) for start in range(0, KV_WIDTH, PAIR)]
    tiles += [("v", start, KV_WIDTH + start) for start in range(0, KV_WIDTH, PAIR)]
    return tiles + [("q", start, 2 * KV_WIDTH + start) for start in range(0, Q_WIDTH, PAIR)]


def partial_products(lifted, slab, weights, acc_ref, source):
    for name, start, place in tiles_of():
        got = jnp.dot(lifted, weights[name][slab, start : start + PAIR], preferred_element_type=F32)
        if source is not None:
            got = got + source[:, place : place + PAIR]
        acc_ref[:, place : place + PAIR] = got


def attention(lifted, slab, total, weights, acc_ref, cos_ref, bias_ref, k_ref, v_ref, mixed_ref):
    length, model = lifted.shape[0], weights["k"].shape[0]
    mean = jnp.sum(total, axis=1, keepdims=True) * (1.0 / model)
    scale = lax.rsqrt(mean + 1e-05) * (1.0 / LIFT)
    cosine = cos_ref[:, :HD] * scale
    sine = cos_ref[:, HD:] * scale
    factor = HD ** (-0.5) * np.log2(np.e)
    cosine_q = cosine * factor
    sine_q = sine * factor
    bias = bias_ref[...]
    ones = jnp.ones((length, HD), BF16)

    def whole(tile):
        name, start, place = tile
        got = jnp.dot(lifted, weights[name][slab, start : start + PAIR], preferred_element_type=F32)
        return got + acc_ref[:, place : place + PAIR]

    def query(tile):
        got = whole(tile)
        upper = rotated(got[:, :HD], cosine_q, sine_q)
        lower = rotated(got[:, HD:], cosine_q, sine_q)
        return jnp.concatenate([upper, lower], axis=0).astype(BF16)

    def score(group, queries):
        key_rows = k_ref[:, group * HD : (group + 1) * HD]
        scores = lax.dot_general(queries, key_rows, (((1,), (1,)), ((), ())), preferred_element_type=F32)
        return scores.reshape(2, length, length) + bias[None]

    def exponents(scores):
        most = jnp.max(scores, axis=2, keepdims=True)
        return jnp.exp2(scores - most).astype(BF16).reshape(2 * length, length)

    def mix(group, expo):
        value_rows = v_ref[:, group * HD : (group + 1) * HD]
        got = jnp.dot(expo, jnp.concatenate([value_rows, ones], axis=1), preferred_element_type=F32)
        mixed = (got[:, :HD] / got[:, HD:]).astype(BF16)
        mixed_ref[:, group * PAIR : group * PAIR + HD] = mixed[:length]
        mixed_ref[:, group * PAIR + HD : (group + 1) * PAIR] = mixed[length:]

    queries, scores, expo = {}, {}, {}
    for tile in tiles_of():
        name, start, place = tile
        if name == "k":
            got = whole(tile)
            for half in range(0, PAIR, HD):
                k_ref[:, start + half : start + half + HD] = rotated(
                    got[:, half : half + HD], cosine, sine
                ).astype(BF16)
        elif name == "v":
            v_ref[:, start : start + PAIR] = (whole(tile) * scale).astype(BF16)
    heads = [tile for tile in tiles_of() if tile[0] == "q"]
    for step in range(KV_HEADS + 3):
        if step < KV_HEADS:
            queries[step] = query(heads[step])
        if 0 <= step - 1 < KV_HEADS:
            scores[step - 1] = score(step - 1, queries.pop(step - 1))
        if 0 <= step - 2 < KV_HEADS:
            expo[step - 2] = exponents(scores.pop(step - 2))
        if 0 <= step - 3 < KV_HEADS:
            mix(step - 3, expo.pop(step - 3))


def out_columns(low, high, mixed_ref, wo_ref, x_ref, out_ref, base):
    length = mixed_ref.shape[0]
    for start in range(low, high, PAIR):
        update = jnp.dot(mixed_ref[...], wo_ref[:, start : start + PAIR], preferred_element_type=F32)
        lanes = slice(start - base, start - base + PAIR)
        out_ref[:length, lanes] = (x_ref[:length, lanes].astype(F32) + update).astype(BF16)


def write_ids(ids_row, out_ref):
    length = ids_row.shape[1]
    out_ref[length:, :] = jnp.zeros((EXTRA, out_ref.shape[1]), BF16)
    out_ref[length:, :length] = jnp.broadcast_to(ids_row, (EXTRA, length)).astype(BF16)


def opening_kernel(
    x_hbm, ids_hbm, gain_hbm, table_hbm, wq_hbm, wk_hbm, wv_hbm, wo_hbm,
    out_ref, mixed_ref, x_last, wq_ref, wk_ref, wv_ref, wo_ref, gain_ref, table_ref,
    x_ref, ids_ref, raw_gain, raw_table, acc_ref, cos_ref, bias_ref, k_ref, v_ref, small_sems, sems,
):
    length, model = x_ref.shape
    slabs = [slice(low, low + PAIR) for low in range(0, model, PAIR)]
    small = [
        pltpu.make_async_copy(x_hbm.at[0], x_ref, small_sems.at[0]),
        pltpu.make_async_copy(gain_hbm, raw_gain, small_sems.at[1]),
        pltpu.make_async_copy(ids_hbm, ids_ref, small_sems.at[2]),
        pltpu.make_async_copy(table_hbm, raw_table, small_sems.at[3]),
        pltpu.make_async_copy(x_hbm.at[0, :, CUTS[1] :], x_last, small_sems.at[4]),
    ]
    for copy in small:
        copy.start()
    copies = {}
    for slab in slabs:
        for name, source, target in (("k", wk_hbm, wk_ref), ("v", wv_hbm, wv_ref), ("q", wq_hbm, wq_ref)):
            copy = pltpu.make_async_copy(source.at[0, slab], target.at[slab], sems.at[len(copies)])
            copies[name, slab.start] = copy
            copy.start()
    quarter = wo_ref.shape[0] // 4
    for low in range(0, wo_ref.shape[0], quarter):
        rows = slice(low, low + quarter)
        copy = pltpu.make_async_copy(wo_hbm.at[0, rows], wo_ref.at[rows], sems.at[len(copies)])
        copies["o", low] = copy
        copy.start()
    for copy in small[:4]:
        copy.wait()
    gain_ref[...] = raw_gain[...].astype(F32) * LIFT
    table_ref[...] = raw_table[...].astype(BF16)
    ids_row = ids_ref[...].astype(F32)
    factors, bias = tables_of(ids_row, table_ref[...])
    cos_ref[...] = factors
    bias_ref[...] = bias
    write_ids(ids_row, out_ref)
    x = x_ref[...].astype(F32)
    total = squares(x)
    lifted = (x * gain_ref[...]).astype(BF16)
    weights = {"k": wk_ref, "v": wv_ref, "q": wq_ref}
    for index, slab in enumerate(slabs):
        for name in "kvq":
            copies[name, slab.start].wait()
        if index + 1 < len(slabs):
            partial_products(lifted[:, slab], slab, weights, acc_ref, acc_ref if index else None)
    attention(
        lifted[:, slabs[-1]], slabs[-1], total, weights, acc_ref, cos_ref, bias_ref, k_ref, v_ref, mixed_ref
    )
    for low in range(0, wo_ref.shape[0], quarter):
        copies["o", low].wait()
    small[4].wait()
    out_columns(CUTS[0], CUTS[1], mixed_ref, wo_ref, x_ref, out_ref, 0)


def first_kernel(
    x_ref, gain_ref, table_ref, wq_ref, wk_ref, wv_ref, acc_ref, total_ref, cos_ref, bias_ref
):
    length = x_ref.shape[0] - EXTRA
    slab = slice(CUTS[0], CUTS[1])
    x = x_ref[:length, :].astype(F32)
    lifted = (x * gain_ref[:, slab]).astype(BF16)
    partial_products(lifted, slab, {"k": wk_ref, "v": wv_ref, "q": wq_ref}, acc_ref, None)
    total_ref[...] = squares(x)
    factors, bias = tables_of(x_ref[length:, :length].astype(F32)[:1], table_ref[...])
    cos_ref[...] = factors
    bias_ref[...] = bias


def second_kernel(
    last, x_first, x_ref, gain_ref, wq_ref, wk_ref, wv_ref, wo_ref, acc_ref, total_ref, cos_ref, bias_ref, *refs
):
    k_ref, v_ref = refs[-2:]
    mixed_ref = refs[-3]
    out_ref = refs[0]
    length = x_ref.shape[0]
    slab = slice(CUTS[1], CUTS[2])
    x = x_ref[...].astype(F32)
    lifted = (x * gain_ref[:, slab]).astype(BF16)
    total = total_ref[...] + squares(x)
    attention(
        lifted, slab, total, {"k": wk_ref, "v": wv_ref, "q": wq_ref}, acc_ref, cos_ref, bias_ref,
        k_ref, v_ref, mixed_ref,
    )
    if last:
        whole = out_ref.at[0]
        out_columns(CUTS[0], CUTS[1], mixed_ref, wo_ref, x_first, whole.at[:, : CUTS[1]], 0)
        out_columns(CUTS[1], CUTS[2], mixed_ref, wo_ref, x_ref, whole.at[:, CUTS[1] :], CUTS[1])
    else:
        out_ref[length:, :] = x_first[length:, :]
        out_columns(CUTS[0], CUTS[1], mixed_ref, wo_ref, x_first, out_ref, 0)


def third_kernel(mixed_ref, x_ref, wo_ref, out_ref):
    out_columns(CUTS[1], CUTS[2], mixed_ref, wo_ref, x_ref, out_ref, CUTS[1])


VMEM = pl.BlockSpec(memory_space=pltpu.VMEM)
HBM = pl.BlockSpec(memory_space=pltpu.HBM)


def kept(shape, dtype):
    return pltpu.VMEM(shape, dtype)


def held(array):
    return pltpu.with_memory_space_constraint(array, pltpu.VMEM)


def left(array):
    return pltpu.with_memory_space_constraint(array, pltpu.HBM)


def passed_along(array, by):
    length = lax.axis_size("section")
    return lax.ppermute(array, "section", [(i, (i + by) % length) for i in range(length)])


def body(micro, segment, gain, w_query, w_key, w_value, w_out):
    length, model = micro.shape[1], micro.shape[2]
    limits = pltpu.CompilerParams(vmem_limit_bytes=32 * 1024 * 1024)
    table = jnp.asarray(rope_table())
    near, far = CUTS[1], CUTS[2] - CUTS[1]
    acc_width = 2 * KV_WIDTH + Q_WIDTH
    mixing = [pltpu.VMEM((length, KV_WIDTH), BF16)] * 2

    def call(kernel, name, shapes, scratch, args):
        shapes = tuple(shapes)
        return pl.pallas_call(
            kernel, out_shape=shapes, in_specs=[VMEM] * len(args), out_specs=(VMEM,) * len(shapes),
            scratch_shapes=scratch, compiler_params=limits, name=name,
        )(*map(held, args))

    out, mixed, x_last, wq, wk, wv, wo, gain, table = pl.pallas_call(
        opening_kernel,
        out_shape=(
            kept((length + EXTRA, near), BF16),
            kept((length, Q_WIDTH), BF16),
            kept((length, far), BF16),
            kept((model, Q_WIDTH), BF16),
            kept((model, KV_WIDTH), BF16),
            kept((model, KV_WIDTH), BF16),
            kept((Q_WIDTH, model), BF16),
            kept((1, model), F32),
            kept(table.shape, BF16),
        ),
        in_specs=[HBM] * 8,
        out_specs=(VMEM,) * 9,
        scratch_shapes=[
            pltpu.VMEM((length, model), BF16),
            pltpu.VMEM(segment.shape, jnp.int32),
            pltpu.VMEM(gain.shape, BF16),
            pltpu.VMEM(table.shape, F32),
            pltpu.VMEM((length, acc_width), F32),
            pltpu.VMEM((length, PAIR), F32),
            pltpu.VMEM((length, length), F32),
            *mixing,
            pltpu.SemaphoreType.DMA((5,)),
            pltpu.SemaphoreType.DMA((3 * (model // PAIR) + 4,)),
        ],
        compiler_params=limits,
        name="opening",
    )(*(left(array) for array in (micro, segment, gain, table, w_query, w_key, w_value, w_out)))

    for tick_index in range(1, TICKS):
        x_first = passed_along(out, 1)
        (rest,) = call(third_kernel, "third", [kept((length, far), BF16)], [], (mixed, x_last, wo))
        x_last = passed_along(rest, 1)
        state = call(
            first_kernel, "first",
            [
                kept((length, acc_width), F32), kept((length, HD), F32),
                kept((length, PAIR), F32), kept((length, length), F32),
            ],
            [], (x_first, gain, table, wq, wk, wv),
        )
        last = tick_index == TICKS - 1
        if last:
            shapes = [jax.ShapeDtypeStruct((1, length, model), BF16)]
            scratch = [pltpu.VMEM((length, Q_WIDTH), BF16), *mixing]
        else:
            shapes = [kept((length + EXTRA, near), BF16), kept((length, Q_WIDTH), BF16)]
            scratch = mixing
        got = call(
            functools.partial(second_kernel, last), "second", shapes, scratch,
            (x_first, x_last, gain, wq, wk, wv, wo, *state),
        )
        if last:
            return got[0]
        out, mixed = got


def solution(mesh):
    in_specs = (
        P(("groups", "section"), None, None),
        P(("groups", "section"), None),
        P("section", None),
        P("section", None, None),
        P("section", None, None),
        P("section", None, None),
        P("section", None, None),
    )
    out_specs = P(("groups", "section"), None, None)
    return jax.shard_map(body, mesh=mesh, in_specs=in_specs, out_specs=out_specs, check_vma=False)
```

time: 135 us -> 59.5 us (0.44)
  matrix products: 55.1 us -> 0 us
  Pallas kernels: 0 us -> 32.6 us
  local copies, waits for them, and re-layouts: 26.9 us -> 0 us
  waiting for transfers between devices: 38.5 us -> 23.1 us
  other arithmetic: 9.85 us -> 0 us
    dot_general x20 -> x0, matrix products: 55.1 us -> none  [the longest x4 16.6 us: respond(): jnp.einsum('kgij,jkd->ikgd', shares, value_rows, preferred_element_type=j...]
    pallas_call x0 -> x10, Pallas kernels: none -> 32.6 us  [the longest x9 20.7 us: call(): pl.pallas_call(kernel, out_shape=shapes, in_specs=[VMEM] * len(args), out...]
    ppermute x6, waiting for transfers between devices: 38.5 us -> 23.1 us  [passed_along(): lax.ppermute(array, 'section', [(i, (i + by) % length) for i in range(len...]
    dot_general x2 -> x0, local copies, waits for them, and re-layouts: 10.5 us -> none  [the longest x1 6.45 us: project(): jnp.dot(normed, wq_layer, preferred_element_type=jnp.float32)]
    convert_element_type x4 -> x0, local copies, waits for them, and re-layouts: 7.77 us -> none  [respond(): mixed = jnp.einsum('kgij,jkd->ikgd', shares, value_rows, preferred_elemen...]
    reshape x4 -> x0, local copies, waits for them, and re-layouts: 5.91 us -> none  [respond(): mixed = mixed.reshape(stop - start, HEADS * HD)]
    another operation x8 -> x0, other arithmetic: 3.98 us -> none
    unnamed x26 -> x0, local copies, waits for them, and re-layouts: 2.75 us -> none
  transfers between devices with their start and end apart: 6 -> 6, of which waited for: 5 -> 6; matrix products, arithmetic and copies ran while one was open for 14% -> 0% of each run, Pallas kernels for 0% -> 8%
where the time goes in v2:
time: 59.5 us; the launch traced here: 59.4 us
  Pallas kernels  32.6 us (55%)
  waiting for transfers between devices  23.1 us (39%)
  starting transfers between devices  3.6 us (6%)
    ppermute x6, waiting for transfers between devices, passed_along(): lax.ppermute(array, 'section', [(i, (i + by) % length) for i in range(len...  23.1 us
    pallas_call x9, Pallas kernels, call(): pl.pallas_call(kernel, out_shape=shapes, in_specs=[VMEM] * len(args), out...  20.7 us
    pallas_call x1, Pallas kernels, body(): pl.pallas_call(opening_kernel, out_shape=(kept((length + EXTRA, near), BF...  11.9 us
    ppermute x6, starting transfers between devices, passed_along(): lax.ppermute(array, 'section', [(i, (i + by) % length) for i in range(len...  3.6 us
  transfers between devices with their start and end apart: 6, of which 6 were waited for; matrix products, arithmetic and copies ran while one was open for 0% of the time, Pallas kernels for 8%

profile of v2, /device:TPU:0, one launch (start us, length us, event | category | flops | bytes accessed | tf_op | source)
XLA Modules:
  0.0 59.4 jit_solution(4572877562134808177)
XLA Ops:
  0.0 11.9 %opening.1 = (bf16[208,512]{1,0:T(8,128)(2,1)S(1)}, bf16[192,2048]{1,0:T(8,128)(2,1)S(1)}, bf16[192,512]{1,0:T(8,128)(2,1)S(1)}, bf16[1024,2048]{1,0:T(8,128)(2,...) custom-call(bf16[1,192,1024]{2,1,0:T(8,128)(2,1)} %x_hbm.1, ...), custom_call_target="tpu_custom_call" | custom-call | tf_op jit(solution)/shard_map/opening/pallas_call | solution.py:289
  11.9 0.5 collective-permute-start
  12.4 0.6 third.3
  13.0 2.7 %collective-permute-start.1 = (bf16[192,512]{1,0:T(8,128)(2,1)S(1)}, bf16[192,512]{1,0:T(8,128)(2,1)S(1)}, u32[]{:S(2)}, u32[]{:S(2)}) collective-permute-start(bf16[192,512]{1,0:T(8,128)(2,1)S(1)} %third.3), channel_id=1, source_target_pairs={{0,1},{1,2},{2,3},{3,4},{4,5},{5,6},{6,7},{7,8},{8,9},{9,10},{10,1... | collective-permute-start | bytes 589832 | tf_op jit(solution)/shard_map/ppermute | solution.py:271
  15.7 5.2 %collective-permute-done.x_ref.x_first = bf16[208,512]{1,0:T(8,128)(2,1)S(1)} collective-permute-done((bf16[208,512]{1,0:T(8,128)(2,1)S(1)}, bf16[208,512]{1,0:T(8,128)(2,1)S(1)}, u32[]{:S(2)}, u32[]{:S(2)}) %collective-permute-start) | collective-permute-done | bytes 213024 | tf_op jit(solution)/shard_map/ppermute | solution.py:271
  20.9 1.0 %first.3 = (f32[192,4096]{1,0:T(8,128)S(1)}, f32[192,128]{1,0:T(8,128)S(1)}, f32[192,256]{1,0:T(8,128)S(1)}, f32[192,192]{1,0:T(8,128)S(1)}) custom-call(bf16[208,512]{1,0:T(8,128)(2,1)S(1)} %collective-permute-done.x_ref.x_first, f32[1,1024]{1,0:T(1,128)S(1)} %get-tuple-element.34.gain_ref, bf16[192,256]{1,0:T(8,128)(2,1)S(1)} %get-tuple-element.38.table_ref, ...), custom_call_target="tpu_custom_call" | custom-call | tf_op jit(solution)/shard_map/first/pallas_call | solution.py:284
  22.0 1.1 %collective-permute-done.1.x_ref = bf16[192,512]{1,0:T(8,128)(2,1)S(1)} collective-permute-done((bf16[192,512]{1,0:T(8,128)(2,1)S(1)}, bf16[192,512]{1,0:T(8,128)(2,1)S(1)}, u32[]{:S(2)}, u32[]{:S(2)}) %collective-permute-start.1) | collective-permute-done | bytes 196640 | tf_op jit(solution)/shard_map/ppermute | solution.py:271
  23.0 4.9 %second.3 = (bf16[208,512]{1,0:T(8,128)(2,1)S(1)}, bf16[192,2048]{1,0:T(8,128)(2,1)S(1)}) custom-call(bf16[208,512]{1,0:T(8,128)(2,1)S(1)} %collective-permute-done.x_ref.x_first, bf16[192,512]{1,0:T(8,128)(2,1)S(1)} %collective-permute-done.1.x_ref, f32[1,1024]{1,0:T(1,128)S(1)} %get-tuple-element.34.gain_ref, ...), custom_call_target="tpu_custom_call" | custom-call | tf_op jit(solution)/shard_map/second/pallas_call | solution.py:284
  27.9 0.2 collective-permute-start.2
  28.2 0.6 third.4
  28.8 0.1 collective-permute-start.3
  28.8 7.3 %collective-permute-done.2.x_ref.x_first = bf16[208,512]{1,0:T(8,128)(2,1)S(1)} collective-permute-done((bf16[208,512]{1,0:T(8,128)(2,1)S(1)}, bf16[208,512]{1,0:T(8,128)(2,1)S(1)}, u32[]{:S(2)}, u32[]{:S(2)}) %collective-permute-start.2) | collective-permute-done | bytes 213024 | tf_op jit(solution)/shard_map/ppermute | solution.py:271
  36.1 1.0 %first.4 = (f32[192,4096]{1,0:T(8,128)S(1)}, f32[192,128]{1,0:T(8,128)S(1)}, f32[192,256]{1,0:T(8,128)S(1)}, f32[192,192]{1,0:T(8,128)S(1)}) custom-call(bf16[208,512]{1,0:T(8,128)(2,1)S(1)} %collective-permute-done.2.x_ref.x_first, f32[1,1024]{1,0:T(1,128)S(1)} %get-tuple-element.34.gain_ref, bf16[192,256]{1,0:T(8,128)(2,1)S(1)} %get-tuple-element.38.table_ref, ...), custom_call_target="tpu_custom_call" | custom-call | tf_op jit(solution)/shard_map/first/pallas_call | solution.py:284
  37.2 1.1 %collective-permute-done.3.x_ref = bf16[192,512]{1,0:T(8,128)(2,1)S(1)} collective-permute-done((bf16[192,512]{1,0:T(8,128)(2,1)S(1)}, bf16[192,512]{1,0:T(8,128)(2,1)S(1)}, u32[]{:S(2)}, u32[]{:S(2)}) %collective-permute-start.3) | collective-permute-done | bytes 196640 | tf_op jit(solution)/shard_map/ppermute | solution.py:271
  38.2 4.9 %second.4 = (bf16[208,512]{1,0:T(8,128)(2,1)S(1)}, bf16[192,2048]{1,0:T(8,128)(2,1)S(1)}) custom-call(bf16[208,512]{1,0:T(8,128)(2,1)S(1)} %collective-permute-done.2.x_ref.x_first, bf16[192,512]{1,0:T(8,128)(2,1)S(1)} %collective-permute-done.3.x_ref, f32[1,1024]{1,0:T(1,128)S(1)} %get-tuple-element.34.gain_ref, ...), custom_call_target="tpu_custom_call" | custom-call | tf_op jit(solution)/shard_map/second/pallas_call | solution.py:284
  43.1 0.1 collective-permute-start.4
  43.2 0.6 third.5
  43.8 0.1 collective-permute-start.5
  43.9 7.3 %collective-permute-done.4.x_ref.x_first = bf16[208,512]{1,0:T(8,128)(2,1)S(1)} collective-permute-done((bf16[208,512]{1,0:T(8,128)(2,1)S(1)}, bf16[208,512]{1,0:T(8,128)(2,1)S(1)}, u32[]{:S(2)}, u32[]{:S(2)}) %collective-permute-start.4) | collective-permute-done | bytes 213024 | tf_op jit(solution)/shard_map/ppermute | solution.py:271
  51.2 1.0 %first.5 = (f32[192,4096]{1,0:T(8,128)S(1)}, f32[192,128]{1,0:T(8,128)S(1)}, f32[192,256]{1,0:T(8,128)S(1)}, f32[192,192]{1,0:T(8,128)S(1)}) custom-call(bf16[208,512]{1,0:T(8,128)(2,1)S(1)} %collective-permute-done.4.x_ref.x_first, f32[1,1024]{1,0:T(1,128)S(1)} %get-tuple-element.34.gain_ref, bf16[192,256]{1,0:T(8,128)(2,1)S(1)} %get-tuple-element.38.table_ref, ...), custom_call_target="tpu_custom_call" | custom-call | tf_op jit(solution)/shard_map/first/pallas_call | solution.py:284
  52.2 1.1 %collective-permute-done.5.x_ref = bf16[192,512]{1,0:T(8,128)(2,1)S(1)} collective-permute-done((bf16[192,512]{1,0:T(8,128)(2,1)S(1)}, bf16[192,512]{1,0:T(8,128)(2,1)S(1)}, u32[]{:S(2)}, u32[]{:S(2)}) %collective-permute-start.5) | collective-permute-done | bytes 196640 | tf_op jit(solution)/shard_map/ppermute | solution.py:271
  53.3 6.1 %second.5 = bf16[1,192,1024]{2,1,0:T(8,128)(2,1)} custom-call(bf16[208,512]{1,0:T(8,128)(2,1)S(1)} %collective-permute-done.4.x_ref.x_first, bf16[192,512]{1,0:T(8,128)(2,1)S(1)} %collective-permute-done.5.x_ref, f32[1,1024]{1,0:T(1,128)S(1)} %get-tuple-element.34.gain_ref, bf16[1024,2048]{1,0:T(8,128)(2,1)S(1)} %get-tuple-element.35.wq_ref, ...), custom_call_target="tpu_custom_call" | custom-call | tf_op jit(solution)/shard_map/second/pallas_call | solution.py:284
Async XLA Ops:
  11.9 9.0 %collective-permute-start = (bf16[208,512]{1,0:T(8,128)(2,1)S(1)}, bf16[208,512]{1,0:T(8,128)(2,1)S(1)}, u32[]{:S(2)}, u32[]{:S(2)}) collective-permute-start(bf16[208,512]{1,0:T(8,128)(2,1)S(1)} %get-tuple-element.30), channel_id=1, source_target_pairs={{0,1},{1,2},{2,3},{3,4},{4,5},{5,6},{6,7},{7,8},{8,9},{9,10},{10,1... | collective-permute-start | bytes 638984 | tf_op jit(solution)/shard_map/ppermute | solution.py:271
  13.0 10.0 %collective-permute-start.1 = (bf16[192,512]{1,0:T(8,128)(2,1)S(1)}, bf16[192,512]{1,0:T(8,128)(2,1)S(1)}, u32[]{:S(2)}, u32[]{:S(2)}) collective-permute-start(bf16[192,512]{1,0:T(8,128)(2,1)S(1)} %third.3), channel_id=1, source_target_pairs={{0,1},{1,2},{2,3},{3,4},{4,5},{5,6},{6,7},{7,8},{8,9},{9,10},{10,1... | collective-permute-start | bytes 589832 | tf_op jit(solution)/shard_map/ppermute | solution.py:271
  27.9 8.2 %collective-permute-start.2 = (bf16[208,512]{1,0:T(8,128)(2,1)S(1)}, bf16[208,512]{1,0:T(8,128)(2,1)S(1)}, u32[]{:S(2)}, u32[]{:S(2)}) collective-permute-start(bf16[208,512]{1,0:T(8,128)(2,1)S(1)} %get-tuple-element.43), channel_id=1, source_target_pairs={{0,1},{1,2},{2,3},{3,4},{4,5},{5,6},{6,7},{7,8},{8,9},{9,10},{10,1... | collective-permute-start | bytes 638984 | tf_op jit(solution)/shard_map/ppermute | solution.py:271
  28.8 9.5 %collective-permute-start.3 = (bf16[192,512]{1,0:T(8,128)(2,1)S(1)}, bf16[192,512]{1,0:T(8,128)(2,1)S(1)}, u32[]{:S(2)}, u32[]{:S(2)}) collective-permute-start(bf16[192,512]{1,0:T(8,128)(2,1)S(1)} %third.4), channel_id=1, source_target_pairs={{0,1},{1,2},{2,3},{3,4},{4,5},{5,6},{6,7},{7,8},{8,9},{9,10},{10,1... | collective-permute-start | bytes 589832 | tf_op jit(solution)/shard_map/ppermute | solution.py:271
  43.1 8.0 %collective-permute-start.4 = (bf16[208,512]{1,0:T(8,128)(2,1)S(1)}, bf16[208,512]{1,0:T(8,128)(2,1)S(1)}, u32[]{:S(2)}, u32[]{:S(2)}) collective-permute-start(bf16[208,512]{1,0:T(8,128)(2,1)S(1)} %get-tuple-element.49), channel_id=1, source_target_pairs={{0,1},{1,2},{2,3},{3,4},{4,5},{5,6},{6,7},{7,8},{8,9},{9,10},{10,1... | collective-permute-start | bytes 638984 | tf_op jit(solution)/shard_map/ppermute | solution.py:271
  43.8 9.5 %collective-permute-start.5 = (bf16[192,512]{1,0:T(8,128)(2,1)S(1)}, bf16[192,512]{1,0:T(8,128)(2,1)S(1)}, u32[]{:S(2)}, u32[]{:S(2)}) collective-permute-start(bf16[192,512]{1,0:T(8,128)(2,1)S(1)} %third.5), channel_id=1, source_target_pairs={{0,1},{1,2},{2,3},{3,4},{4,5},{5,6},{6,7},{7,8},{8,9},{9,10},{10,1... | collective-permute-start | bytes 589832 | tf_op jit(solution)/shard_map/ppermute | solution.py:271

commit v3 on v0

v3 whole, which is shorter than its diff:
```python
import functools

import jax
import jax.numpy as jnp
import numpy as np
from jax import lax
from jax.experimental import pallas as pl
from jax.experimental.pallas import tpu as pltpu
from jax.sharding import PartitionSpec as P

HEADS = 16
KV_HEADS = 8
HD = 128
TICKS = 4
MAX_LEN = 96
CHUNKS = 3
EXTRA = 16
LIFT = 16.0
HIDDEN = -1e30
PAIR = 2 * HD
Q_WIDTH = HEADS * HD
KV_WIDTH = KV_HEADS * HD
BF16 = jnp.bfloat16
F32 = jnp.float32


def rope_table():
    middle = HD // 2
    spacing = 1000000.0 ** (-2.0 * np.arange(middle) / HD)
    angles = np.arange(MAX_LEN)[:, None] * spacing[None, :]
    cosine, sine = np.cos(angles), np.sin(angles)
    whole = np.concatenate([cosine, cosine, -sine, sine], axis=1).astype(np.float32)
    high = whole.astype(jnp.bfloat16).astype(np.float32)
    low = (whole - high).astype(jnp.bfloat16).astype(np.float32)
    return np.concatenate([high, low], axis=0)


def tables_of(ids_row, table):
    length = ids_row.shape[1]
    across = jnp.broadcast_to(ids_row, (length, length))
    down = across.T
    row_index = lax.broadcasted_iota(jnp.int32, (length, length), 0)
    column = lax.broadcasted_iota(jnp.int32, (length, length), 1)
    matched = across == down
    places = jnp.sum(jnp.where(matched & (column < row_index), 1.0, 0.0), axis=1, keepdims=True)
    bias = jnp.where(matched & (column <= row_index), 0.0, HIDDEN)
    slots = lax.broadcasted_iota(jnp.int32, (length, 2 * MAX_LEN), 1)
    slots = jnp.where(slots >= MAX_LEN, slots - MAX_LEN, slots).astype(F32)
    one_hot = jnp.where(slots == places, 1.0, 0.0).astype(BF16)
    factors = jnp.dot(one_hot, table, preferred_element_type=F32)
    return factors, bias


def rotated(values, cosine, sine):
    return values * cosine + pltpu.roll(values, HD // 2, 1) * sine


def layer(x, gain, weights, wait, cos_rows, bias_rows, kept_keys, kept_values, k_ref, v_ref, mixed_ref, write):
    size, model = x.shape
    wq_ref, wk_ref, wv_ref, wo_ref = weights
    scale = lax.rsqrt(jnp.mean(x * x, axis=1, keepdims=True) + 1e-05) * (1.0 / LIFT)
    lifted = (x * gain).astype(BF16)
    cosine = cos_rows[:, :HD] * scale
    sine = cos_rows[:, HD:] * scale
    factor = HD ** (-0.5) * np.log2(np.e)
    cosine_q = cosine * factor
    sine_q = sine * factor

    for start in range(0, KV_WIDTH, PAIR):
        wait("k", start)
        got = jnp.dot(lifted, wk_ref[:, start : start + PAIR], preferred_element_type=F32)
        for half in range(0, PAIR, HD):
            turned = rotated(got[:, half : half + HD], cosine, sine)
            k_ref[:, start + half : start + half + HD] = turned.astype(BF16)
    for start in range(0, KV_WIDTH, PAIR):
        wait("v", start)
        got = jnp.dot(lifted, wv_ref[:, start : start + PAIR], preferred_element_type=F32)
        v_ref[:, start : start + PAIR] = (got * scale).astype(BF16)
    queries = []
    for start in range(0, Q_WIDTH, PAIR):
        wait("q", start)
        got = jnp.dot(lifted, wq_ref[:, start : start + PAIR], preferred_element_type=F32)
        upper = rotated(got[:, :HD], cosine_q, sine_q)
        lower = rotated(got[:, HD:], cosine_q, sine_q)
        queries.append(jnp.concatenate([upper, lower], axis=0).astype(BF16))

    count = bias_rows.shape[1]
    ones = jnp.ones((count, HD), BF16)
    groups = range(KV_HEADS)
    scores = []
    for group in groups:
        lanes = slice(group * HD, (group + 1) * HD)
        key_rows = jnp.concatenate([rows[:, lanes] for rows in kept_keys] + [k_ref[:, lanes]], axis=0)
        got = lax.dot_general(queries[group], key_rows, (((1,), (1,)), ((), ())), preferred_element_type=F32)
        scores.append(got.reshape(2, size, count) + bias_rows[None])
    most = [jnp.max(part, axis=2, keepdims=True) for part in scores]
    expo = [jnp.exp2(scores[g] - most[g]).astype(BF16).reshape(2 * size, count) for g in groups]
    got = []
    for group in groups:
        lanes = slice(group * HD, (group + 1) * HD)
        value_rows = jnp.concatenate([rows[:, lanes] for rows in kept_values] + [v_ref[:, lanes]], axis=0)
        value_rows = jnp.concatenate([value_rows, ones], axis=1)
        got.append(jnp.dot(expo[group], value_rows, preferred_element_type=F32))
    for group in groups:
        total = got[group][:, HD:]
        inverse = pl.reciprocal(total, approx=True)
        inverse = inverse * (2.0 - total * inverse)
        mixed = (got[group][:, :HD] * inverse).astype(BF16)
        mixed_ref[:, group * PAIR : group * PAIR + HD] = mixed[:size]
        mixed_ref[:, group * PAIR + HD : (group + 1) * PAIR] = mixed[size:]
    for start in range(0, model, PAIR):
        wait("o", start)
        update = jnp.dot(mixed_ref[...], wo_ref[:, start : start + PAIR], preferred_element_type=F32)
        write(start, x[:, start : start + PAIR] + update)


def first_key(low):
    return max(0, low - MAX_LEN + 1) // 16 * 16


def kept_rows(index, size, refs):
    least = first_key(index * size)
    return [ref[max(0, least - place * size) :] for place, ref in enumerate(refs) if (place + 1) * size > least]


def write_ids(ids_row, out_ref, size):
    length = ids_row.shape[1]
    out_ref[size:, :] = jnp.zeros((EXTRA, out_ref.shape[1]), BF16)
    out_ref[size:, :length] = jnp.broadcast_to(ids_row, (EXTRA, length)).astype(BF16)


def opening_kernel(
    size, x_hbm, ids_hbm, gain_hbm, table_hbm, wq_hbm, wk_hbm, wv_hbm, wo_hbm,
    out_ref, k_ref, v_ref, cos_ref, bias_ref, wq_ref, wk_ref, wv_ref, wo_ref, gain_ref, table_ref, *refs,
):
    rest_refs, refs = refs[: CHUNKS - 1], refs[CHUNKS - 1 :]
    x_ref, ids_ref, raw_gain, raw_table, mixed_ref, small_sems, sems = refs
    small = [
        pltpu.make_async_copy(ids_hbm, ids_ref, small_sems.at[0]),
        pltpu.make_async_copy(table_hbm, raw_table, small_sems.at[1]),
        pltpu.make_async_copy(gain_hbm, raw_gain, small_sems.at[2]),
        pltpu.make_async_copy(x_hbm.at[0, :size], x_ref, small_sems.at[3]),
    ]
    late = [
        pltpu.make_async_copy(x_hbm.at[0, (i + 1) * size : (i + 2) * size], rest_refs[i], small_sems.at[4 + i])
        for i in range(CHUNKS - 1)
    ]
    made = []

    def batch(source, target, rows, lanes):
        step = (rows.stop - rows.start) // 4
        copies = []
        for low in range(rows.start, rows.stop, step):
            part = (slice(low, low + step), lanes)
            copies.append(pltpu.make_async_copy(source.at[(0, *part)], target.at[part], sems.at[len(made)]))
            made.append(copies[-1])
        return copies

    model, half = wk_ref.shape[0], Q_WIDTH // 2
    everything = slice(0, model)
    batches = [
        batch(wk_hbm, wk_ref, everything, slice(0, KV_WIDTH)),
        batch(wv_hbm, wv_ref, everything, slice(0, KV_WIDTH)),
        batch(wq_hbm, wq_ref, everything, slice(0, half)),
        batch(wq_hbm, wq_ref, everything, slice(half, Q_WIDTH)),
        batch(wo_hbm, wo_ref, slice(0, Q_WIDTH), slice(0, model // 2)),
        batch(wo_hbm, wo_ref, slice(0, Q_WIDTH), slice(model // 2, model)),
    ]
    arrivals = {("k", 0): 0, ("v", 0): 1, ("q", 0): 2, ("q", half): 3, ("o", 0): 4, ("o", model // 2): 5}

    def begin(index):
        if index < len(batches):
            for copy in batches[index]:
                copy.start()
        if index == len(batches):
            for copy in late:
                copy.start()

    def wait(name, start):
        index = arrivals.get((name, start))
        if index is not None:
            for copy in batches[index]:
                copy.wait()
            begin(index + 2)

    for copy in small:
        copy.start()
    begin(0)
    begin(1)
    for copy in small:
        copy.wait()
    gain_ref[...] = raw_gain[...].astype(F32) * LIFT
    table_ref[...] = raw_table[...].astype(BF16)
    ids_row = ids_ref[...].astype(F32)
    factors, bias = tables_of(ids_row, table_ref[...])
    cos_ref[...] = factors
    bias_ref[...] = bias
    write_ids(ids_row, out_ref, size)

    def write(start, values):
        out_ref[:size, start : start + PAIR] = values.astype(BF16)

    layer(
        x_ref[...].astype(F32), gain_ref[...], (wq_ref, wk_ref, wv_ref, wo_ref), wait,
        cos_ref[:size, :], bias_ref[:size, :size], [], [], k_ref, v_ref, mixed_ref, write,
    )
    for copy in late:
        copy.wait()


def chunk_kernel(index, last, x_ref, gain_ref, wq_ref, wk_ref, wv_ref, wo_ref, *refs):
    refs = list(refs)
    mixed_ref = refs.pop(-1)
    size = mixed_ref.shape[0]
    low, high = index * size, (index + 1) * size
    if index == 0:
        table_ref = refs.pop(0)
        out_ref, k_ref, v_ref, cos_ref, bias_ref = refs
        factors, bias = tables_of(x_ref[size:, : CHUNKS * size].astype(F32)[:1], table_ref[...])
        cos_ref[...] = factors
        bias_ref[...] = bias
        if not last:
            out_ref[size:, :] = x_ref[size:, :]
        keys, values = [], []
    else:
        cos_ref, bias_ref = refs[:2]
        keys, values, refs = refs[2 : 2 + index], refs[2 + index : 2 + 2 * index], refs[2 + 2 * index :]
        if last and index == CHUNKS - 1:
            done, (whole_ref, out_ref, k_ref, v_ref, sems) = refs[:index], refs[index:]
            copies = [
                pltpu.make_async_copy(done[i].at[:size], whole_ref.at[0, i * size : (i + 1) * size], sems.at[i])
                for i in range(index)
            ]
            for copy in copies:
                copy.start()
        else:
            out_ref, k_ref, v_ref = refs

    def write(start, result):
        out_ref[:size, start : start + PAIR] = result.astype(BF16)

    layer(
        x_ref[:size, :].astype(F32), gain_ref[...], (wq_ref, wk_ref, wv_ref, wo_ref), lambda name, start: None,
        cos_ref[low:high, :], bias_ref[low:high, first_key(low) : high],
        kept_rows(index, size, keys), kept_rows(index, size, values), k_ref, v_ref, mixed_ref, write,
    )
    if last and index == CHUNKS - 1:
        copy = pltpu.make_async_copy(out_ref, whole_ref.at[0, low:high], sems.at[index])
        copy.start()
        for each in copies + [copy]:
            each.wait()


VMEM = pl.BlockSpec(memory_space=pltpu.VMEM)
HBM = pl.BlockSpec(memory_space=pltpu.HBM)


def kept(shape, dtype):
    return pltpu.VMEM(shape, dtype)


def held(array):
    return pltpu.with_memory_space_constraint(array, pltpu.VMEM)


def left(array):
    return pltpu.with_memory_space_constraint(array, pltpu.HBM)


def passed_along(array, by):
    length = lax.axis_size("section")
    return lax.ppermute(array, "section", [(i, (i + by) % length) for i in range(length)])


def body(micro, segment, gain, w_query, w_key, w_value, w_out):
    length, model = micro.shape[1], micro.shape[2]
    size = length // CHUNKS
    limits = pltpu.CompilerParams(vmem_limit_bytes=32 * 1024 * 1024)
    table = jnp.asarray(rope_table())
    rows = [size + EXTRA] + [size] * (CHUNKS - 1)
    key_values = [kept((size, KV_WIDTH), BF16)] * 2
    tables = [kept((length, PAIR), F32), kept((length, length), F32)]
    mixing = pltpu.VMEM((size, Q_WIDTH), BF16)

    got = pl.pallas_call(
        functools.partial(opening_kernel, size),
        out_shape=(
            kept((rows[0], model), BF16),
            *key_values,
            *tables,
            kept((model, Q_WIDTH), BF16),
            kept((model, KV_WIDTH), BF16),
            kept((model, KV_WIDTH), BF16),
            kept((Q_WIDTH, model), BF16),
            kept((1, model), F32),
            kept(table.shape, BF16),
            *[kept((size, model), BF16)] * (CHUNKS - 1),
        ),
        in_specs=[HBM] * 8,
        out_specs=(VMEM,) * (10 + CHUNKS),
        scratch_shapes=[
            pltpu.VMEM((size, model), BF16),
            pltpu.VMEM(segment.shape, jnp.int32),
            pltpu.VMEM(gain.shape, BF16),
            pltpu.VMEM(table.shape, F32),
            mixing,
            pltpu.SemaphoreType.DMA((3 + CHUNKS,)),
            pltpu.SemaphoreType.DMA((24,)),
        ],
        compiler_params=limits,
        name="opening",
    )(*(left(array) for array in (micro, segment, gain, table, w_query, w_key, w_value, w_out)))
    out, k_rows, v_rows, cosines, bias = got[:5]
    weights = (got[9], *got[5:9])
    table = got[10]
    streams = [out, *got[11:]]

    for tick_index in range(TICKS):
        last = tick_index == TICKS - 1
        outs, keys, values = [], [], []
        for index in range(CHUNKS):
            if tick_index == 0 and index == 0:
                outs.append(passed_along(streams[0], 1))
                keys.append(k_rows)
                values.append(v_rows)
                continue
            args = [streams[index], *weights]
            shapes = [kept((rows[index], model), BF16), *key_values]
            scratch = [mixing]
            if index == 0:
                args.append(table)
                shapes += tables
            else:
                args += [cosines, bias, *keys, *values]
            specs = [VMEM] * len(shapes)
            ending = last and index == CHUNKS - 1
            if ending:
                args += outs
                shapes = [jax.ShapeDtypeStruct((1, length, model), BF16)]
                specs = [pl.BlockSpec(memory_space=pl.ANY)]
                scratch = [
                    pltpu.VMEM((size, model), BF16), *[pltpu.VMEM((size, KV_WIDTH), BF16)] * 2,
                    pltpu.SemaphoreType.DMA((CHUNKS,)), mixing,
                ]
            got = pl.pallas_call(
                functools.partial(chunk_kernel, index, last),
                out_shape=tuple(shapes), in_specs=[VMEM] * len(args), out_specs=tuple(specs),
                scratch_shapes=scratch, compiler_params=limits, name="chunk_%d_%d" % (tick_index, index),
            )(*map(held, args))
            if ending:
                return got[0]
            if index == 0:
                cosines, bias = got[3:]
            keys.append(got[1])
            values.append(got[2])
            outs.append(got[0] if last else passed_along(got[0], 1))
        streams = outs


def solution(mesh):
    in_specs = (
        P(("groups", "section"), None, None),
        P(("groups", "section"), None),
        P("section", None),
        P("section", None, None),
        P("section", None, None),
        P("section", None, None),
        P("section", None, None),
    )
    out_specs = P(("groups", "section"), None, None)
    return jax.shard_map(body, mesh=mesh, in_specs=in_specs, out_specs=out_specs, check_vma=False)
```

time: 135 us -> 51.8 us (0.38)
  matrix products: 55.1 us -> 0 us
  Pallas kernels: 0 us -> 41.6 us
  waiting for transfers between devices: 38.5 us -> 1.25 us
  local copies, waits for them, and re-layouts: 26.9 us -> 0 us
  other arithmetic: 9.85 us -> 0 us
  starting transfers between devices: 3.85 us -> 8.52 us
    dot_general x20 -> x0, matrix products: 55.1 us -> none  [the longest x4 16.6 us: respond(): jnp.einsum('kgij,jkd->ikgd', shares, value_rows, preferred_element_type=j...]
    pallas_call x0 -> x12, Pallas kernels: none -> 41.6 us  [the longest x11 33.8 us: body(): pl.pallas_call(functools.partial(chunk_kernel, index, last), out_shape=tu...]
    ppermute x6 -> x9, waiting for transfers between devices: 38.5 us -> 1.25 us  [passed_along(): lax.ppermute(array, 'section', [(i, (i + by) % length) for i in range(len...]
    dot_general x2 -> x0, local copies, waits for them, and re-layouts: 10.5 us -> none  [the longest x1 6.45 us: project(): jnp.dot(normed, wq_layer, preferred_element_type=jnp.float32)]
    convert_element_type x4 -> x0, local copies, waits for them, and re-layouts: 7.77 us -> none  [respond(): mixed = jnp.einsum('kgij,jkd->ikgd', shares, value_rows, preferred_elemen...]
    reshape x4 -> x0, local copies, waits for them, and re-layouts: 5.91 us -> none  [respond(): mixed = mixed.reshape(stop - start, HEADS * HD)]
    ppermute x6 -> x9, starting transfers between devices: 3.85 us -> 8.52 us  [passed_along(): lax.ppermute(array, 'section', [(i, (i + by) % length) for i in range(len...]
    another operation x8 -> x0, other arithmetic: 3.98 us -> none
  transfers between devices with their start and end apart: 6 -> 9, of which waited for: 5 -> 1; matrix products, arithmetic and copies ran while one was open for 14% -> 0% of each run, Pallas kernels for 0% -> 59%
where the time goes in v3:
time: 51.8 us; the launch traced here: 51.6 us
  Pallas kernels  41.6 us (80%)
  starting transfers between devices  8.52 us (16%)
  waiting for transfers between devices  1.25 us (2%)
    pallas_call x11, Pallas kernels, body(): pl.pallas_call(functools.partial(chunk_kernel, index, last), out_shape=tu...  33.8 us
    ppermute x9, starting transfers between devices, passed_along(): lax.ppermute(array, 'section', [(i, (i + by) % length) for i in range(len...  8.52 us
    pallas_call x1, Pallas kernels, body(): pl.pallas_call(functools.partial(opening_kernel, size), out_shape=(kept((...  7.82 us
    ppermute x9, waiting for transfers between devices, passed_along(): lax.ppermute(array, 'section', [(i, (i + by) % length) for i in range(len...  1.25 us
  transfers between devices with their start and end apart: 9, of which 1 were waited for; matrix products, arithmetic and copies ran while one was open for 0% of the time, Pallas kernels for 59%

profile of v3, /device:TPU:0, one launch (start us, length us, event | category | flops | bytes accessed | tf_op | source)
XLA Modules:
  0.0 51.6 jit_solution(15038540278661069810)
XLA Ops:
  0.0 7.8 %opening.1 = (bf16[80,1024]{1,0:T(8,128)(2,1)S(1)}, bf16[64,1024]{1,0:T(8,128)(2,1)S(1)}, bf16[64,1024]{1,0:T(8,128)(2,1)S(1)}, f32[192,256]{1,0:T(8,128)S(1)}, ...) custom-call(bf16[1,192,1024]{2,1,0:T(8,128)(2,1)} %x_hbm.1, ...), custom_call_target="tpu_custom_call" | custom-call | tf_op jit(solution)/shard_map/opening/pallas_call | solution.py:285
  7.8 0.5 collective-permute-start.1
  8.3 2.8 %chunk_0_1.1 = (bf16[64,1024]{1,0:T(8,128)(2,1)S(1)}, bf16[64,1024]{1,0:T(8,128)(2,1)S(1)}, bf16[64,1024]{1,0:T(8,128)(2,1)S(1)}) custom-call(bf16[64,1024]{1,0:T(8,128)(2,1)S(1)} %get-tuple-element.57.x_ref, f32[1,1024]{1,0:T(1,128)S(1)} %get-tuple-element.49.gain_ref, bf16[1024,2048]{1,0:T(8,128)(2,1)S(1)} %get-tuple-element.50.wq_ref, ...), custom_call_target="tpu_custom_call" | custom-call | tf_op jit(solution)/shard_map/chunk_0_1/pallas_call | solution.py:345
  11.2 2.7 %collective-permute-start.2 = (bf16[64,1024]{1,0:T(8,128)(2,1)S(1)}, bf16[64,1024]{1,0:T(8,128)(2,1)S(1)}, u32[]{:S(2)}, u32[]{:S(2)}) collective-permute-start(bf16[64,1024]{1,0:T(8,128)(2,1)S(1)} %get-tuple-element.67), channel_id=1, source_target_pairs={{0,1},{1,2},{2,3},{3,4},{4,5},{5,6},{6,7},{7,8},{8,9},{9,10},{10,1... | collective-permute-start | bytes 393224 | tf_op jit(solution)/shard_map/ppermute | solution.py:272
  13.8 3.3 %chunk_0_2.1 = (bf16[64,1024]{1,0:T(8,128)(2,1)S(1)}, bf16[64,1024]{1,0:T(8,128)(2,1)}, bf16[64,1024]{1,0:T(8,128)(2,1)}) custom-call(bf16[64,1024]{1,0:T(8,128)(2,1)S(1)} %get-tuple-element.48.x_ref, f32[1,1024]{1,0:T(1,128)S(1)} %get-tuple-element.49.gain_ref, bf16[1024,2048]{1,0:T(8,128)(2,1)S(1)} %get-tuple-element.50.wq_ref, ...), custom_call_target="tpu_custom_call" | custom-call | tf_op jit(solution)/shard_map/chunk_0_2/pallas_call | solution.py:345
  17.2 0.0 collective-permute-start
  17.2 0.0 collective-permute-done.1.x_ref
  17.2 3.0 %chunk_1_0.1 = (bf16[80,1024]{1,0:T(8,128)(2,1)S(1)}, bf16[64,1024]{1,0:T(8,128)(2,1)S(1)}, bf16[64,1024]{1,0:T(8,128)(2,1)S(1)}, f32[192,256]{1,0:T(8,128)S(1)}, f32[192,192]{1,0:T(8,128)S(1)}) custom-call(bf16[80,1024]{1,0:T(8,128)(2,1)S(1)} %collective-permute-done.1.x_ref, f32[1,1024]{1,0:T(1,128)S(1)} %get-tuple-element.49.gain_ref, ...), custom_call_target="tpu_custom_call" | custom-call | tf_op jit(solution)/shard_map/chunk_1_0/pallas_call | solution.py:345
  20.2 1.7 %collective-permute-start.4 = (bf16[80,1024]{1,0:T(8,128)(2,1)S(1)}, bf16[80,1024]{1,0:T(8,128)(2,1)S(1)}, u32[]{:S(2)}, u32[]{:S(2)}) collective-permute-start(bf16[80,1024]{1,0:T(8,128)(2,1)S(1)} %get-tuple-element.72), channel_id=1, source_target_pairs={{0,1},{1,2},{2,3},{3,4},{4,5},{5,6},{6,7},{7,8},{8,9},{9,10},{10,1... | collective-permute-start | bytes 491528 | tf_op jit(solution)/shard_map/ppermute | solution.py:272
  21.9 0.0 collective-permute-done.2.x_ref
  21.9 2.8 %chunk_1_1.1 = (bf16[64,1024]{1,0:T(8,128)(2,1)S(1)}, bf16[64,1024]{1,0:T(8,128)(2,1)S(1)}, bf16[64,1024]{1,0:T(8,128)(2,1)S(1)}) custom-call(bf16[64,1024]{1,0:T(8,128)(2,1)S(1)} %collective-permute-done.2.x_ref, f32[1,1024]{1,0:T(1,128)S(1)} %get-tuple-element.49.gain_ref, bf16[1024,2048]{1,0:T(8,128)(2,1)S(1)} %get-tuple-element.50.wq_ref, ...), custom_call_target="tpu_custom_call" | custom-call | tf_op jit(solution)/shard_map/chunk_1_1/pallas_call | solution.py:345
  24.7 0.3 collective-permute-start.5
  25.0 0.0 collective-permute-done.x_ref
  25.0 3.3 %chunk_1_2.1 = (bf16[64,1024]{1,0:T(8,128)(2,1)S(1)}, bf16[64,1024]{1,0:T(8,128)(2,1)}, bf16[64,1024]{1,0:T(8,128)(2,1)}) custom-call(bf16[64,1024]{1,0:T(8,128)(2,1)S(1)} %collective-permute-done.x_ref, f32[1,1024]{1,0:T(1,128)S(1)} %get-tuple-element.49.gain_ref, bf16[1024,2048]{1,0:T(8,128)(2,1)S(1)} %get-tuple-element.50.wq_ref, ...), custom_call_target="tpu_custom_call" | custom-call | tf_op jit(solution)/shard_map/chunk_1_2/pallas_call | solution.py:345
  28.3 1.6 %collective-permute-start.3 = (bf16[64,1024]{1,0:T(8,128)(2,1)S(1)}, bf16[64,1024]{1,0:T(8,128)(2,1)S(1)}, u32[]{:S(2)}, u32[]{:S(2)}) collective-permute-start(bf16[64,1024]{1,0:T(8,128)(2,1)S(1)} %get-tuple-element.71), channel_id=1, source_target_pairs={{0,1},{1,2},{2,3},{3,4},{4,5},{5,6},{6,7},{7,8},{8,9},{9,10},{10,1... | collective-permute-start | bytes 393224 | tf_op jit(solution)/shard_map/ppermute | solution.py:272
  29.9 0.0 collective-permute-done.4.x_ref
  29.9 3.0 %chunk_2_0.1 = (bf16[80,1024]{1,0:T(8,128)(2,1)S(1)}, bf16[64,1024]{1,0:T(8,128)(2,1)S(1)}, bf16[64,1024]{1,0:T(8,128)(2,1)S(1)}, f32[192,256]{1,0:T(8,128)S(1)}, f32[192,192]{1,0:T(8,128)S(1)}) custom-call(bf16[80,1024]{1,0:T(8,128)(2,1)S(1)} %collective-permute-done.4.x_ref, f32[1,1024]{1,0:T(1,128)S(1)} %get-tuple-element.49.gain_ref, ...), custom_call_target="tpu_custom_call" | custom-call | tf_op jit(solution)/shard_map/chunk_2_0/pallas_call | solution.py:345
  32.9 0.1 collective-permute-start.7
  33.0 0.0 collective-permute-done.5.x_ref
  33.0 2.8 %chunk_2_1.1 = (bf16[64,1024]{1,0:T(8,128)(2,1)S(1)}, bf16[64,1024]{1,0:T(8,128)(2,1)S(1)}, bf16[64,1024]{1,0:T(8,128)(2,1)S(1)}) custom-call(bf16[64,1024]{1,0:T(8,128)(2,1)S(1)} %collective-permute-done.5.x_ref, f32[1,1024]{1,0:T(1,128)S(1)} %get-tuple-element.49.gain_ref, bf16[1024,2048]{1,0:T(8,128)(2,1)S(1)} %get-tuple-element.50.wq_ref, ...), custom_call_target="tpu_custom_call" | custom-call | tf_op jit(solution)/shard_map/chunk_2_1/pallas_call | solution.py:345
  35.8 1.7 %collective-permute-start.8 = (bf16[64,1024]{1,0:T(8,128)(2,1)S(1)}, bf16[64,1024]{1,0:T(8,128)(2,1)S(1)}, u32[]{:S(2)}, u32[]{:S(2)}) collective-permute-start(bf16[64,1024]{1,0:T(8,128)(2,1)S(1)} %get-tuple-element.85), channel_id=1, source_target_pairs={{0,1},{1,2},{2,3},{3,4},{4,5},{5,6},{6,7},{7,8},{8,9},{9,10},{10,1... | collective-permute-start | bytes 393224 | tf_op jit(solution)/shard_map/ppermute | solution.py:272
  37.5 0.0 collective-permute-done.3.x_ref
  37.5 3.3 %chunk_2_2.1 = (bf16[64,1024]{1,0:T(8,128)(2,1)S(1)}, bf16[64,1024]{1,0:T(8,128)(2,1)}, bf16[64,1024]{1,0:T(8,128)(2,1)}) custom-call(bf16[64,1024]{1,0:T(8,128)(2,1)S(1)} %collective-permute-done.3.x_ref, f32[1,1024]{1,0:T(1,128)S(1)} %get-tuple-element.49.gain_ref, bf16[1024,2048]{1,0:T(8,128)(2,1)S(1)} %get-tuple-element.50.wq_ref, ...), custom_call_target="tpu_custom_call" | custom-call | tf_op jit(solution)/shard_map/chunk_2_2/pallas_call | solution.py:345
  40.8 0.0 collective-permute-start.6
  40.8 0.0 collective-permute-done.7.x_ref
  40.8 3.0 %chunk_3_0.1 = (bf16[80,1024]{1,0:T(8,128)(2,1)S(1)}, bf16[64,1024]{1,0:T(8,128)(2,1)S(1)}, bf16[64,1024]{1,0:T(8,128)(2,1)S(1)}, f32[192,256]{1,0:T(8,128)S(1)}, f32[192,192]{1,0:T(8,128)S(1)}) custom-call(bf16[80,1024]{1,0:T(8,128)(2,1)S(1)} %collective-permute-done.7.x_ref, f32[1,1024]{1,0:T(1,128)S(1)} %get-tuple-element.49.gain_ref, ...), custom_call_target="tpu_custom_call" | custom-call | tf_op jit(solution)/shard_map/chunk_3_0/pallas_call | solution.py:345
  43.8 0.0 collective-permute-done.8.x_ref
  43.8 2.8 %chunk_3_1.1 = (bf16[64,1024]{1,0:T(8,128)(2,1)S(1)}, bf16[64,1024]{1,0:T(8,128)(2,1)S(1)}, bf16[64,1024]{1,0:T(8,128)(2,1)S(1)}) custom-call(bf16[64,1024]{1,0:T(8,128)(2,1)S(1)} %collective-permute-done.8.x_ref, f32[1,1024]{1,0:T(1,128)S(1)} %get-tuple-element.49.gain_ref, bf16[1024,2048]{1,0:T(8,128)(2,1)S(1)} %get-tuple-element.50.wq_ref, ...), custom_call_target="tpu_custom_call" | custom-call | tf_op jit(solution)/shard_map/chunk_3_1/pallas_call | solution.py:345
  46.7 1.2 %collective-permute-done.6.x_ref = bf16[64,1024]{1,0:T(8,128)(2,1)S(1)} collective-permute-done((bf16[64,1024]{1,0:T(8,128)(2,1)S(1)}, bf16[64,1024]{1,0:T(8,128)(2,1)S(1)}, u32[]{:S(2)}, u32[]{:S(2)}) %collective-permute-start.6) | collective-permute-done | bytes 131104 | tf_op jit(solution)/shard_map/ppermute | solution.py:272
  47.9 3.5 %chunk_3_2.1 = bf16[1,192,1024]{2,1,0:T(8,128)(2,1)} custom-call(bf16[64,1024]{1,0:T(8,128)(2,1)S(1)} %collective-permute-done.6.x_ref, f32[1,1024]{1,0:T(1,128)S(1)} %get-tuple-element.49.gain_ref, bf16[1024,2048]{1,0:T(8,128)(2,1)S(1)} %get-tuple-element.50.wq_ref, bf16[1024,1024]{1,0:T(8,128)(2,1)S(1)} %get-tuple-element.51.wk_ref, ...), custom_call_target="tpu_custom_call" | custom-call | tf_op jit(solution)/shard_map/chunk_3_2/pallas_call | solution.py:345
Async XLA Ops:
  7.8 9.4 %collective-permute-start.1 = (bf16[80,1024]{1,0:T(8,128)(2,1)S(1)}, bf16[80,1024]{1,0:T(8,128)(2,1)S(1)}, u32[]{:S(2)}, u32[]{:S(2)}) collective-permute-start(bf16[80,1024]{1,0:T(8,128)(2,1)S(1)} %get-tuple-element.62), channel_id=1, source_target_pairs={{0,1},{1,2},{2,3},{3,4},{4,5},{5,6},{6,7},{7,8},{8,9},{9,10},{10,1... | collective-permute-start | bytes 491528 | tf_op jit(solution)/shard_map/ppermute | solution.py:272
  11.2 10.7 %collective-permute-start.2 = (bf16[64,1024]{1,0:T(8,128)(2,1)S(1)}, bf16[64,1024]{1,0:T(8,128)(2,1)S(1)}, u32[]{:S(2)}, u32[]{:S(2)}) collective-permute-start(bf16[64,1024]{1,0:T(8,128)(2,1)S(1)} %get-tuple-element.67), channel_id=1, source_target_pairs={{0,1},{1,2},{2,3},{3,4},{4,5},{5,6},{6,7},{7,8},{8,9},{9,10},{10,1... | collective-permute-start | bytes 393224 | tf_op jit(solution)/shard_map/ppermute | solution.py:272
  17.2 7.8 %collective-permute-start = (bf16[64,1024]{1,0:T(8,128)(2,1)S(1)}, bf16[64,1024]{1,0:T(8,128)(2,1)S(1)}, u32[]{:S(2)}, u32[]{:S(2)}) collective-permute-start(bf16[64,1024]{1,0:T(8,128)(2,1)S(1)} %get-tuple-element.61), channel_id=1, source_target_pairs={{0,1},{1,2},{2,3},{3,4},{4,5},{5,6},{6,7},{7,8},{8,9},{9,10},{10,1... | collective-permute-start | bytes 393224 | tf_op jit(solution)/shard_map/ppermute | solution.py:272
  20.2 9.7 %collective-permute-start.4 = (bf16[80,1024]{1,0:T(8,128)(2,1)S(1)}, bf16[80,1024]{1,0:T(8,128)(2,1)S(1)}, u32[]{:S(2)}, u32[]{:S(2)}) collective-permute-start(bf16[80,1024]{1,0:T(8,128)(2,1)S(1)} %get-tuple-element.72), channel_id=1, source_target_pairs={{0,1},{1,2},{2,3},{3,4},{4,5},{5,6},{6,7},{7,8},{8,9},{9,10},{10,1... | collective-permute-start | bytes 491528 | tf_op jit(solution)/shard_map/ppermute | solution.py:272
  24.7 8.3 %collective-permute-start.5 = (bf16[64,1024]{1,0:T(8,128)(2,1)S(1)}, bf16[64,1024]{1,0:T(8,128)(2,1)S(1)}, u32[]{:S(2)}, u32[]{:S(2)}) collective-permute-start(bf16[64,1024]{1,0:T(8,128)(2,1)S(1)} %get-tuple-element.76), channel_id=1, source_target_pairs={{0,1},{1,2},{2,3},{3,4},{4,5},{5,6},{6,7},{7,8},{8,9},{9,10},{10,1... | collective-permute-start | bytes 393224 | tf_op jit(solution)/shard_map/ppermute | solution.py:272
  28.3 9.2 %collective-permute-start.3 = (bf16[64,1024]{1,0:T(8,128)(2,1)S(1)}, bf16[64,1024]{1,0:T(8,128)(2,1)S(1)}, u32[]{:S(2)}, u32[]{:S(2)}) collective-permute-start(bf16[64,1024]{1,0:T(8,128)(2,1)S(1)} %get-tuple-element.71), channel_id=1, source_target_pairs={{0,1},{1,2},{2,3},{3,4},{4,5},{5,6},{6,7},{7,8},{8,9},{9,10},{10,1... | collective-permute-start | bytes 393224 | tf_op jit(solution)/shard_map/ppermute | solution.py:272
  32.9 7.9 %collective-permute-start.7 = (bf16[80,1024]{1,0:T(8,128)(2,1)S(1)}, bf16[80,1024]{1,0:T(8,128)(2,1)S(1)}, u32[]{:S(2)}, u32[]{:S(2)}) collective-permute-start(bf16[80,1024]{1,0:T(8,128)(2,1)S(1)} %get-tuple-element.81), channel_id=1, source_target_pairs={{0,1},{1,2},{2,3},{3,4},{4,5},{5,6},{6,7},{7,8},{8,9},{9,10},{10,1... | collective-permute-start | bytes 491528 | tf_op jit(solution)/shard_map/ppermute | solution.py:272
  35.8 8.0 %collective-permute-start.8 = (bf16[64,1024]{1,0:T(8,128)(2,1)S(1)}, bf16[64,1024]{1,0:T(8,128)(2,1)S(1)}, u32[]{:S(2)}, u32[]{:S(2)}) collective-permute-start(bf16[64,1024]{1,0:T(8,128)(2,1)S(1)} %get-tuple-element.85), channel_id=1, source_target_pairs={{0,1},{1,2},{2,3},{3,4},{4,5},{5,6},{6,7},{7,8},{8,9},{9,10},{10,1... | collective-permute-start | bytes 393224 | tf_op jit(solution)/shard_map/ppermute | solution.py:272
  40.8 7.1 %collective-permute-start.6 = (bf16[64,1024]{1,0:T(8,128)(2,1)S(1)}, bf16[64,1024]{1,0:T(8,128)(2,1)S(1)}, u32[]{:S(2)}, u32[]{:S(2)}) collective-permute-start(bf16[64,1024]{1,0:T(8,128)(2,1)S(1)} %get-tuple-element.80), channel_id=1, source_target_pairs={{0,1},{1,2},{2,3},{3,4},{4,5},{5,6},{6,7},{7,8},{8,9},{9,10},{10,1... | collective-permute-start | bytes 393224 | tf_op jit(solution)/shard_map/ppermute | solution.py:272

commit v4 on v3

--- a/solution.py
+++ b/solution.py
@@ -13,7 +13,7 @@
 HD = 128
 TICKS = 4
 MAX_LEN = 96
-CHUNKS = 3
+CHUNKS = 2
 EXTRA = 16
 LIFT = 16.0
 HIDDEN = -1e30
@@ -157,16 +157,16 @@
         return copies
 
     model, half = wk_ref.shape[0], Q_WIDTH // 2
-    everything = slice(0, model)
+    narrow, wide = slice(0, KV_WIDTH), slice(0, Q_WIDTH)
     batches = [
-        batch(wk_hbm, wk_ref, everything, slice(0, KV_WIDTH)),
-        batch(wv_hbm, wv_ref, everything, slice(0, KV_WIDTH)),
-        batch(wq_hbm, wq_ref, everything, slice(0, half)),
-        batch(wq_hbm, wq_ref, everything, slice(half, Q_WIDTH)),
-        batch(wo_hbm, wo_ref, slice(0, Q_WIDTH), slice(0, model // 2)),
-        batch(wo_hbm, wo_ref, slice(0, Q_WIDTH), slice(model // 2, model)),
+        batch(wk_hbm, wk_ref, slice(0, model), narrow),
+        batch(wv_hbm, wv_ref, slice(0, model), narrow),
+        batch(wq_hbm, wq_ref, slice(0, model // 2), wide),
+        batch(wq_hbm, wq_ref, slice(model // 2, model), wide),
+        batch(wo_hbm, wo_ref, slice(0, half), slice(0, model)),
+        batch(wo_hbm, wo_ref, slice(half, Q_WIDTH), slice(0, model)),
     ]
-    arrivals = {("k", 0): 0, ("v", 0): 1, ("q", 0): 2, ("q", half): 3, ("o", 0): 4, ("o", model // 2): 5}
+    arrivals = {("k", 0): (0,), ("v", 0): (1,), ("q", 0): (2, 3), ("o", 0): (4, 5)}
 
     def begin(index):
         if index < len(batches):
@@ -177,16 +177,15 @@
                 copy.start()
 
     def wait(name, start):
-        index = arrivals.get((name, start))
-        if index is not None:
+        for index in arrivals.get((name, start), ()):
             for copy in batches[index]:
                 copy.wait()
-            begin(index + 2)
+            begin(index + 3)
 
     for copy in small:
         copy.start()
-    begin(0)
-    begin(1)
+    for index in range(3):
+        begin(index)
     for copy in small:
         copy.wait()
     gain_ref[...] = raw_gain[...].astype(F32) * LIFT

time: 51.8 us -> 45.7 us (0.88)
  Pallas kernels: 41.6 us -> 29.7 us
  waiting for transfers between devices: 1.25 us -> 12.4 us
  starting transfers between devices: 8.52 us -> 3.26 us
    pallas_call x11 -> x7, Pallas kernels: 33.8 us -> 22.5 us  [body(): pl.pallas_call(functools.partial(chunk_kernel, index, last), out_shape=tu...]
    ppermute x9 -> x6, waiting for transfers between devices: 1.25 us -> 12.4 us  [passed_along(): lax.ppermute(array, 'section', [(i, (i + by) % length) for i in range(len...]
    ppermute x9 -> x6, starting transfers between devices: 8.52 us -> 3.26 us  [passed_along(): lax.ppermute(array, 'section', [(i, (i + by) % length) for i in range(len...]
    pallas_call x1, Pallas kernels: 7.82 us -> 7.15 us  [body(): pl.pallas_call(functools.partial(opening_kernel, size), out_shape=(kept((...]
  transfers between devices with their start and end apart: 9 -> 6, of which waited for: 1 -> 6; matrix products, arithmetic and copies ran while one was open for 0% -> 0% of each run, Pallas kernels for 59% -> 42%
where the time goes in v4:
time: 45.7 us; the launch traced here: 45.6 us
  Pallas kernels  29.7 us (65%)
  waiting for transfers between devices  12.4 us (27%)
  starting transfers between devices  3.26 us (7%)
    pallas_call x7, Pallas kernels, body(): pl.pallas_call(functools.partial(chunk_kernel, index, last), out_shape=tu...  22.5 us
    ppermute x6, waiting for transfers between devices, passed_along(): lax.ppermute(array, 'section', [(i, (i + by) % length) for i in range(len...  12.4 us
    pallas_call x1, Pallas kernels, body(): pl.pallas_call(functools.partial(opening_kernel, size), out_shape=(kept((...  7.15 us
    ppermute x6, starting transfers between devices, passed_along(): lax.ppermute(array, 'section', [(i, (i + by) % length) for i in range(len...  3.26 us
  transfers between devices with their start and end apart: 6, of which 6 were waited for; matrix products, arithmetic and copies ran while one was open for 0% of the time, Pallas kernels for 42%

profile of v4, /device:TPU:0, one launch (start us, length us, event | category | flops | bytes accessed | tf_op | source)
XLA Modules:
  0.0 45.6 jit_solution(9136253404317371772)
XLA Ops:
  0.0 7.1 %opening.1 = (bf16[112,1024]{1,0:T(8,128)(2,1)S(1)}, bf16[96,1024]{1,0:T(8,128)(2,1)S(1)}, bf16[96,1024]{1,0:T(8,128)(2,1)S(1)}, f32[192,256]{1,0:T(8,128)S(1)},...) custom-call(bf16[1,192,1024]{2,1,0:T(8,128)(2,1)} %x_hbm.1, ...), custom_call_target="tpu_custom_call" | custom-call | tf_op jit(solution)/shard_map/opening/pallas_call | solution.py:284
  7.2 0.5 %collective-permute-start.1 = (bf16[112,1024]{1,0:T(8,128)(2,1)S(1)}, bf16[112,1024]{1,0:T(8,128)(2,1)S(1)}, u32[]{:S(2)}, u32[]{:S(2)}) collective-permute-start(bf16[112,1024]{1,0:T(8,128)(2,1)S(1)} %get-tuple-element.46), channel_id=1, source_target_pairs={{0,1},{1,2},{2,3},{3,4},{4,5},{5,6},{6,7},{7,8},{8,9},{9,10},{10,1... | collective-permute-start | bytes 688136 | tf_op jit(solution)/shard_map/ppermute | solution.py:271
  7.7 3.4 %chunk_0_1.1 = (bf16[96,1024]{1,0:T(8,128)(2,1)S(1)}, bf16[96,1024]{1,0:T(8,128)(2,1)}, bf16[96,1024]{1,0:T(8,128)(2,1)}) custom-call(bf16[96,1024]{1,0:T(8,128)(2,1)S(1)} %get-tuple-element.35.x_ref, f32[1,1024]{1,0:T(1,128)S(1)} %get-tuple-element.36.gain_ref, bf16[1024,2048]{1,0:T(8,128)(2,1)S(1)} %get-tuple-element.37.wq_ref, ...), custom_call_target="tpu_custom_call" | custom-call | tf_op jit(solution)/shard_map/chunk_0_1/pallas_call | solution.py:344
  11.1 2.6 %collective-permute-start = (bf16[96,1024]{1,0:T(8,128)(2,1)S(1)}, bf16[96,1024]{1,0:T(8,128)(2,1)S(1)}, u32[]{:S(2)}, u32[]{:S(2)}) collective-permute-start(bf16[96,1024]{1,0:T(8,128)(2,1)S(1)} %get-tuple-element.45), channel_id=1, source_target_pairs={{0,1},{1,2},{2,3},{3,4},{4,5},{5,6},{6,7},{7,8},{8,9},{9,10},{10,1... | collective-permute-start | bytes 589832 | tf_op jit(solution)/shard_map/ppermute | solution.py:271
  13.7 2.7 %collective-permute-done.1.x_ref = bf16[112,1024]{1,0:T(8,128)(2,1)S(1)} collective-permute-done((bf16[112,1024]{1,0:T(8,128)(2,1)S(1)}, bf16[112,1024]{1,0:T(8,128)(2,1)S(1)}, u32[]{:S(2)}, u32[]{:S(2)}) %collective-permute-start.1) | collective-permute-done | bytes 229408 | tf_op jit(solution)/shard_map/ppermute | solution.py:271
  16.4 2.9 %chunk_1_0.1 = (bf16[112,1024]{1,0:T(8,128)(2,1)S(1)}, bf16[96,1024]{1,0:T(8,128)(2,1)S(1)}, bf16[96,1024]{1,0:T(8,128)(2,1)S(1)}, f32[192,256]{1,0:T(8,128)S(1)}, f32[192,192]{1,0:T(8,128)S(1)}) custom-call(bf16[112,1024]{1,0:T(8,128)(2,1)S(1)} %collective-permute-done.1.x_ref, f32[1,1024]{1,0:T(1,128)S(1)} %get-tuple-element.36.gain_ref, ...), custom_call_target="tpu_custom_call" | custom-call | tf_op jit(solution)/shard_map/chunk_1_0/pallas_call | solution.py:344
  19.3 0.1 collective-permute-start.3
  19.3 0.1 collective-permute-done.x_ref
  19.4 3.4 %chunk_1_1.1 = (bf16[96,1024]{1,0:T(8,128)(2,1)S(1)}, bf16[96,1024]{1,0:T(8,128)(2,1)}, bf16[96,1024]{1,0:T(8,128)(2,1)}) custom-call(bf16[96,1024]{1,0:T(8,128)(2,1)S(1)} %collective-permute-done.x_ref, f32[1,1024]{1,0:T(1,128)S(1)} %get-tuple-element.36.gain_ref, bf16[1024,2048]{1,0:T(8,128)(2,1)S(1)} %get-tuple-element.37.wq_ref, ...), custom_call_target="tpu_custom_call" | custom-call | tf_op jit(solution)/shard_map/chunk_1_1/pallas_call | solution.py:344
  22.8 0.0 collective-permute-start.2
  22.8 4.6 %collective-permute-done.3.x_ref = bf16[112,1024]{1,0:T(8,128)(2,1)S(1)} collective-permute-done((bf16[112,1024]{1,0:T(8,128)(2,1)S(1)}, bf16[112,1024]{1,0:T(8,128)(2,1)S(1)}, u32[]{:S(2)}, u32[]{:S(2)}) %collective-permute-start.3) | collective-permute-done | bytes 229408 | tf_op jit(solution)/shard_map/ppermute | solution.py:271
  27.5 2.9 %chunk_2_0.1 = (bf16[112,1024]{1,0:T(8,128)(2,1)S(1)}, bf16[96,1024]{1,0:T(8,128)(2,1)S(1)}, bf16[96,1024]{1,0:T(8,128)(2,1)S(1)}, f32[192,256]{1,0:T(8,128)S(1)}, f32[192,192]{1,0:T(8,128)S(1)}) custom-call(bf16[112,1024]{1,0:T(8,128)(2,1)S(1)} %collective-permute-done.3.x_ref, f32[1,1024]{1,0:T(1,128)S(1)} %get-tuple-element.36.gain_ref, ...), custom_call_target="tpu_custom_call" | custom-call | tf_op jit(solution)/shard_map/chunk_2_0/pallas_call | solution.py:344
  30.4 0.1 collective-permute-start.5
  30.5 0.2 collective-permute-done.2.x_ref
  30.6 3.4 %chunk_2_1.1 = (bf16[96,1024]{1,0:T(8,128)(2,1)S(1)}, bf16[96,1024]{1,0:T(8,128)(2,1)}, bf16[96,1024]{1,0:T(8,128)(2,1)}) custom-call(bf16[96,1024]{1,0:T(8,128)(2,1)S(1)} %collective-permute-done.2.x_ref, f32[1,1024]{1,0:T(1,128)S(1)} %get-tuple-element.36.gain_ref, bf16[1024,2048]{1,0:T(8,128)(2,1)S(1)} %get-tuple-element.37.wq_ref, ...), custom_call_target="tpu_custom_call" | custom-call | tf_op jit(solution)/shard_map/chunk_2_1/pallas_call | solution.py:344
  34.0 0.0 collective-permute-start.4
  34.0 4.5 %collective-permute-done.5.x_ref = bf16[112,1024]{1,0:T(8,128)(2,1)S(1)} collective-permute-done((bf16[112,1024]{1,0:T(8,128)(2,1)S(1)}, bf16[112,1024]{1,0:T(8,128)(2,1)S(1)}, u32[]{:S(2)}, u32[]{:S(2)}) %collective-permute-start.5) | collective-permute-done | bytes 229408 | tf_op jit(solution)/shard_map/ppermute | solution.py:271
  38.6 2.9 %chunk_3_0.1 = (bf16[112,1024]{1,0:T(8,128)(2,1)S(1)}, bf16[96,1024]{1,0:T(8,128)(2,1)S(1)}, bf16[96,1024]{1,0:T(8,128)(2,1)S(1)}, f32[192,256]{1,0:T(8,128)S(1)}, f32[192,192]{1,0:T(8,128)S(1)}) custom-call(bf16[112,1024]{1,0:T(8,128)(2,1)S(1)} %collective-permute-done.5.x_ref, f32[1,1024]{1,0:T(1,128)S(1)} %get-tuple-element.36.gain_ref, ...), custom_call_target="tpu_custom_call" | custom-call | tf_op jit(solution)/shard_map/chunk_3_0/pallas_call | solution.py:344
  41.5 0.3 collective-permute-done.4.x_ref
  41.8 3.6 %chunk_3_1.1 = bf16[1,192,1024]{2,1,0:T(8,128)(2,1)} custom-call(bf16[96,1024]{1,0:T(8,128)(2,1)S(1)} %collective-permute-done.4.x_ref, f32[1,1024]{1,0:T(1,128)S(1)} %get-tuple-element.36.gain_ref, bf16[1024,2048]{1,0:T(8,128)(2,1)S(1)} %get-tuple-element.37.wq_ref, bf16[1024,1024]{1,0:T(8,128)(2,1)S(1)} %get-tuple-element.38.wk_ref, ...), custom_call_target="tpu_custom_call" | custom-call | tf_op jit(solution)/shard_map/chunk_3_1/pallas_call | solution.py:344
Async XLA Ops:
  7.2 9.2 %collective-permute-start.1 = (bf16[112,1024]{1,0:T(8,128)(2,1)S(1)}, bf16[112,1024]{1,0:T(8,128)(2,1)S(1)}, u32[]{:S(2)}, u32[]{:S(2)}) collective-permute-start(bf16[112,1024]{1,0:T(8,128)(2,1)S(1)} %get-tuple-element.46), channel_id=1, source_target_pairs={{0,1},{1,2},{2,3},{3,4},{4,5},{5,6},{6,7},{7,8},{8,9},{9,10},{10,1... | collective-permute-start | bytes 688136 | tf_op jit(solution)/shard_map/ppermute | solution.py:271
  11.1 8.4 %collective-permute-start = (bf16[96,1024]{1,0:T(8,128)(2,1)S(1)}, bf16[96,1024]{1,0:T(8,128)(2,1)S(1)}, u32[]{:S(2)}, u32[]{:S(2)}) collective-permute-start(bf16[96,1024]{1,0:T(8,128)(2,1)S(1)} %get-tuple-element.45), channel_id=1, source_target_pairs={{0,1},{1,2},{2,3},{3,4},{4,5},{5,6},{6,7},{7,8},{8,9},{9,10},{10,1... | collective-permute-start | bytes 589832 | tf_op jit(solution)/shard_map/ppermute | solution.py:271
  19.3 8.2 %collective-permute-start.3 = (bf16[112,1024]{1,0:T(8,128)(2,1)S(1)}, bf16[112,1024]{1,0:T(8,128)(2,1)S(1)}, u32[]{:S(2)}, u32[]{:S(2)}) collective-permute-start(bf16[112,1024]{1,0:T(8,128)(2,1)S(1)} %get-tuple-element.53), channel_id=1, source_target_pairs={{0,1},{1,2},{2,3},{3,4},{4,5},{5,6},{6,7},{7,8},{8,9},{9,10},{10,1... | collective-permute-start | bytes 688136 | tf_op jit(solution)/shard_map/ppermute | solution.py:271
  22.8 7.8 %collective-permute-start.2 = (bf16[96,1024]{1,0:T(8,128)(2,1)S(1)}, bf16[96,1024]{1,0:T(8,128)(2,1)S(1)}, u32[]{:S(2)}, u32[]{:S(2)}) collective-permute-start(bf16[96,1024]{1,0:T(8,128)(2,1)S(1)} %get-tuple-element.52), channel_id=1, source_target_pairs={{0,1},{1,2},{2,3},{3,4},{4,5},{5,6},{6,7},{7,8},{8,9},{9,10},{10,1... | collective-permute-start | bytes 589832 | tf_op jit(solution)/shard_map/ppermute | solution.py:271
  30.4 8.2 %collective-permute-start.5 = (bf16[112,1024]{1,0:T(8,128)(2,1)S(1)}, bf16[112,1024]{1,0:T(8,128)(2,1)S(1)}, u32[]{:S(2)}, u32[]{:S(2)}) collective-permute-start(bf16[112,1024]{1,0:T(8,128)(2,1)S(1)} %get-tuple-element.59), channel_id=1, source_target_pairs={{0,1},{1,2},{2,3},{3,4},{4,5},{5,6},{6,7},{7,8},{8,9},{9,10},{10,1... | collective-permute-start | bytes 688136 | tf_op jit(solution)/shard_map/ppermute | solution.py:271
  34.0 7.8 %collective-permute-start.4 = (bf16[96,1024]{1,0:T(8,128)(2,1)S(1)}, bf16[96,1024]{1,0:T(8,128)(2,1)S(1)}, u32[]{:S(2)}, u32[]{:S(2)}) collective-permute-start(bf16[96,1024]{1,0:T(8,128)(2,1)S(1)} %get-tuple-element.58), channel_id=1, source_target_pairs={{0,1},{1,2},{2,3},{3,4},{4,5},{5,6},{6,7},{7,8},{8,9},{9,10},{10,1... | collective-permute-start | bytes 589832 | tf_op jit(solution)/shard_map/ppermute | solution.py:271

commit v5 on v4

--- a/solution.py
+++ b/solution.py
@@ -35,27 +35,42 @@
     return np.concatenate([high, low], axis=0)
 
 
+def blocks_of(low, size):
+    if low == 0 and size <= MAX_LEN:
+        return [(0, size, 0, size)]
+    step = HD - MAX_LEN
+    return [(top, step, max(0, low + top - MAX_LEN), low + top + step) for top in range(0, size, step)]
+
+
 def tables_of(ids_row, table):
     length = ids_row.shape[1]
-    across = jnp.broadcast_to(ids_row, (length, length))
-    down = across.T
-    row_index = lax.broadcasted_iota(jnp.int32, (length, length), 0)
-    column = lax.broadcasted_iota(jnp.int32, (length, length), 1)
-    matched = across == down
-    places = jnp.sum(jnp.where(matched & (column < row_index), 1.0, 0.0), axis=1, keepdims=True)
-    bias = jnp.where(matched & (column <= row_index), 0.0, HIDDEN)
+    size = length // CHUNKS
+    down = jnp.broadcast_to(ids_row, (HD, length)).T
+    places, biases = [], []
+    for low in range(0, length, size):
+        for top, height, first, _ in blocks_of(low, size):
+            rows = slice(low + top, low + top + height)
+            row_index = lax.broadcasted_iota(jnp.int32, (height, HD), 0) + rows.start
+            column = lax.broadcasted_iota(jnp.int32, (height, HD), 1) + first
+            matched = jnp.broadcast_to(ids_row[:, first : first + HD], (height, HD)) == down[rows]
+            earlier = jnp.where(matched & (column < row_index), 1.0, 0.0)
+            places.append(jnp.sum(earlier, axis=1, keepdims=True))
+            biases.append(jnp.where(matched & (column <= row_index), 0.0, HIDDEN))
     slots = lax.broadcasted_iota(jnp.int32, (length, 2 * MAX_LEN), 1)
     slots = jnp.where(slots >= MAX_LEN, slots - MAX_LEN, slots).astype(F32)
-    one_hot = jnp.where(slots == places, 1.0, 0.0).astype(BF16)
+    one_hot = jnp.where(slots == jnp.concatenate(places, axis=0), 1.0, 0.0).astype(BF16)
     factors = jnp.dot(one_hot, table, preferred_element_type=F32)
-    return factors, bias
+    return factors, jnp.concatenate(biases, axis=0)
 
 
 def rotated(values, cosine, sine):
     return values * cosine + pltpu.roll(values, HD // 2, 1) * sine
 
 
-def layer(x, gain, weights, wait, cos_rows, bias_rows, kept_keys, kept_values, k_ref, v_ref, mixed_ref, write):
+def layer(
+    x, gain, weights, wait, low, cos_rows, bias_ref, kept_keys, kept_values, k_ref, v_ref, mixed_ref, write,
+    split_out=False,
+):
     size, model = x.shape
     wq_ref, wk_ref, wv_ref, wo_ref = weights
     scale = lax.rsqrt(jnp.mean(x * x, axis=1, keepdims=True) + 1e-05) * (1.0 / LIFT)
@@ -67,60 +82,79 @@
     sine_q = sine * factor
 
     for start in range(0, KV_WIDTH, PAIR):
+        wait("v", start)
+        got = jnp.dot(lifted, wv_ref[:, start : start + PAIR], preferred_element_type=F32)
+        v_ref[:, start : start + PAIR] = (got * scale).astype(BF16)
+    for start in range(0, KV_WIDTH, PAIR):
         wait("k", start)
         got = jnp.dot(lifted, wk_ref[:, start : start + PAIR], preferred_element_type=F32)
         for half in range(0, PAIR, HD):
             turned = rotated(got[:, half : half + HD], cosine, sine)
             k_ref[:, start + half : start + half + HD] = turned.astype(BF16)
-    for start in range(0, KV_WIDTH, PAIR):
-        wait("v", start)
-        got = jnp.dot(lifted, wv_ref[:, start : start + PAIR], preferred_element_type=F32)
-        v_ref[:, start : start + PAIR] = (got * scale).astype(BF16)
     queries = []
     for start in range(0, Q_WIDTH, PAIR):
         wait("q", start)
         got = jnp.dot(lifted, wq_ref[:, start : start + PAIR], preferred_element_type=F32)
         upper = rotated(got[:, :HD], cosine_q, sine_q)
         lower = rotated(got[:, HD:], cosine_q, sine_q)
-        queries.append(jnp.concatenate([upper, lower], axis=0).astype(BF16))
-
-    count = bias_rows.shape[1]
-    ones = jnp.ones((count, HD), BF16)
+        queries.append((upper.astype(BF16), lower.astype(BF16)))
+
+    blocks = blocks_of(low, size)
     groups = range(KV_HEADS)
+    spots = [(group, block) for group in groups for block in blocks]
+
+    def seen(kept_parts, own_ref, lanes, first, last):
+        parts = []
+        for place, ref in enumerate([*kept_parts, own_ref]):
+            start, stop = max(first, place * size), min(last, (place + 1) * size)
+            if start < stop:
+                parts.append(ref[start - place * size : stop - place * size, lanes])
+        return parts[0] if len(parts) == 1 else jnp.concatenate(parts, axis=0)
+
     scores = []
-    for group in groups:
+    for group, (top, height, first, last) in spots:
         lanes = slice(group * HD, (group + 1) * HD)
-        key_rows = jnp.concatenate([rows[:, lanes] for rows in kept_keys] + [k_ref[:, lanes]], axis=0)
-        got = lax.dot_general(queries[group], key_rows, (((1,), (1,)), ((), ())), preferred_element_type=F32)
-        scores.append(got.reshape(2, size, count) + bias_rows[None])
+        upper, lower = queries[group]
+        both = jnp.concatenate([upper[top : top + height], lower[top : top + height]], axis=0)
+        key_rows = seen(kept_keys, k_ref, lanes, first, last)
+        got = lax.dot_general(both, key_rows, (((1,), (1,)), ((), ())), preferred_element_type=F32)
+        bias = bias_ref[low + top : low + top + height, : last - first]
+        scores.append(got.reshape(2, height, last - first) + bias[None])
     most = [jnp.max(part, axis=2, keepdims=True) for part in scores]
-    expo = [jnp.exp2(scores[g] - most[g]).astype(BF16).reshape(2 * size, count) for g in groups]
+    expo = [
+        jnp.exp2((part - peak).astype(BF16)).reshape(2 * part.shape[1], part.shape[2])
+        for part, peak in zip(scores, most)
+    ]
     got = []
-    for group in groups:
+    for (group, (top, height, first, last)), part in zip(spots, expo):
         lanes = slice(group * HD, (group + 1) * HD)
-        value_rows = jnp.concatenate([rows[:, lanes] for rows in kept_values] + [v_ref[:, lanes]], axis=0)
-        value_rows = jnp.concatenate([value_rows, ones], axis=1)
-        got.append(jnp.dot(expo[group], value_rows, preferred_element_type=F32))
-    for group in groups:
-        total = got[group][:, HD:]
+        value_rows = seen(kept_values, v_ref, lanes, first, last)
+        value_rows = jnp.concatenate([value_rows, jnp.ones((last - first, HD), BF16)], axis=1)
+        got.append(jnp.dot(part, value_rows, preferred_element_type=F32))
+    for (group, (top, height, first, last)), part in zip(spots, got):
+        total = part[:, HD:]
         inverse = pl.reciprocal(total, approx=True)
         inverse = inverse * (2.0 - total * inverse)
-        mixed = (got[group][:, :HD] * inverse).astype(BF16)
-        mixed_ref[:, group * PAIR : group * PAIR + HD] = mixed[:size]
-        mixed_ref[:, group * PAIR + HD : (group + 1) * PAIR] = mixed[size:]
+        mixed = (part[:, :HD] * inverse).astype(BF16)
+        mixed_ref[top : top + height, group * PAIR : group * PAIR + HD] = mixed[:height]
+        mixed_ref[top : top + height, group * PAIR + HD : (group + 1) * PAIR] = mixed[height:]
+    half = Q_WIDTH // 2
+    if split_out:
+        wait("o", 0)
+        updates = [
+            jnp.dot(mixed_ref[:, :half], wo_ref[:half, start : start + PAIR], preferred_element_type=F32)
+            for start in range(0, model, PAIR)
+        ]
+        wait("o", half)
+        for start, update in zip(range(0, model, PAIR), updates):
+            update = update + jnp.dot(
+                mixed_ref[:, half:], wo_ref[half:, start : start + PAIR], preferred_element_type=F32
+            )
+            write(start, x[:, start : start + PAIR] + update)
+        return
     for start in range(0, model, PAIR):
-        wait("o", start)
         update = jnp.dot(mixed_ref[...], wo_ref[:, start : start + PAIR], preferred_element_type=F32)
         write(start, x[:, start : start + PAIR] + update)
-
-
-def first_key(low):
-    return max(0, low - MAX_LEN + 1) // 16 * 16
-
-
-def kept_rows(index, size, refs):
-    least = first_key(index * size)
-    return [ref[max(0, least - place * size) :] for place, ref in enumerate(refs) if (place + 1) * size > least]
 
 
 def write_ids(ids_row, out_ref, size):
@@ -159,14 +193,14 @@
     model, half = wk_ref.shape[0], Q_WIDTH // 2
     narrow, wide = slice(0, KV_WIDTH), slice(0, Q_WIDTH)
     batches = [
+        batch(wv_hbm, wv_ref, slice(0, model), narrow),
         batch(wk_hbm, wk_ref, slice(0, model), narrow),
-        batch(wv_hbm, wv_ref, slice(0, model), narrow),
         batch(wq_hbm, wq_ref, slice(0, model // 2), wide),
         batch(wq_hbm, wq_ref, slice(model // 2, model), wide),
         batch(wo_hbm, wo_ref, slice(0, half), slice(0, model)),
         batch(wo_hbm, wo_ref, slice(half, Q_WIDTH), slice(0, model)),
     ]
-    arrivals = {("k", 0): (0,), ("v", 0): (1,), ("q", 0): (2, 3), ("o", 0): (4, 5)}
+    arrivals = {("v", 0): (0,), ("k", 0): (1,), ("q", 0): (2, 3), ("o", 0): (4,), ("o", half): (5,)}
 
     def begin(index):
         if index < len(batches):
@@ -180,11 +214,11 @@
         for index in arrivals.get((name, start), ()):
             for copy in batches[index]:
                 copy.wait()
-            begin(index + 3)
+            begin(index + 4)
 
     for copy in small:
         copy.start()
-    for index in range(3):
+    for index in range(4):
         begin(index)
     for copy in small:
         copy.wait()
@@ -201,7 +235,7 @@
 
     layer(
         x_ref[...].astype(F32), gain_ref[...], (wq_ref, wk_ref, wv_ref, wo_ref), wait,
-        cos_ref[:size, :], bias_ref[:size, :size], [], [], k_ref, v_ref, mixed_ref, write,
+        0, cos_ref[:size, :], bias_ref, [], [], k_ref, v_ref, mixed_ref, write, split_out=True,
     )
     for copy in late:
         copy.wait()
@@ -240,8 +274,7 @@
 
     layer(
         x_ref[:size, :].astype(F32), gain_ref[...], (wq_ref, wk_ref, wv_ref, wo_ref), lambda name, start: None,
-        cos_ref[low:high, :], bias_ref[low:high, first_key(low) : high],
-        kept_rows(index, size, keys), kept_rows(index, size, values), k_ref, v_ref, mixed_ref, write,
+        low, cos_ref[low:high, :], bias_ref, keys, values, k_ref, v_ref, mixed_ref, write,
     )
     if last and index == CHUNKS - 1:
         copy = pltpu.make_async_copy(out_ref, whole_ref.at[0, low:high], sems.at[index])
@@ -278,7 +311,7 @@
     table = jnp.asarray(rope_table())
     rows = [size + EXTRA] + [size] * (CHUNKS - 1)
     key_values = [kept((size, KV_WIDTH), BF16)] * 2
-    tables = [kept((length, PAIR), F32), kept((length, length), F32)]
+    tables = [kept((length, PAIR), F32), kept((length, HD), F32)]
     mixing = pltpu.VMEM((size, Q_WIDTH), BF16)
 
     got = pl.pallas_call(

time: 45.7 us -> 46.9 us (1.026)
  Pallas kernels: 29.7 us -> 31.5 us
  waiting for transfers between devices: 12.4 us -> 11.7 us
    pallas_call x7, Pallas kernels: 22.5 us -> 23.8 us  [body(): pl.pallas_call(functools.partial(chunk_kernel, index, last), out_shape=tu...]
    ppermute x6, waiting for transfers between devices: 12.4 us -> 11.7 us  [passed_along(): lax.ppermute(array, 'section', [(i, (i + by) % length) for i in range(len...]
    pallas_call x1, Pallas kernels: 7.15 us -> 7.69 us  [body(): pl.pallas_call(functools.partial(opening_kernel, size), out_shape=(kept((...]
  transfers between devices with their start and end apart: 6 -> 6, of which waited for: 6 -> 3; matrix products, arithmetic and copies ran while one was open for 0% -> 0% of each run, Pallas kernels for 42% -> 43%
where the time goes in v5:
time: 46.9 us; the launch traced here: 46.7 us
  Pallas kernels  31.5 us (67%)
  waiting for transfers between devices  11.7 us (25%)
  starting transfers between devices  3.25 us (7%)
    pallas_call x7, Pallas kernels, body(): pl.pallas_call(functools.partial(chunk_kernel, index, last), out_shape=tu...  23.8 us
    ppermute x6, waiting for transfers between devices, passed_along(): lax.ppermute(array, 'section', [(i, (i + by) % length) for i in range(len...  11.7 us
    pallas_call x1, Pallas kernels, body(): pl.pallas_call(functools.partial(opening_kernel, size), out_shape=(kept((...  7.69 us
    ppermute x6, starting transfers between devices, passed_along(): lax.ppermute(array, 'section', [(i, (i + by) % length) for i in range(len...  3.25 us
  transfers between devices with their start and end apart: 6, of which 3 were waited for; matrix products, arithmetic and copies ran while one was open for 0% of the time, Pallas kernels for 43%

profile of v5, /device:TPU:0, one launch (start us, length us, event | category | flops | bytes accessed | tf_op | source)
XLA Modules:
  0.0 46.7 jit_solution(17660395817467944096)
XLA Ops:
  0.0 7.7 %opening.1 = (bf16[112,1024]{1,0:T(8,128)(2,1)S(1)}, bf16[96,1024]{1,0:T(8,128)(2,1)S(1)}, bf16[96,1024]{1,0:T(8,128)(2,1)S(1)}, f32[192,256]{1,0:T(8,128)S(1)},...) custom-call(bf16[1,192,1024]{2,1,0:T(8,128)(2,1)} %x_hbm.1, ...), custom_call_target="tpu_custom_call" | custom-call | tf_op jit(solution)/shard_map/opening/pallas_call | solution.py:317
  7.7 0.5 %collective-permute-start.1 = (bf16[112,1024]{1,0:T(8,128)(2,1)S(1)}, bf16[112,1024]{1,0:T(8,128)(2,1)S(1)}, u32[]{:S(2)}, u32[]{:S(2)}) collective-permute-start(bf16[112,1024]{1,0:T(8,128)(2,1)S(1)} %get-tuple-element.46), channel_id=1, source_target_pairs={{0,1},{1,2},{2,3},{3,4},{4,5},{5,6},{6,7},{7,8},{8,9},{9,10},{10,1... | collective-permute-start | bytes 688136 | tf_op jit(solution)/shard_map/ppermute | solution.py:304
  8.2 3.5 %chunk_0_1.1 = (bf16[96,1024]{1,0:T(8,128)(2,1)S(1)}, bf16[96,1024]{1,0:T(8,128)(2,1)}, bf16[96,1024]{1,0:T(8,128)(2,1)}) custom-call(bf16[96,1024]{1,0:T(8,128)(2,1)S(1)} %get-tuple-element.35.x_ref, f32[1,1024]{1,0:T(1,128)S(1)} %get-tuple-element.36.gain_ref, bf16[1024,2048]{1,0:T(8,128)(2,1)S(1)} %get-tuple-element.37.wq_ref, ...), custom_call_target="tpu_custom_call" | custom-call | tf_op jit(solution)/shard_map/chunk_0_1/pallas_call | solution.py:377
  11.8 2.6 %collective-permute-start = (bf16[96,1024]{1,0:T(8,128)(2,1)S(1)}, bf16[96,1024]{1,0:T(8,128)(2,1)S(1)}, u32[]{:S(2)}, u32[]{:S(2)}) collective-permute-start(bf16[96,1024]{1,0:T(8,128)(2,1)S(1)} %get-tuple-element.45), channel_id=1, source_target_pairs={{0,1},{1,2},{2,3},{3,4},{4,5},{5,6},{6,7},{7,8},{8,9},{9,10},{10,1... | collective-permute-start | bytes 589832 | tf_op jit(solution)/shard_map/ppermute | solution.py:304
  14.4 2.5 %collective-permute-done.1.x_ref = bf16[112,1024]{1,0:T(8,128)(2,1)S(1)} collective-permute-done((bf16[112,1024]{1,0:T(8,128)(2,1)S(1)}, bf16[112,1024]{1,0:T(8,128)(2,1)S(1)}, u32[]{:S(2)}, u32[]{:S(2)}) %collective-permute-start.1) | collective-permute-done | bytes 229408 | tf_op jit(solution)/shard_map/ppermute | solution.py:304
  16.9 3.2 %chunk_1_0.1 = (bf16[112,1024]{1,0:T(8,128)(2,1)S(1)}, bf16[96,1024]{1,0:T(8,128)(2,1)S(1)}, bf16[96,1024]{1,0:T(8,128)(2,1)S(1)}, f32[192,256]{1,0:T(8,128)S(1)}, f32[192,128]{1,0:T(8,128)S(1)}) custom-call(bf16[112,1024]{1,0:T(8,128)(2,1)S(1)} %collective-permute-done.1.x_ref, f32[1,1024]{1,0:T(1,128)S(1)} %get-tuple-element.36.gain_ref, ...), custom_call_target="tpu_custom_call" | custom-call | tf_op jit(solution)/shard_map/chunk_1_0/pallas_call | solution.py:377
  20.1 0.1 collective-permute-start.3
  20.1 0.0 collective-permute-done.x_ref
  20.2 3.5 %chunk_1_1.1 = (bf16[96,1024]{1,0:T(8,128)(2,1)S(1)}, bf16[96,1024]{1,0:T(8,128)(2,1)}, bf16[96,1024]{1,0:T(8,128)(2,1)}) custom-call(bf16[96,1024]{1,0:T(8,128)(2,1)S(1)} %collective-permute-done.x_ref, f32[1,1024]{1,0:T(1,128)S(1)} %get-tuple-element.36.gain_ref, bf16[1024,2048]{1,0:T(8,128)(2,1)S(1)} %get-tuple-element.37.wq_ref, ...), custom_call_target="tpu_custom_call" | custom-call | tf_op jit(solution)/shard_map/chunk_1_1/pallas_call | solution.py:377
  23.7 0.0 collective-permute-start.2
  23.7 4.6 %collective-permute-done.3.x_ref = bf16[112,1024]{1,0:T(8,128)(2,1)S(1)} collective-permute-done((bf16[112,1024]{1,0:T(8,128)(2,1)S(1)}, bf16[112,1024]{1,0:T(8,128)(2,1)S(1)}, u32[]{:S(2)}, u32[]{:S(2)}) %collective-permute-start.3) | collective-permute-done | bytes 229408 | tf_op jit(solution)/shard_map/ppermute | solution.py:304
  28.3 3.2 %chunk_2_0.1 = (bf16[112,1024]{1,0:T(8,128)(2,1)S(1)}, bf16[96,1024]{1,0:T(8,128)(2,1)S(1)}, bf16[96,1024]{1,0:T(8,128)(2,1)S(1)}, f32[192,256]{1,0:T(8,128)S(1)}, f32[192,128]{1,0:T(8,128)S(1)}) custom-call(bf16[112,1024]{1,0:T(8,128)(2,1)S(1)} %collective-permute-done.3.x_ref, f32[1,1024]{1,0:T(1,128)S(1)} %get-tuple-element.36.gain_ref, ...), custom_call_target="tpu_custom_call" | custom-call | tf_op jit(solution)/shard_map/chunk_2_0/pallas_call | solution.py:377
  31.4 0.1 collective-permute-start.5
  31.5 0.0 collective-permute-done.2.x_ref
  31.5 3.5 %chunk_2_1.1 = (bf16[96,1024]{1,0:T(8,128)(2,1)S(1)}, bf16[96,1024]{1,0:T(8,128)(2,1)}, bf16[96,1024]{1,0:T(8,128)(2,1)}) custom-call(bf16[96,1024]{1,0:T(8,128)(2,1)S(1)} %collective-permute-done.2.x_ref, f32[1,1024]{1,0:T(1,128)S(1)} %get-tuple-element.36.gain_ref, bf16[1024,2048]{1,0:T(8,128)(2,1)S(1)} %get-tuple-element.37.wq_ref, ...), custom_call_target="tpu_custom_call" | custom-call | tf_op jit(solution)/shard_map/chunk_2_1/pallas_call | solution.py:377
  35.1 0.0 collective-permute-start.4
  35.1 4.6 %collective-permute-done.5.x_ref = bf16[112,1024]{1,0:T(8,128)(2,1)S(1)} collective-permute-done((bf16[112,1024]{1,0:T(8,128)(2,1)S(1)}, bf16[112,1024]{1,0:T(8,128)(2,1)S(1)}, u32[]{:S(2)}, u32[]{:S(2)}) %collective-permute-start.5) | collective-permute-done | bytes 229408 | tf_op jit(solution)/shard_map/ppermute | solution.py:304
  39.6 3.2 %chunk_3_0.1 = (bf16[112,1024]{1,0:T(8,128)(2,1)S(1)}, bf16[96,1024]{1,0:T(8,128)(2,1)S(1)}, bf16[96,1024]{1,0:T(8,128)(2,1)S(1)}, f32[192,256]{1,0:T(8,128)S(1)}, f32[192,128]{1,0:T(8,128)S(1)}) custom-call(bf16[112,1024]{1,0:T(8,128)(2,1)S(1)} %collective-permute-done.5.x_ref, f32[1,1024]{1,0:T(1,128)S(1)} %get-tuple-element.36.gain_ref, ...), custom_call_target="tpu_custom_call" | custom-call | tf_op jit(solution)/shard_map/chunk_3_0/pallas_call | solution.py:377
  42.8 0.0 collective-permute-done.4.x_ref
  42.8 3.7 %chunk_3_1.1 = bf16[1,192,1024]{2,1,0:T(8,128)(2,1)} custom-call(bf16[96,1024]{1,0:T(8,128)(2,1)S(1)} %collective-permute-done.4.x_ref, f32[1,1024]{1,0:T(1,128)S(1)} %get-tuple-element.36.gain_ref, bf16[1024,2048]{1,0:T(8,128)(2,1)S(1)} %get-tuple-element.37.wq_ref, bf16[1024,1024]{1,0:T(8,128)(2,1)S(1)} %get-tuple-element.38.wk_ref, ...), custom_call_target="tpu_custom_call" | custom-call | tf_op jit(solution)/shard_map/chunk_3_1/pallas_call | solution.py:377
Async XLA Ops:
  7.7 9.2 %collective-permute-start.1 = (bf16[112,1024]{1,0:T(8,128)(2,1)S(1)}, bf16[112,1024]{1,0:T(8,128)(2,1)S(1)}, u32[]{:S(2)}, u32[]{:S(2)}) collective-permute-start(bf16[112,1024]{1,0:T(8,128)(2,1)S(1)} %get-tuple-element.46), channel_id=1, source_target_pairs={{0,1},{1,2},{2,3},{3,4},{4,5},{5,6},{6,7},{7,8},{8,9},{9,10},{10,1... | collective-permute-start | bytes 688136 | tf_op jit(solution)/shard_map/ppermute | solution.py:304
  11.8 8.4 %collective-permute-start = (bf16[96,1024]{1,0:T(8,128)(2,1)S(1)}, bf16[96,1024]{1,0:T(8,128)(2,1)S(1)}, u32[]{:S(2)}, u32[]{:S(2)}) collective-permute-start(bf16[96,1024]{1,0:T(8,128)(2,1)S(1)} %get-tuple-element.45), channel_id=1, source_target_pairs={{0,1},{1,2},{2,3},{3,4},{4,5},{5,6},{6,7},{7,8},{8,9},{9,10},{10,1... | collective-permute-start | bytes 589832 | tf_op jit(solution)/shard_map/ppermute | solution.py:304
  20.1 8.2 %collective-permute-start.3 = (bf16[112,1024]{1,0:T(8,128)(2,1)S(1)}, bf16[112,1024]{1,0:T(8,128)(2,1)S(1)}, u32[]{:S(2)}, u32[]{:S(2)}) collective-permute-start(bf16[112,1024]{1,0:T(8,128)(2,1)S(1)} %get-tuple-element.53), channel_id=1, source_target_pairs={{0,1},{1,2},{2,3},{3,4},{4,5},{5,6},{6,7},{7,8},{8,9},{9,10},{10,1... | collective-permute-start | bytes 688136 | tf_op jit(solution)/shard_map/ppermute | solution.py:304
  23.7 7.8 %collective-permute-start.2 = (bf16[96,1024]{1,0:T(8,128)(2,1)S(1)}, bf16[96,1024]{1,0:T(8,128)(2,1)S(1)}, u32[]{:S(2)}, u32[]{:S(2)}) collective-permute-start(bf16[96,1024]{1,0:T(8,128)(2,1)S(1)} %get-tuple-element.52), channel_id=1, source_target_pairs={{0,1},{1,2},{2,3},{3,4},{4,5},{5,6},{6,7},{7,8},{8,9},{9,10},{10,1... | collective-permute-start | bytes 589832 | tf_op jit(solution)/shard_map/ppermute | solution.py:304
  31.4 8.2 %collective-permute-start.5 = (bf16[112,1024]{1,0:T(8,128)(2,1)S(1)}, bf16[112,1024]{1,0:T(8,128)(2,1)S(1)}, u32[]{:S(2)}, u32[]{:S(2)}) collective-permute-start(bf16[112,1024]{1,0:T(8,128)(2,1)S(1)} %get-tuple-element.59), channel_id=1, source_target_pairs={{0,1},{1,2},{2,3},{3,4},{4,5},{5,6},{6,7},{7,8},{8,9},{9,10},{10,1... | collective-permute-start | bytes 688136 | tf_op jit(solution)/shard_map/ppermute | solution.py:304
  35.1 7.8 %collective-permute-start.4 = (bf16[96,1024]{1,0:T(8,128)(2,1)S(1)}, bf16[96,1024]{1,0:T(8,128)(2,1)S(1)}, u32[]{:S(2)}, u32[]{:S(2)}) collective-permute-start(bf16[96,1024]{1,0:T(8,128)(2,1)S(1)} %get-tuple-element.58), channel_id=1, source_target_pairs={{0,1},{1,2},{2,3},{3,4},{4,5},{5,6},{6,7},{7,8},{8,9},{9,10},{10,1... | collective-permute-start | bytes 589832 | tf_op jit(solution)/shard_map/ppermute | solution.py:304

commit v6 on v4

--- a/solution.py
+++ b/solution.py
@@ -55,8 +55,12 @@
     return values * cosine + pltpu.roll(values, HD // 2, 1) * sine
 
 
-def layer(x, gain, weights, wait, cos_rows, bias_rows, kept_keys, kept_values, k_ref, v_ref, mixed_ref, write):
-    size, model = x.shape
+def layer(
+    looped, x_ref, size, gain, weights, wait, cos_rows, bias_rows, kept_keys, kept_values,
+    k_ref, v_ref, q_ref, mixed_ref, write,
+):
+    model = x_ref.shape[1]
+    x = x_ref[:size, :].astype(F32)
     wq_ref, wk_ref, wv_ref, wo_ref = weights
     scale = lax.rsqrt(jnp.mean(x * x, axis=1, keepdims=True) + 1e-05) * (1.0 / LIFT)
     lifted = (x * gain).astype(BF16)
@@ -66,52 +70,80 @@
     cosine_q = cosine * factor
     sine_q = sine * factor
 
-    for start in range(0, KV_WIDTH, PAIR):
-        wait("k", start)
-        got = jnp.dot(lifted, wk_ref[:, start : start + PAIR], preferred_element_type=F32)
-        for half in range(0, PAIR, HD):
-            turned = rotated(got[:, half : half + HD], cosine, sine)
-            k_ref[:, start + half : start + half + HD] = turned.astype(BF16)
-    for start in range(0, KV_WIDTH, PAIR):
-        wait("v", start)
-        got = jnp.dot(lifted, wv_ref[:, start : start + PAIR], preferred_element_type=F32)
-        v_ref[:, start : start + PAIR] = (got * scale).astype(BF16)
-    queries = []
-    for start in range(0, Q_WIDTH, PAIR):
-        wait("q", start)
-        got = jnp.dot(lifted, wq_ref[:, start : start + PAIR], preferred_element_type=F32)
-        upper = rotated(got[:, :HD], cosine_q, sine_q)
-        lower = rotated(got[:, HD:], cosine_q, sine_q)
-        queries.append(jnp.concatenate([upper, lower], axis=0).astype(BF16))
-
     count = bias_rows.shape[1]
     ones = jnp.ones((count, HD), BF16)
-    groups = range(KV_HEADS)
-    scores = []
-    for group in groups:
-        lanes = slice(group * HD, (group + 1) * HD)
-        key_rows = jnp.concatenate([rows[:, lanes] for rows in kept_keys] + [k_ref[:, lanes]], axis=0)
-        got = lax.dot_general(queries[group], key_rows, (((1,), (1,)), ((), ())), preferred_element_type=F32)
-        scores.append(got.reshape(2, size, count) + bias_rows[None])
-    most = [jnp.max(part, axis=2, keepdims=True) for part in scores]
-    expo = [jnp.exp2(scores[g] - most[g]).astype(BF16).reshape(2 * size, count) for g in groups]
-    got = []
-    for group in groups:
-        lanes = slice(group * HD, (group + 1) * HD)
-        value_rows = jnp.concatenate([rows[:, lanes] for rows in kept_values] + [v_ref[:, lanes]], axis=0)
-        value_rows = jnp.concatenate([value_rows, ones], axis=1)
-        got.append(jnp.dot(expo[group], value_rows, preferred_element_type=F32))
-    for group in groups:
-        total = got[group][:, HD:]
-        inverse = pl.reciprocal(total, approx=True)
-        inverse = inverse * (2.0 - total * inverse)
-        mixed = (got[group][:, :HD] * inverse).astype(BF16)
-        mixed_ref[:, group * PAIR : group * PAIR + HD] = mixed[:size]
-        mixed_ref[:, group * PAIR + HD : (group + 1) * PAIR] = mixed[size:]
-    for start in range(0, model, PAIR):
-        wait("o", start)
-        update = jnp.dot(mixed_ref[...], wo_ref[:, start : start + PAIR], preferred_element_type=F32)
-        write(start, x[:, start : start + PAIR] + update)
+
+    def lanes_of(index, width):
+        if isinstance(index, int):
+            return slice(index * width, (index + 1) * width)
+        return pl.ds(pl.multiple_of(index * width, width), width)
+
+    def loop(steps, unroll, visit):
+        if not looped:
+            for index in range(steps):
+                visit([index])
+            return
+
+        def step(turn, carry):
+            visit([turn * unroll + offset for offset in range(unroll)])
+            return carry
+
+        lax.fori_loop(0, steps // unroll, step, 0)
+
+    def keys_and_values(indices):
+        for index in indices:
+            lanes = lanes_of(index, PAIR)
+            wait("k", index)
+            got = jnp.dot(lifted, wk_ref[:, lanes], preferred_element_type=F32)
+            turned = [rotated(got[:, half : half + HD], cosine, sine) for half in range(0, PAIR, HD)]
+            k_ref[:, lanes] = jnp.concatenate(turned, axis=1).astype(BF16)
+            wait("v", index)
+            got = jnp.dot(lifted, wv_ref[:, lanes], preferred_element_type=F32)
+            v_ref[:, lanes] = (got * scale).astype(BF16)
+
+    def queries(indices):
+        for index in indices:
+            wait("q", index)
+            got = jnp.dot(lifted, wq_ref[:, lanes_of(index, PAIR)], preferred_element_type=F32)
+            q_ref[index, :size] = rotated(got[:, :HD], cosine_q, sine_q).astype(BF16)
+            q_ref[index, size:] = rotated(got[:, HD:], cosine_q, sine_q).astype(BF16)
+
+    def attend(groups):
+        scores = []
+        for group in groups:
+            lanes = lanes_of(group, HD)
+            key_rows = jnp.concatenate([rows[:, lanes] for rows in kept_keys] + [k_ref[:, lanes]], axis=0)
+            got = lax.dot_general(q_ref[group], key_rows, (((1,), (1,)), ((), ())), preferred_element_type=F32)
+            scores.append(got.reshape(2, size, count) + bias_rows[None])
+        most = [jnp.max(part, axis=2, keepdims=True) for part in scores]
+        expo = [jnp.exp2(part - peak).astype(BF16).reshape(2 * size, count) for part, peak in zip(scores, most)]
+        got = []
+        for group, part in zip(groups, expo):
+            lanes = lanes_of(group, HD)
+            value_rows = jnp.concatenate([rows[:, lanes] for rows in kept_values] + [v_ref[:, lanes]], axis=0)
+            value_rows = jnp.concatenate([value_rows, ones], axis=1)
+            got.append(jnp.dot(part, value_rows, preferred_element_type=F32))
+        for group, part in zip(groups, got):
+            total = part[:, HD:]
+            inverse = pl.reciprocal(total, approx=True)
+            inverse = inverse * (2.0 - total * inverse)
+            mixed = (part[:, :HD] * inverse).astype(BF16)
+            mixed_ref[:, lanes_of(group, PAIR)] = jnp.concatenate([mixed[:size], mixed[size:]], axis=1)
+
+    def outputs(indices):
+        for index in indices:
+            wait("o", index)
+            lanes = lanes_of(index, PAIR)
+            update = jnp.dot(mixed_ref[...], wo_ref[:, lanes], preferred_element_type=F32)
+            write(lanes, x_ref[:size, lanes].astype(F32) + update)
+
+    loop(KV_WIDTH // PAIR, 1, keys_and_values)
+    loop(Q_WIDTH // PAIR, 2, queries)
+    if looped:
+        loop(KV_HEADS, 4, attend)
+    else:
+        attend(range(KV_HEADS))
+    loop(model // PAIR, 2, outputs)
 
 
 def first_key(low):
@@ -120,7 +152,7 @@
 
 def kept_rows(index, size, refs):
     least = first_key(index * size)
-    return [ref[max(0, least - place * size) :] for place, ref in enumerate(refs) if (place + 1) * size > least]
+    return [ref.at[max(0, least - place * size) :] for place, ref in enumerate(refs) if (place + 1) * size > least]
 
 
 def write_ids(ids_row, out_ref, size):
@@ -134,7 +166,7 @@
     out_ref, k_ref, v_ref, cos_ref, bias_ref, wq_ref, wk_ref, wv_ref, wo_ref, gain_ref, table_ref, *refs,
 ):
     rest_refs, refs = refs[: CHUNKS - 1], refs[CHUNKS - 1 :]
-    x_ref, ids_ref, raw_gain, raw_table, mixed_ref, small_sems, sems = refs
+    x_ref, ids_ref, raw_gain, raw_table, q_ref, mixed_ref, small_sems, sems = refs
     small = [
         pltpu.make_async_copy(ids_hbm, ids_ref, small_sems.at[0]),
         pltpu.make_async_copy(table_hbm, raw_table, small_sems.at[1]),
@@ -176,8 +208,8 @@
             for copy in late:
                 copy.start()
 
-    def wait(name, start):
-        for index in arrivals.get((name, start), ()):
+    def wait(name, tile):
+        for index in arrivals.get((name, tile), ()):
             for copy in batches[index]:
                 copy.wait()
             begin(index + 3)
@@ -196,12 +228,12 @@
     bias_ref[...] = bias
     write_ids(ids_row, out_ref, size)
 
-    def write(start, values):
-        out_ref[:size, start : start + PAIR] = values.astype(BF16)
+    def write(lanes, values):
+        out_ref[:size, lanes] = values.astype(BF16)
 
     layer(
-        x_ref[...].astype(F32), gain_ref[...], (wq_ref, wk_ref, wv_ref, wo_ref), wait,
-        cos_ref[:size, :], bias_ref[:size, :size], [], [], k_ref, v_ref, mixed_ref, write,
+        False, x_ref, size, gain_ref[...], (wq_ref, wk_ref, wv_ref, wo_ref), wait,
+        cos_ref[:size, :], bias_ref[:size, :size], [], [], k_ref, v_ref, q_ref, mixed_ref, write,
     )
     for copy in late:
         copy.wait()
@@ -210,6 +242,7 @@
 def chunk_kernel(index, last, x_ref, gain_ref, wq_ref, wk_ref, wv_ref, wo_ref, *refs):
     refs = list(refs)
     mixed_ref = refs.pop(-1)
+    q_ref = refs.pop(-1)
     size = mixed_ref.shape[0]
     low, high = index * size, (index + 1) * size
     if index == 0:
@@ -235,13 +268,13 @@
         else:
             out_ref, k_ref, v_ref = refs
 
-    def write(start, result):
-        out_ref[:size, start : start + PAIR] = result.astype(BF16)
+    def write(lanes, result):
+        out_ref[:size, lanes] = result.astype(BF16)
 
     layer(
-        x_ref[:size, :].astype(F32), gain_ref[...], (wq_ref, wk_ref, wv_ref, wo_ref), lambda name, start: None,
+        True, x_ref, size, gain_ref[...], (wq_ref, wk_ref, wv_ref, wo_ref), lambda name, index: None,
         cos_ref[low:high, :], bias_ref[low:high, first_key(low) : high],
-        kept_rows(index, size, keys), kept_rows(index, size, values), k_ref, v_ref, mixed_ref, write,
+        kept_rows(index, size, keys), kept_rows(index, size, values), k_ref, v_ref, q_ref, mixed_ref, write,
     )
     if last and index == CHUNKS - 1:
         copy = pltpu.make_async_copy(out_ref, whole_ref.at[0, low:high], sems.at[index])
@@ -279,7 +312,7 @@
     rows = [size + EXTRA] + [size] * (CHUNKS - 1)
     key_values = [kept((size, KV_WIDTH), BF16)] * 2
     tables = [kept((length, PAIR), F32), kept((length, length), F32)]
-    mixing = pltpu.VMEM((size, Q_WIDTH), BF16)
+    mixing = [pltpu.VMEM((KV_HEADS, 2 * size, HD), BF16), pltpu.VMEM((size, Q_WIDTH), BF16)]
 
     got = pl.pallas_call(
         functools.partial(opening_kernel, size),
@@ -302,7 +335,7 @@
             pltpu.VMEM(segment.shape, jnp.int32),
             pltpu.VMEM(gain.shape, BF16),
             pltpu.VMEM(table.shape, F32),
-            mixing,
+            *mixing,
             pltpu.SemaphoreType.DMA((3 + CHUNKS,)),
             pltpu.SemaphoreType.DMA((24,)),
         ],
@@ -325,7 +358,7 @@
                 continue
             args = [streams[index], *weights]
             shapes = [kept((rows[index], model), BF16), *key_values]
-            scratch = [mixing]
+            scratch = mixing
             if index == 0:
                 args.append(table)
                 shapes += tables
@@ -339,7 +372,7 @@
                 specs = [pl.BlockSpec(memory_space=pl.ANY)]
                 scratch = [
                     pltpu.VMEM((size, model), BF16), *[pltpu.VMEM((size, KV_WIDTH), BF16)] * 2,
-                    pltpu.SemaphoreType.DMA((CHUNKS,)), mixing,
+                    pltpu.SemaphoreType.DMA((CHUNKS,)), *mixing,
                 ]
             got = pl.pallas_call(
                 functools.partial(chunk_kernel, index, last),

time: 45.7 us -> 56 us (1.23)
  Pallas kernels: 29.7 us -> 47.3 us
  waiting for transfers between devices: 12.4 us -> 3.16 us
  starting transfers between devices: 3.26 us -> 5.16 us
    pallas_call x7, Pallas kernels: 22.5 us -> 40.1 us  [body(): pl.pallas_call(functools.partial(chunk_kernel, index, last), out_shape=tu...]
    ppermute x6, waiting for transfers between devices: 12.4 us -> 3.16 us  [passed_along(): lax.ppermute(array, 'section', [(i, (i + by) % length) for i in range(len...]
    ppermute x6, starting transfers between devices: 3.26 us -> 5.16 us  [passed_along(): lax.ppermute(array, 'section', [(i, (i + by) % length) for i in range(len...]
  transfers between devices with their start and end apart: 6 -> 6, of which waited for: 6 -> 3; matrix products, arithmetic and copies ran while one was open for 0% -> 0% of each run, Pallas kernels for 42% -> 61%
where the time goes in v6:
time: 56 us; the launch traced here: 55.8 us
  Pallas kernels  47.3 us (84%)
  starting transfers between devices  5.16 us (9%)
  waiting for transfers between devices  3.16 us (6%)
    pallas_call x7, Pallas kernels, body(): pl.pallas_call(functools.partial(chunk_kernel, index, last), out_shape=tu...  40.1 us
    pallas_call x1, Pallas kernels, body(): pl.pallas_call(functools.partial(opening_kernel, size), out_shape=(kept((...  7.16 us
    ppermute x6, starting transfers between devices, passed_along(): lax.ppermute(array, 'section', [(i, (i + by) % length) for i in range(len...  5.16 us
    ppermute x6, waiting for transfers between devices, passed_along(): lax.ppermute(array, 'section', [(i, (i + by) % length) for i in range(len...  3.16 us
  transfers between devices with their start and end apart: 6, of which 3 were waited for; matrix products, arithmetic and copies ran while one was open for 0% of the time, Pallas kernels for 61%

profile of v6, /device:TPU:0, one launch (start us, length us, event | category | flops | bytes accessed | tf_op | source)
XLA Modules:
  0.0 55.8 jit_solution(10181065313369979001)
XLA Ops:
  0.0 7.2 %opening.1 = (bf16[112,1024]{1,0:T(8,128)(2,1)S(1)}, bf16[96,1024]{1,0:T(8,128)(2,1)S(1)}, bf16[96,1024]{1,0:T(8,128)(2,1)S(1)}, f32[192,256]{1,0:T(8,128)S(1)},...) custom-call(bf16[1,192,1024]{2,1,0:T(8,128)(2,1)} %x_hbm.1, ...), custom_call_target="tpu_custom_call" | custom-call | tf_op jit(solution)/shard_map/opening/pallas_call | solution.py:317
  7.2 0.5 collective-permute-start.1
  7.7 5.7 %chunk_0_1.1 = (bf16[96,1024]{1,0:T(8,128)(2,1)S(1)}, bf16[96,1024]{1,0:T(8,128)(2,1)}, bf16[96,1024]{1,0:T(8,128)(2,1)}) custom-call(bf16[96,1024]{1,0:T(8,128)(2,1)S(1)} %get-tuple-element.35.x_ref, f32[1,1024]{1,0:T(1,128)S(1)} %get-tuple-element.36.gain_ref, bf16[1024,2048]{1,0:T(8,128)(2,1)S(1)} %get-tuple-element.37.wq_ref, ...), custom_call_target="tpu_custom_call" | custom-call | tf_op jit(solution)/shard_map/chunk_0_1/pallas_call | solution.py:377
  13.4 2.6 %collective-permute-start = (bf16[96,1024]{1,0:T(8,128)(2,1)S(1)}, bf16[96,1024]{1,0:T(8,128)(2,1)S(1)}, u32[]{:S(2)}, u32[]{:S(2)}) collective-permute-start(bf16[96,1024]{1,0:T(8,128)(2,1)S(1)} %get-tuple-element.45), channel_id=1, source_target_pairs={{0,1},{1,2},{2,3},{3,4},{4,5},{5,6},{6,7},{7,8},{8,9},{9,10},{10,1... | collective-permute-start | bytes 589832 | tf_op jit(solution)/shard_map/ppermute | solution.py:304
  16.1 0.3 collective-permute-done.1.x_ref
  16.4 5.6 %chunk_1_0.1 = (bf16[112,1024]{1,0:T(8,128)(2,1)S(1)}, bf16[96,1024]{1,0:T(8,128)(2,1)S(1)}, bf16[96,1024]{1,0:T(8,128)(2,1)S(1)}, f32[192,256]{1,0:T(8,128)S(1)}, f32[192,192]{1,0:T(8,128)S(1)}) custom-call(bf16[112,1024]{1,0:T(8,128)(2,1)S(1)} %collective-permute-done.1.x_ref, f32[1,1024]{1,0:T(1,128)S(1)} %get-tuple-element.36.gain_ref, ...), custom_call_target="tpu_custom_call" | custom-call | tf_op jit(solution)/shard_map/chunk_1_0/pallas_call | solution.py:377
  21.9 0.1 collective-permute-start.3
  22.0 0.0 collective-permute-done.x_ref
  22.0 5.7 %chunk_1_1.1 = (bf16[96,1024]{1,0:T(8,128)(2,1)S(1)}, bf16[96,1024]{1,0:T(8,128)(2,1)}, bf16[96,1024]{1,0:T(8,128)(2,1)}) custom-call(bf16[96,1024]{1,0:T(8,128)(2,1)S(1)} %collective-permute-done.x_ref, f32[1,1024]{1,0:T(1,128)S(1)} %get-tuple-element.36.gain_ref, bf16[1024,2048]{1,0:T(8,128)(2,1)S(1)} %get-tuple-element.37.wq_ref, ...), custom_call_target="tpu_custom_call" | custom-call | tf_op jit(solution)/shard_map/chunk_1_1/pallas_call | solution.py:377
  27.8 1.3 %collective-permute-start.2 = (bf16[96,1024]{1,0:T(8,128)(2,1)S(1)}, bf16[96,1024]{1,0:T(8,128)(2,1)S(1)}, u32[]{:S(2)}, u32[]{:S(2)}) collective-permute-start(bf16[96,1024]{1,0:T(8,128)(2,1)S(1)} %get-tuple-element.52), channel_id=1, source_target_pairs={{0,1},{1,2},{2,3},{3,4},{4,5},{5,6},{6,7},{7,8},{8,9},{9,10},{10,1... | collective-permute-start | bytes 589832 | tf_op jit(solution)/shard_map/ppermute | solution.py:304
  29.1 1.1 %collective-permute-done.3.x_ref = bf16[112,1024]{1,0:T(8,128)(2,1)S(1)} collective-permute-done((bf16[112,1024]{1,0:T(8,128)(2,1)S(1)}, bf16[112,1024]{1,0:T(8,128)(2,1)S(1)}, u32[]{:S(2)}, u32[]{:S(2)}) %collective-permute-start.3) | collective-permute-done | bytes 229408 | tf_op jit(solution)/shard_map/ppermute | solution.py:304
  30.1 5.6 %chunk_2_0.1 = (bf16[112,1024]{1,0:T(8,128)(2,1)S(1)}, bf16[96,1024]{1,0:T(8,128)(2,1)S(1)}, bf16[96,1024]{1,0:T(8,128)(2,1)S(1)}, f32[192,256]{1,0:T(8,128)S(1)}, f32[192,192]{1,0:T(8,128)S(1)}) custom-call(bf16[112,1024]{1,0:T(8,128)(2,1)S(1)} %collective-permute-done.3.x_ref, f32[1,1024]{1,0:T(1,128)S(1)} %get-tuple-element.36.gain_ref, ...), custom_call_target="tpu_custom_call" | custom-call | tf_op jit(solution)/shard_map/chunk_2_0/pallas_call | solution.py:377
  35.7 0.1 collective-permute-start.5
  35.8 0.0 collective-permute-done.2.x_ref
  35.8 5.7 %chunk_2_1.1 = (bf16[96,1024]{1,0:T(8,128)(2,1)S(1)}, bf16[96,1024]{1,0:T(8,128)(2,1)}, bf16[96,1024]{1,0:T(8,128)(2,1)}) custom-call(bf16[96,1024]{1,0:T(8,128)(2,1)S(1)} %collective-permute-done.2.x_ref, f32[1,1024]{1,0:T(1,128)S(1)} %get-tuple-element.36.gain_ref, bf16[1024,2048]{1,0:T(8,128)(2,1)S(1)} %get-tuple-element.37.wq_ref, ...), custom_call_target="tpu_custom_call" | custom-call | tf_op jit(solution)/shard_map/chunk_2_1/pallas_call | solution.py:377
  41.5 0.6 %collective-permute-start.4 = (bf16[96,1024]{1,0:T(8,128)(2,1)S(1)}, bf16[96,1024]{1,0:T(8,128)(2,1)S(1)}, u32[]{:S(2)}, u32[]{:S(2)}) collective-permute-start(bf16[96,1024]{1,0:T(8,128)(2,1)S(1)} %get-tuple-element.58), channel_id=1, source_target_pairs={{0,1},{1,2},{2,3},{3,4},{4,5},{5,6},{6,7},{7,8},{8,9},{9,10},{10,1... | collective-permute-start | bytes 589832 | tf_op jit(solution)/shard_map/ppermute | solution.py:304
  42.1 1.8 %collective-permute-done.5.x_ref = bf16[112,1024]{1,0:T(8,128)(2,1)S(1)} collective-permute-done((bf16[112,1024]{1,0:T(8,128)(2,1)S(1)}, bf16[112,1024]{1,0:T(8,128)(2,1)S(1)}, u32[]{:S(2)}, u32[]{:S(2)}) %collective-permute-start.5) | collective-permute-done | bytes 229408 | tf_op jit(solution)/shard_map/ppermute | solution.py:304
  43.9 5.6 %chunk_3_0.1 = (bf16[112,1024]{1,0:T(8,128)(2,1)S(1)}, bf16[96,1024]{1,0:T(8,128)(2,1)S(1)}, bf16[96,1024]{1,0:T(8,128)(2,1)S(1)}, f32[192,256]{1,0:T(8,128)S(1)}, f32[192,192]{1,0:T(8,128)S(1)}) custom-call(bf16[112,1024]{1,0:T(8,128)(2,1)S(1)} %collective-permute-done.5.x_ref, f32[1,1024]{1,0:T(1,128)S(1)} %get-tuple-element.36.gain_ref, ...), custom_call_target="tpu_custom_call" | custom-call | tf_op jit(solution)/shard_map/chunk_3_0/pallas_call | solution.py:377
  49.5 0.0 collective-permute-done.4.x_ref
  49.5 6.2 %chunk_3_1.1 = bf16[1,192,1024]{2,1,0:T(8,128)(2,1)} custom-call(bf16[96,1024]{1,0:T(8,128)(2,1)S(1)} %collective-permute-done.4.x_ref, f32[1,1024]{1,0:T(1,128)S(1)} %get-tuple-element.36.gain_ref, bf16[1024,2048]{1,0:T(8,128)(2,1)S(1)} %get-tuple-element.37.wq_ref, bf16[1024,1024]{1,0:T(8,128)(2,1)S(1)} %get-tuple-element.38.wk_ref, ...), custom_call_target="tpu_custom_call" | custom-call | tf_op jit(solution)/shard_map/chunk_3_1/pallas_call | solution.py:377
Async XLA Ops:
  7.2 9.2 %collective-permute-start.1 = (bf16[112,1024]{1,0:T(8,128)(2,1)S(1)}, bf16[112,1024]{1,0:T(8,128)(2,1)S(1)}, u32[]{:S(2)}, u32[]{:S(2)}) collective-permute-start(bf16[112,1024]{1,0:T(8,128)(2,1)S(1)} %get-tuple-element.46), channel_id=1, source_target_pairs={{0,1},{1,2},{2,3},{3,4},{4,5},{5,6},{6,7},{7,8},{8,9},{9,10},{10,1... | collective-permute-start | bytes 688136 | tf_op jit(solution)/shard_map/ppermute | solution.py:304
  13.4 8.6 %collective-permute-start = (bf16[96,1024]{1,0:T(8,128)(2,1)S(1)}, bf16[96,1024]{1,0:T(8,128)(2,1)S(1)}, u32[]{:S(2)}, u32[]{:S(2)}) collective-permute-start(bf16[96,1024]{1,0:T(8,128)(2,1)S(1)} %get-tuple-element.45), channel_id=1, source_target_pairs={{0,1},{1,2},{2,3},{3,4},{4,5},{5,6},{6,7},{7,8},{8,9},{9,10},{10,1... | collective-permute-start | bytes 589832 | tf_op jit(solution)/shard_map/ppermute | solution.py:304
  21.9 8.2 %collective-permute-start.3 = (bf16[112,1024]{1,0:T(8,128)(2,1)S(1)}, bf16[112,1024]{1,0:T(8,128)(2,1)S(1)}, u32[]{:S(2)}, u32[]{:S(2)}) collective-permute-start(bf16[112,1024]{1,0:T(8,128)(2,1)S(1)} %get-tuple-element.53), channel_id=1, source_target_pairs={{0,1},{1,2},{2,3},{3,4},{4,5},{5,6},{6,7},{7,8},{8,9},{9,10},{10,1... | collective-permute-start | bytes 688136 | tf_op jit(solution)/shard_map/ppermute | solution.py:304
  27.8 8.0 %collective-permute-start.2 = (bf16[96,1024]{1,0:T(8,128)(2,1)S(1)}, bf16[96,1024]{1,0:T(8,128)(2,1)S(1)}, u32[]{:S(2)}, u32[]{:S(2)}) collective-permute-start(bf16[96,1024]{1,0:T(8,128)(2,1)S(1)} %get-tuple-element.52), channel_id=1, source_target_pairs={{0,1},{1,2},{2,3},{3,4},{4,5},{5,6},{6,7},{7,8},{8,9},{9,10},{10,1... | collective-permute-start | bytes 589832 | tf_op jit(solution)/shard_map/ppermute | solution.py:304
  35.7 8.2 %collective-permute-start.5 = (bf16[112,1024]{1,0:T(8,128)(2,1)S(1)}, bf16[112,1024]{1,0:T(8,128)(2,1)S(1)}, u32[]{:S(2)}, u32[]{:S(2)}) collective-permute-start(bf16[112,1024]{1,0:T(8,128)(2,1)S(1)} %get-tuple-element.59), channel_id=1, source_target_pairs={{0,1},{1,2},{2,3},{3,4},{4,5},{5,6},{6,7},{7,8},{8,9},{9,10},{10,1... | collective-permute-start | bytes 688136 | tf_op jit(solution)/shard_map/ppermute | solution.py:304
  41.5 8.0 %collective-permute-start.4 = (bf16[96,1024]{1,0:T(8,128)(2,1)S(1)}, bf16[96,1024]{1,0:T(8,128)(2,1)S(1)}, u32[]{:S(2)}, u32[]{:S(2)}) collective-permute-start(bf16[96,1024]{1,0:T(8,128)(2,1)S(1)} %get-tuple-element.58), channel_id=1, source_target_pairs={{0,1},{1,2},{2,3},{3,4},{4,5},{5,6},{6,7},{7,8},{8,9},{9,10},{10,1... | collective-permute-start | bytes 589832 | tf_op jit(solution)/shard_map/ppermute | solution.py:304

commit v7 on v4

--- a/solution.py
+++ b/solution.py
@@ -207,7 +207,30 @@
         copy.wait()
 
 
-def chunk_kernel(index, last, x_ref, gain_ref, wq_ref, wk_ref, wv_ref, wo_ref, *refs):
+def chunk_kernel(index, last, paired, *refs):
+    refs = list(refs)
+    if paired:
+        outer, inner, sem, x_ref = refs.pop(0), refs.pop(0), refs.pop(-1), refs.pop(-1)
+        odd = lax.rem(lax.axis_index("section"), 2)
+
+        @pl.when(odd == 0)
+        def _():
+            copy = pltpu.make_async_copy(outer.at[0], x_ref, sem)
+            copy.start()
+            copy.wait()
+
+        @pl.when(odd == 1)
+        def _():
+            copy = pltpu.make_async_copy(inner.at[0], x_ref, sem)
+            copy.start()
+            copy.wait()
+
+    else:
+        x_ref = refs.pop(0)
+    chunk_rows(index, last, x_ref, *refs)
+
+
+def chunk_rows(index, last, x_ref, gain_ref, wq_ref, wk_ref, wv_ref, wo_ref, *refs):
     refs = list(refs)
     mixed_ref = refs.pop(-1)
     size = mixed_ref.shape[0]
@@ -266,9 +289,11 @@
     return pltpu.with_memory_space_constraint(array, pltpu.HBM)
 
 
-def passed_along(array, by):
+def passed_along(array):
     length = lax.axis_size("section")
-    return lax.ppermute(array, "section", [(i, (i + by) % length) for i in range(length)])
+    inner = [[i, i + 1] for i in range(0, length, 2)]
+    outer = [[i, (i + 1) % length] for i in range(1, length, 2)]
+    return tuple(lax.all_gather(array, "section", axis_index_groups=groups) for groups in (outer, inner))
 
 
 def body(micro, segment, gain, w_query, w_key, w_value, w_out):
@@ -319,11 +344,12 @@
         outs, keys, values = [], [], []
         for index in range(CHUNKS):
             if tick_index == 0 and index == 0:
-                outs.append(passed_along(streams[0], 1))
+                outs.append(passed_along(streams[0]))
                 keys.append(k_rows)
                 values.append(v_rows)
                 continue
-            args = [streams[index], *weights]
+            paired = isinstance(streams[index], tuple)
+            args = [*(streams[index] if paired else [streams[index]]), *weights]
             shapes = [kept((rows[index], model), BF16), *key_values]
             scratch = [mixing]
             if index == 0:
@@ -341,18 +367,20 @@
                     pltpu.VMEM((size, model), BF16), *[pltpu.VMEM((size, KV_WIDTH), BF16)] * 2,
                     pltpu.SemaphoreType.DMA((CHUNKS,)), mixing,
                 ]
+            if paired:
+                scratch = [*scratch, pltpu.VMEM((rows[index], model), BF16), pltpu.SemaphoreType.DMA]
             got = pl.pallas_call(
-                functools.partial(chunk_kernel, index, last),
-                out_shape=tuple(shapes), in_specs=[VMEM] * len(args), out_specs=tuple(specs),
+                functools.partial(chunk_kernel, index, last, paired),
+                out_shape=tuple(shapes), in_specs=[HBM] * (2 * paired) + [VMEM] * (len(args) - 2 * paired), out_specs=tuple(specs),
                 scratch_shapes=scratch, compiler_params=limits, name="chunk_%d_%d" % (tick_index, index),
-            )(*map(held, args))
+            )(*map(left, args[: 2 * paired]), *map(held, args[2 * paired :]))
             if ending:
                 return got[0]
             if index == 0:
                 cosines, bias = got[3:]
             keys.append(got[1])
             values.append(got[2])
-            outs.append(got[0] if last else passed_along(got[0], 1))
+            outs.append(got[0] if last else passed_along(got[0]))
         streams = outs
 
 

time: 45.7 us -> 103 us (2.25)
  blocking collectives: 0 us -> 67.2 us
  waiting for transfers between devices: 12.4 us -> 0 us
  Pallas kernels: 29.7 us -> 35.3 us
  starting transfers between devices: 3.26 us -> 0 us
    all_gather x0 -> x12, blocking collectives: none -> 67.2 us  [passed_along(): lax.all_gather(array, 'section', axis_index_groups=groups)]
    ppermute x6 -> x0, waiting for transfers between devices: 12.4 us -> none  [passed_along(): lax.ppermute(array, 'section', [(i, (i + by) % length) for i in range(len...]
    pallas_call x7, Pallas kernels: 22.5 us -> 28.1 us  [body(): pl.pallas_call(functools.partial(chunk_kernel, index, last, paired), out_...]
    ppermute x6 -> x0, starting transfers between devices: 3.26 us -> none  [passed_along(): lax.ppermute(array, 'section', [(i, (i + by) % length) for i in range(len...]
  transfers between devices with their start and end apart: 6 -> 0, of which waited for: 6 -> 0; matrix products, arithmetic and copies ran while one was open for 0% -> 0% of each run, Pallas kernels for 42% -> 0%
where the time goes in v7:
time: 103 us
  blocking collectives  67.2 us (65%)
  Pallas kernels  35.3 us (34%)
    all_gather x12, blocking collectives, passed_along(): lax.all_gather(array, 'section', axis_index_groups=groups)  67.2 us
    pallas_call x7, Pallas kernels, body(): pl.pallas_call(functools.partial(chunk_kernel, index, last, paired), out_...  28.1 us
    pallas_call x1, Pallas kernels, body(): pl.pallas_call(functools.partial(opening_kernel, size), out_shape=(kept((...  7.15 us

profile of v7, /device:TPU:0, one launch (start us, length us, event | category | flops | bytes accessed | tf_op | source)
XLA Modules:
  0.0 102.7 jit_solution(1803797714204662404)
XLA Ops:
  0.0 7.1 %opening.1 = (bf16[112,1024]{1,0:T(8,128)(2,1)S(1)}, bf16[96,1024]{1,0:T(8,128)(2,1)S(1)}, bf16[96,1024]{1,0:T(8,128)(2,1)S(1)}, f32[192,256]{1,0:T(8,128)S(1)},...) custom-call(bf16[1,192,1024]{2,1,0:T(8,128)(2,1)} %x_hbm.1, ...), custom_call_target="tpu_custom_call" | custom-call | tf_op jit(solution)/shard_map/opening/pallas_call | solution.py:309
  7.2 3.4 %chunk_0_1.1 = (bf16[96,1024]{1,0:T(8,128)(2,1)S(1)}, bf16[96,1024]{1,0:T(8,128)(2,1)}, bf16[96,1024]{1,0:T(8,128)(2,1)}) custom-call(bf16[96,1024]{1,0:T(8,128)(2,1)S(1)} %get-tuple-element.35.refs_0_, f32[1,1024]{1,0:T(1,128)S(1)} %get-tuple-element.36.refs_1_.refs_2_, bf16[1024,2048]{1,0:T(8,128)(2,1)S(1)} %get-tuple-element.37.refs_2_.refs_3_, ...), custom_call_target="tpu_custom_call" | custom-call | tf_op jit(solution)/shard_map/chunk_0_1/pallas_call | solution.py:372
  10.5 9.5 %all-gather = bf16[192,1024]{1,0:T(8,128)(2,1)} all-gather(bf16[96,1024]{1,0:T(8,128)(2,1)S(1)} %get-tuple-element.45), channel_id=2, replica_groups={{1,2},{3,4},{5,6},{7,8},{9,10},{11,12},{13,14},{15,0},{17,18},{19,20},{..., dimensions={0}, use_global_device_ids=true | all-gather | bytes 589824 | tf_op jit(solution)/shard_map/all_gather | solution.py:296
  20.1 2.2 %all-gather.1 = bf16[192,1024]{1,0:T(8,128)(2,1)} all-gather(bf16[96,1024]{1,0:T(8,128)(2,1)S(1)} %get-tuple-element.45), channel_id=3, replica_groups={{0,1},{2,3},{4,5},{6,7},{8,9},{10,11},{12,13},{14,15},{16,17},{18,19},{..., dimensions={0}, use_global_device_ids=true | all-gather | bytes 589824 | tf_op jit(solution)/shard_map/all_gather | solution.py:296
  22.3 9.0 %all-gather.2 = bf16[224,1024]{1,0:T(8,128)(2,1)} all-gather(bf16[112,1024]{1,0:T(8,128)(2,1)S(1)} %get-tuple-element.46), channel_id=4, replica_groups={{1,2},{3,4},{5,6},{7,8},{9,10},{11,12},{13,14},{15,0},{17,18},{19,20},{..., dimensions={0}, use_global_device_ids=true | all-gather | bytes 688128 | tf_op jit(solution)/shard_map/all_gather | solution.py:296
  31.3 2.3 %all-gather.3 = bf16[224,1024]{1,0:T(8,128)(2,1)} all-gather(bf16[112,1024]{1,0:T(8,128)(2,1)S(1)} %get-tuple-element.46), channel_id=5, replica_groups={{0,1},{2,3},{4,5},{6,7},{8,9},{10,11},{12,13},{14,15},{16,17},{18,19},{..., dimensions={0}, use_global_device_ids=true | all-gather | bytes 688128 | tf_op jit(solution)/shard_map/all_gather | solution.py:296
  33.5 3.9 %chunk_1_0.1 = (bf16[112,1024]{1,0:T(8,128)(2,1)S(1)}, bf16[96,1024]{1,0:T(8,128)(2,1)S(1)}, bf16[96,1024]{1,0:T(8,128)(2,1)S(1)}, f32[192,256]{1,0:T(8,128)S(1)}, f32[192,192]{1,0:T(8,128)S(1)}) custom-call(bf16[2,112,1024]{2,1,0:T(8,128)(2,1)} %bitcast.14, bf16[2,112,1024]{2,1,0:T(8,128)(2,1)} %bitcast.15, ...), custom_call_target="tpu_custom_call" | custom-call | tf_op jit(solution)/shard_map/chunk_1_0/pallas_call | solution.py:372
  37.4 4.3 %chunk_1_1.1 = (bf16[96,1024]{1,0:T(8,128)(2,1)S(1)}, bf16[96,1024]{1,0:T(8,128)(2,1)}, bf16[96,1024]{1,0:T(8,128)(2,1)}) custom-call(bf16[2,96,1024]{2,1,0:T(8,128)(2,1)} %bitcast.20, bf16[2,96,1024]{2,1,0:T(8,128)(2,1)} %bitcast.21, f32[1,1024]{1,0:T(1,128)S(1)} %get-tuple-element.36.refs_1_.refs_2_, ...), custom_call_target="tpu_custom_call" | custom-call | tf_op jit(solution)/shard_map/chunk_1_1/pallas_call | solution.py:372
  41.7 8.6 %all-gather.4 = bf16[192,1024]{1,0:T(8,128)(2,1)} all-gather(bf16[96,1024]{1,0:T(8,128)(2,1)S(1)} %get-tuple-element.52), channel_id=6, replica_groups={{1,2},{3,4},{5,6},{7,8},{9,10},{11,12},{13,14},{15,0},{17,18},{19,20},{..., dimensions={0}, use_global_device_ids=true | all-gather | bytes 589824 | tf_op jit(solution)/shard_map/all_gather | solution.py:296
  50.3 2.2 %all-gather.5 = bf16[192,1024]{1,0:T(8,128)(2,1)} all-gather(bf16[96,1024]{1,0:T(8,128)(2,1)S(1)} %get-tuple-element.52), channel_id=7, replica_groups={{0,1},{2,3},{4,5},{6,7},{8,9},{10,11},{12,13},{14,15},{16,17},{18,19},{..., dimensions={0}, use_global_device_ids=true | all-gather | bytes 589824 | tf_op jit(solution)/shard_map/all_gather | solution.py:296
  52.5 9.0 %all-gather.6 = bf16[224,1024]{1,0:T(8,128)(2,1)} all-gather(bf16[112,1024]{1,0:T(8,128)(2,1)S(1)} %get-tuple-element.53), channel_id=8, replica_groups={{1,2},{3,4},{5,6},{7,8},{9,10},{11,12},{13,14},{15,0},{17,18},{19,20},{..., dimensions={0}, use_global_device_ids=true | all-gather | bytes 688128 | tf_op jit(solution)/shard_map/all_gather | solution.py:296
  61.5 2.4 %all-gather.7 = bf16[224,1024]{1,0:T(8,128)(2,1)} all-gather(bf16[112,1024]{1,0:T(8,128)(2,1)S(1)} %get-tuple-element.53), channel_id=9, replica_groups={{0,1},{2,3},{4,5},{6,7},{8,9},{10,11},{12,13},{14,15},{16,17},{18,19},{..., dimensions={0}, use_global_device_ids=true | all-gather | bytes 688128 | tf_op jit(solution)/shard_map/all_gather | solution.py:296
  63.9 3.9 %chunk_2_0.1 = (bf16[112,1024]{1,0:T(8,128)(2,1)S(1)}, bf16[96,1024]{1,0:T(8,128)(2,1)S(1)}, bf16[96,1024]{1,0:T(8,128)(2,1)S(1)}, f32[192,256]{1,0:T(8,128)S(1)}, f32[192,192]{1,0:T(8,128)S(1)}) custom-call(bf16[2,112,1024]{2,1,0:T(8,128)(2,1)} %bitcast.16, bf16[2,112,1024]{2,1,0:T(8,128)(2,1)} %bitcast.17, ...), custom_call_target="tpu_custom_call" | custom-call | tf_op jit(solution)/shard_map/chunk_2_0/pallas_call | solution.py:372
  67.8 4.3 %chunk_2_1.1 = (bf16[96,1024]{1,0:T(8,128)(2,1)S(1)}, bf16[96,1024]{1,0:T(8,128)(2,1)}, bf16[96,1024]{1,0:T(8,128)(2,1)}) custom-call(bf16[2,96,1024]{2,1,0:T(8,128)(2,1)} %bitcast.22, bf16[2,96,1024]{2,1,0:T(8,128)(2,1)} %bitcast.23, f32[1,1024]{1,0:T(1,128)S(1)} %get-tuple-element.36.refs_1_.refs_2_, ...), custom_call_target="tpu_custom_call" | custom-call | tf_op jit(solution)/shard_map/chunk_2_1/pallas_call | solution.py:372
  72.2 8.6 %all-gather.8 = bf16[192,1024]{1,0:T(8,128)(2,1)} all-gather(bf16[96,1024]{1,0:T(8,128)(2,1)S(1)} %get-tuple-element.58), channel_id=10, replica_groups={{1,2},{3,4},{5,6},{7,8},{9,10},{11,12},{13,14},{15,0},{17,18},{19,20},{..., dimensions={0}, use_global_device_ids=true | all-gather | bytes 589824 | tf_op jit(solution)/shard_map/all_gather | solution.py:296
  80.7 2.2 %all-gather.9 = bf16[192,1024]{1,0:T(8,128)(2,1)} all-gather(bf16[96,1024]{1,0:T(8,128)(2,1)S(1)} %get-tuple-element.58), channel_id=11, replica_groups={{0,1},{2,3},{4,5},{6,7},{8,9},{10,11},{12,13},{14,15},{16,17},{18,19},{..., dimensions={0}, use_global_device_ids=true | all-gather | bytes 589824 | tf_op jit(solution)/shard_map/all_gather | solution.py:296
  82.9 9.0 %all-gather.10 = bf16[224,1024]{1,0:T(8,128)(2,1)} all-gather(bf16[112,1024]{1,0:T(8,128)(2,1)S(1)} %get-tuple-element.59), channel_id=12, replica_groups={{1,2},{3,4},{5,6},{7,8},{9,10},{11,12},{13,14},{15,0},{17,18},{19,20},{..., dimensions={0}, use_global_device_ids=true | all-gather | bytes 688128 | tf_op jit(solution)/shard_map/all_gather | solution.py:296
  91.9 2.3 %all-gather.11 = bf16[224,1024]{1,0:T(8,128)(2,1)} all-gather(bf16[112,1024]{1,0:T(8,128)(2,1)S(1)} %get-tuple-element.59), channel_id=13, replica_groups={{0,1},{2,3},{4,5},{6,7},{8,9},{10,11},{12,13},{14,15},{16,17},{18,19},{..., dimensions={0}, use_global_device_ids=true | all-gather | bytes 688128 | tf_op jit(solution)/shard_map/all_gather | solution.py:296
  94.2 3.9 %chunk_3_0.1 = (bf16[112,1024]{1,0:T(8,128)(2,1)S(1)}, bf16[96,1024]{1,0:T(8,128)(2,1)S(1)}, bf16[96,1024]{1,0:T(8,128)(2,1)S(1)}, f32[192,256]{1,0:T(8,128)S(1)}, f32[192,192]{1,0:T(8,128)S(1)}) custom-call(bf16[2,112,1024]{2,1,0:T(8,128)(2,1)} %bitcast.12, bf16[2,112,1024]{2,1,0:T(8,128)(2,1)} %bitcast.13, ...), custom_call_target="tpu_custom_call" | custom-call | tf_op jit(solution)/shard_map/chunk_3_0/pallas_call | solution.py:372
  98.1 4.5 %chunk_3_1.1 = bf16[1,192,1024]{2,1,0:T(8,128)(2,1)} custom-call(bf16[2,96,1024]{2,1,0:T(8,128)(2,1)} %bitcast.18, bf16[2,96,1024]{2,1,0:T(8,128)(2,1)} %bitcast.19, f32[1,1024]{1,0:T(1,128)S(1)} %get-tuple-element.36.refs_1_.refs_2_, bf16[1024,2048]{1,0:T(8,128)(2,1)S(1)} %get-tuple-element.37.refs_2_.refs_3_, ...), custom_call_target="tpu_custom_call" | custom-call | tf_op jit(solution)/shard_map/chunk_3_1/pallas_call | solution.py:372

commit v8 on v4

--- a/solution.py
+++ b/solution.py
@@ -55,7 +55,14 @@
     return values * cosine + pltpu.roll(values, HD // 2, 1) * sine
 
 
-def layer(x, gain, weights, wait, cos_rows, bias_rows, kept_keys, kept_values, k_ref, v_ref, mixed_ref, write):
+def blocks_of(low, size):
+    if low == 0 and size <= MAX_LEN:
+        return [(0, size, 0, size)]
+    step = HD - MAX_LEN
+    return [(top, step, max(0, low + top - MAX_LEN), low + top + step) for top in range(0, size, step)]
+
+
+def layer(x, gain, weights, wait, low, cos_rows, bias_ref, kept_keys, kept_values, k_ref, v_ref, mixed_ref, write):
     size, model = x.shape
     wq_ref, wk_ref, wv_ref, wo_ref = weights
     scale = lax.rsqrt(jnp.mean(x * x, axis=1, keepdims=True) + 1e-05) * (1.0 / LIFT)
@@ -82,45 +89,50 @@
         got = jnp.dot(lifted, wq_ref[:, start : start + PAIR], preferred_element_type=F32)
         upper = rotated(got[:, :HD], cosine_q, sine_q)
         lower = rotated(got[:, HD:], cosine_q, sine_q)
-        queries.append(jnp.concatenate([upper, lower], axis=0).astype(BF16))
-
-    count = bias_rows.shape[1]
-    ones = jnp.ones((count, HD), BF16)
-    groups = range(KV_HEADS)
+        queries.append((upper.astype(BF16), lower.astype(BF16)))
+
+    blocks = blocks_of(low, size)
+    biases = [bias_ref[low + top : low + top + height, first:last] for top, height, first, last in blocks]
+    spots = [(group, index) for group in range(KV_HEADS) for index in range(len(blocks))]
+
+    def seen(kept_parts, own_ref, group, first, last):
+        lanes, parts = slice(group * HD, (group + 1) * HD), []
+        for place, ref in enumerate([*kept_parts, own_ref]):
+            start, stop = max(first, place * size), min(last, (place + 1) * size)
+            if start < stop:
+                parts.append(ref[start - place * size : stop - place * size, lanes])
+        return parts[0] if len(parts) == 1 else jnp.concatenate(parts, axis=0)
+
     scores = []
-    for group in groups:
-        lanes = slice(group * HD, (group + 1) * HD)
-        key_rows = jnp.concatenate([rows[:, lanes] for rows in kept_keys] + [k_ref[:, lanes]], axis=0)
-        got = lax.dot_general(queries[group], key_rows, (((1,), (1,)), ((), ())), preferred_element_type=F32)
-        scores.append(got.reshape(2, size, count) + bias_rows[None])
+    for group, index in spots:
+        top, height, first, last = blocks[index]
+        both = jnp.concatenate([half[top : top + height] for half in queries[group]], axis=0)
+        key_rows = seen(kept_keys, k_ref, group, first, last)
+        got = lax.dot_general(both, key_rows, (((1,), (1,)), ((), ())), preferred_element_type=F32)
+        scores.append(got.reshape(2, height, last - first) + biases[index][None])
     most = [jnp.max(part, axis=2, keepdims=True) for part in scores]
-    expo = [jnp.exp2(scores[g] - most[g]).astype(BF16).reshape(2 * size, count) for g in groups]
+    expo = [
+        jnp.exp2(part - peak).astype(BF16).reshape(2 * part.shape[1], part.shape[2])
+        for part, peak in zip(scores, most)
+    ]
     got = []
-    for group in groups:
-        lanes = slice(group * HD, (group + 1) * HD)
-        value_rows = jnp.concatenate([rows[:, lanes] for rows in kept_values] + [v_ref[:, lanes]], axis=0)
-        value_rows = jnp.concatenate([value_rows, ones], axis=1)
-        got.append(jnp.dot(expo[group], value_rows, preferred_element_type=F32))
-    for group in groups:
-        total = got[group][:, HD:]
+    for (group, index), part in zip(spots, expo):
+        first, last = blocks[index][2:]
+        ones = jnp.ones((last - first, HD), BF16)
+        value_rows = jnp.concatenate([seen(kept_values, v_ref, group, first, last), ones], axis=1)
+        got.append(jnp.dot(part, value_rows, preferred_element_type=F32))
+    for (group, index), part in zip(spots, got):
+        top, height = blocks[index][:2]
+        total = part[:, HD:]
         inverse = pl.reciprocal(total, approx=True)
         inverse = inverse * (2.0 - total * inverse)
-        mixed = (got[group][:, :HD] * inverse).astype(BF16)
-        mixed_ref[:, group * PAIR : group * PAIR + HD] = mixed[:size]
-        mixed_ref[:, group * PAIR + HD : (group + 1) * PAIR] = mixed[size:]
+        mixed = (part[:, :HD] * inverse).astype(BF16)
+        mixed_ref[top : top + height, group * PAIR : group * PAIR + HD] = mixed[:height]
+        mixed_ref[top : top + height, group * PAIR + HD : (group + 1) * PAIR] = mixed[height:]
     for start in range(0, model, PAIR):
         wait("o", start)
         update = jnp.dot(mixed_ref[...], wo_ref[:, start : start + PAIR], preferred_element_type=F32)
         write(start, x[:, start : start + PAIR] + update)
-
-
-def first_key(low):
-    return max(0, low - MAX_LEN + 1) // 16 * 16
-
-
-def kept_rows(index, size, refs):
-    least = first_key(index * size)
-    return [ref[max(0, least - place * size) :] for place, ref in enumerate(refs) if (place + 1) * size > least]
 
 
 def write_ids(ids_row, out_ref, size):
@@ -148,7 +160,7 @@
     made = []
 
     def batch(source, target, rows, lanes):
-        step = (rows.stop - rows.start) // 4
+        step = (rows.stop - rows.start) // 8
         copies = []
         for low in range(rows.start, rows.stop, step):
             part = (slice(low, low + step), lanes)
@@ -180,11 +192,11 @@
         for index in arrivals.get((name, start), ()):
             for copy in batches[index]:
                 copy.wait()
-            begin(index + 3)
+            begin(index + 2)
 
     for copy in small:
         copy.start()
-    for index in range(3):
+    for index in range(2):
         begin(index)
     for copy in small:
         copy.wait()
@@ -201,7 +213,7 @@
 
     layer(
         x_ref[...].astype(F32), gain_ref[...], (wq_ref, wk_ref, wv_ref, wo_ref), wait,
-        cos_ref[:size, :], bias_ref[:size, :size], [], [], k_ref, v_ref, mixed_ref, write,
+        0, cos_ref[:size, :], bias_ref, [], [], k_ref, v_ref, mixed_ref, write,
     )
     for copy in late:
         copy.wait()
@@ -240,8 +252,7 @@
 
     layer(
         x_ref[:size, :].astype(F32), gain_ref[...], (wq_ref, wk_ref, wv_ref, wo_ref), lambda name, start: None,
-        cos_ref[low:high, :], bias_ref[low:high, first_key(low) : high],
-        kept_rows(index, size, keys), kept_rows(index, size, values), k_ref, v_ref, mixed_ref, write,
+        low, cos_ref[low:high, :], bias_ref, keys, values, k_ref, v_ref, mixed_ref, write,
     )
     if last and index == CHUNKS - 1:
         copy = pltpu.make_async_copy(out_ref, whole_ref.at[0, low:high], sems.at[index])
@@ -304,7 +315,7 @@
             pltpu.VMEM(table.shape, F32),
             mixing,
             pltpu.SemaphoreType.DMA((3 + CHUNKS,)),
-            pltpu.SemaphoreType.DMA((24,)),
+            pltpu.SemaphoreType.DMA((48,)),
         ],
         compiler_params=limits,
         name="opening",

time: 45.7 us -> 47.8 us (1.046)
  Pallas kernels: 29.7 us -> 31.8 us
    pallas_call x1, Pallas kernels: 7.15 us -> 8.63 us  [body(): pl.pallas_call(functools.partial(opening_kernel, size), out_shape=(kept((...]
    pallas_call x7, Pallas kernels: 22.5 us -> 23.1 us  [body(): pl.pallas_call(functools.partial(chunk_kernel, index, last), out_shape=tu...]
  transfers between devices with their start and end apart: 6 -> 6, of which waited for: 6 -> 6; matrix products, arithmetic and copies ran while one was open for 0% -> 0% of each run, Pallas kernels for 42% -> 41%
where the time goes in v8:
time: 47.8 us; the launch traced here: 47.6 us
  Pallas kernels  31.8 us (67%)
  waiting for transfers between devices  12.4 us (26%)
  starting transfers between devices  3.26 us (7%)
    pallas_call x7, Pallas kernels, body(): pl.pallas_call(functools.partial(chunk_kernel, index, last), out_shape=tu...  23.1 us
    ppermute x6, waiting for transfers between devices, passed_along(): lax.ppermute(array, 'section', [(i, (i + by) % length) for i in range(len...  12.4 us
    pallas_call x1, Pallas kernels, body(): pl.pallas_call(functools.partial(opening_kernel, size), out_shape=(kept((...  8.63 us
    ppermute x6, starting transfers between devices, passed_along(): lax.ppermute(array, 'section', [(i, (i + by) % length) for i in range(len...  3.26 us
  transfers between devices with their start and end apart: 6, of which 6 were waited for; matrix products, arithmetic and copies ran while one was open for 0% of the time, Pallas kernels for 41%

profile of v8, /device:TPU:0, one launch (start us, length us, event | category | flops | bytes accessed | tf_op | source)
XLA Modules:
  0.0 47.6 jit_solution(7955446869774656399)
XLA Ops:
  0.0 8.6 %opening.1 = (bf16[112,1024]{1,0:T(8,128)(2,1)S(1)}, bf16[96,1024]{1,0:T(8,128)(2,1)S(1)}, bf16[96,1024]{1,0:T(8,128)(2,1)S(1)}, f32[192,256]{1,0:T(8,128)S(1)},...) custom-call(bf16[1,192,1024]{2,1,0:T(8,128)(2,1)} %x_hbm.1, ...), custom_call_target="tpu_custom_call" | custom-call | tf_op jit(solution)/shard_map/opening/pallas_call | solution.py:295
  8.6 0.5 %collective-permute-start.1 = (bf16[112,1024]{1,0:T(8,128)(2,1)S(1)}, bf16[112,1024]{1,0:T(8,128)(2,1)S(1)}, u32[]{:S(2)}, u32[]{:S(2)}) collective-permute-start(bf16[112,1024]{1,0:T(8,128)(2,1)S(1)} %get-tuple-element.46), channel_id=1, source_target_pairs={{0,1},{1,2},{2,3},{3,4},{4,5},{5,6},{6,7},{7,8},{8,9},{9,10},{10,1... | collective-permute-start | bytes 688136 | tf_op jit(solution)/shard_map/ppermute | solution.py:282
  9.2 3.5 %chunk_0_1.1 = (bf16[96,1024]{1,0:T(8,128)(2,1)S(1)}, bf16[96,1024]{1,0:T(8,128)(2,1)}, bf16[96,1024]{1,0:T(8,128)(2,1)}) custom-call(bf16[96,1024]{1,0:T(8,128)(2,1)S(1)} %get-tuple-element.35.x_ref, f32[1,1024]{1,0:T(1,128)S(1)} %get-tuple-element.36.gain_ref, bf16[1024,2048]{1,0:T(8,128)(2,1)S(1)} %get-tuple-element.37.wq_ref, ...), custom_call_target="tpu_custom_call" | custom-call | tf_op jit(solution)/shard_map/chunk_0_1/pallas_call | solution.py:355
  12.7 2.6 %collective-permute-start = (bf16[96,1024]{1,0:T(8,128)(2,1)S(1)}, bf16[96,1024]{1,0:T(8,128)(2,1)S(1)}, u32[]{:S(2)}, u32[]{:S(2)}) collective-permute-start(bf16[96,1024]{1,0:T(8,128)(2,1)S(1)} %get-tuple-element.45), channel_id=1, source_target_pairs={{0,1},{1,2},{2,3},{3,4},{4,5},{5,6},{6,7},{7,8},{8,9},{9,10},{10,1... | collective-permute-start | bytes 589832 | tf_op jit(solution)/shard_map/ppermute | solution.py:282
  15.3 2.5 %collective-permute-done.1.x_ref = bf16[112,1024]{1,0:T(8,128)(2,1)S(1)} collective-permute-done((bf16[112,1024]{1,0:T(8,128)(2,1)S(1)}, bf16[112,1024]{1,0:T(8,128)(2,1)S(1)}, u32[]{:S(2)}, u32[]{:S(2)}) %collective-permute-start.1) | collective-permute-done | bytes 229408 | tf_op jit(solution)/shard_map/ppermute | solution.py:282
  17.9 2.9 %chunk_1_0.1 = (bf16[112,1024]{1,0:T(8,128)(2,1)S(1)}, bf16[96,1024]{1,0:T(8,128)(2,1)S(1)}, bf16[96,1024]{1,0:T(8,128)(2,1)S(1)}, f32[192,256]{1,0:T(8,128)S(1)}, f32[192,192]{1,0:T(8,128)S(1)}) custom-call(bf16[112,1024]{1,0:T(8,128)(2,1)S(1)} %collective-permute-done.1.x_ref, f32[1,1024]{1,0:T(1,128)S(1)} %get-tuple-element.36.gain_ref, ...), custom_call_target="tpu_custom_call" | custom-call | tf_op jit(solution)/shard_map/chunk_1_0/pallas_call | solution.py:355
  20.8 0.1 collective-permute-start.3
  20.8 0.2 collective-permute-done.x_ref
  21.1 3.6 %chunk_1_1.1 = (bf16[96,1024]{1,0:T(8,128)(2,1)S(1)}, bf16[96,1024]{1,0:T(8,128)(2,1)}, bf16[96,1024]{1,0:T(8,128)(2,1)}) custom-call(bf16[96,1024]{1,0:T(8,128)(2,1)S(1)} %collective-permute-done.x_ref, f32[1,1024]{1,0:T(1,128)S(1)} %get-tuple-element.36.gain_ref, bf16[1024,2048]{1,0:T(8,128)(2,1)S(1)} %get-tuple-element.37.wq_ref, ...), custom_call_target="tpu_custom_call" | custom-call | tf_op jit(solution)/shard_map/chunk_1_1/pallas_call | solution.py:355
  24.6 0.0 collective-permute-start.2
  24.6 4.3 %collective-permute-done.3.x_ref = bf16[112,1024]{1,0:T(8,128)(2,1)S(1)} collective-permute-done((bf16[112,1024]{1,0:T(8,128)(2,1)S(1)}, bf16[112,1024]{1,0:T(8,128)(2,1)S(1)}, u32[]{:S(2)}, u32[]{:S(2)}) %collective-permute-start.3) | collective-permute-done | bytes 229408 | tf_op jit(solution)/shard_map/ppermute | solution.py:282
  29.0 2.9 %chunk_2_0.1 = (bf16[112,1024]{1,0:T(8,128)(2,1)S(1)}, bf16[96,1024]{1,0:T(8,128)(2,1)S(1)}, bf16[96,1024]{1,0:T(8,128)(2,1)S(1)}, f32[192,256]{1,0:T(8,128)S(1)}, f32[192,192]{1,0:T(8,128)S(1)}) custom-call(bf16[112,1024]{1,0:T(8,128)(2,1)S(1)} %collective-permute-done.3.x_ref, f32[1,1024]{1,0:T(1,128)S(1)} %get-tuple-element.36.gain_ref, ...), custom_call_target="tpu_custom_call" | custom-call | tf_op jit(solution)/shard_map/chunk_2_0/pallas_call | solution.py:355
  31.9 0.1 collective-permute-start.5
  32.0 0.5 collective-permute-done.2.x_ref
  32.4 3.5 %chunk_2_1.1 = (bf16[96,1024]{1,0:T(8,128)(2,1)S(1)}, bf16[96,1024]{1,0:T(8,128)(2,1)}, bf16[96,1024]{1,0:T(8,128)(2,1)}) custom-call(bf16[96,1024]{1,0:T(8,128)(2,1)S(1)} %collective-permute-done.2.x_ref, f32[1,1024]{1,0:T(1,128)S(1)} %get-tuple-element.36.gain_ref, bf16[1024,2048]{1,0:T(8,128)(2,1)S(1)} %get-tuple-element.37.wq_ref, ...), custom_call_target="tpu_custom_call" | custom-call | tf_op jit(solution)/shard_map/chunk_2_1/pallas_call | solution.py:355
  36.0 0.0 collective-permute-start.4
  36.0 4.1 %collective-permute-done.5.x_ref = bf16[112,1024]{1,0:T(8,128)(2,1)S(1)} collective-permute-done((bf16[112,1024]{1,0:T(8,128)(2,1)S(1)}, bf16[112,1024]{1,0:T(8,128)(2,1)S(1)}, u32[]{:S(2)}, u32[]{:S(2)}) %collective-permute-start.5) | collective-permute-done | bytes 229408 | tf_op jit(solution)/shard_map/ppermute | solution.py:282
  40.1 2.9 %chunk_3_0.1 = (bf16[112,1024]{1,0:T(8,128)(2,1)S(1)}, bf16[96,1024]{1,0:T(8,128)(2,1)S(1)}, bf16[96,1024]{1,0:T(8,128)(2,1)S(1)}, f32[192,256]{1,0:T(8,128)S(1)}, f32[192,192]{1,0:T(8,128)S(1)}) custom-call(bf16[112,1024]{1,0:T(8,128)(2,1)S(1)} %collective-permute-done.5.x_ref, f32[1,1024]{1,0:T(1,128)S(1)} %get-tuple-element.36.gain_ref, ...), custom_call_target="tpu_custom_call" | custom-call | tf_op jit(solution)/shard_map/chunk_3_0/pallas_call | solution.py:355
  43.0 0.8 %collective-permute-done.4.x_ref = bf16[96,1024]{1,0:T(8,128)(2,1)S(1)} collective-permute-done((bf16[96,1024]{1,0:T(8,128)(2,1)S(1)}, bf16[96,1024]{1,0:T(8,128)(2,1)S(1)}, u32[]{:S(2)}, u32[]{:S(2)}) %collective-permute-start.4) | collective-permute-done | bytes 196640 | tf_op jit(solution)/shard_map/ppermute | solution.py:282
  43.8 3.7 %chunk_3_1.1 = bf16[1,192,1024]{2,1,0:T(8,128)(2,1)} custom-call(bf16[96,1024]{1,0:T(8,128)(2,1)S(1)} %collective-permute-done.4.x_ref, f32[1,1024]{1,0:T(1,128)S(1)} %get-tuple-element.36.gain_ref, bf16[1024,2048]{1,0:T(8,128)(2,1)S(1)} %get-tuple-element.37.wq_ref, bf16[1024,1024]{1,0:T(8,128)(2,1)S(1)} %get-tuple-element.38.wk_ref, ...), custom_call_target="tpu_custom_call" | custom-call | tf_op jit(solution)/shard_map/chunk_3_1/pallas_call | solution.py:355
Async XLA Ops:
  8.6 9.2 %collective-permute-start.1 = (bf16[112,1024]{1,0:T(8,128)(2,1)S(1)}, bf16[112,1024]{1,0:T(8,128)(2,1)S(1)}, u32[]{:S(2)}, u32[]{:S(2)}) collective-permute-start(bf16[112,1024]{1,0:T(8,128)(2,1)S(1)} %get-tuple-element.46), channel_id=1, source_target_pairs={{0,1},{1,2},{2,3},{3,4},{4,5},{5,6},{6,7},{7,8},{8,9},{9,10},{10,1... | collective-permute-start | bytes 688136 | tf_op jit(solution)/shard_map/ppermute | solution.py:282
  12.7 8.4 %collective-permute-start = (bf16[96,1024]{1,0:T(8,128)(2,1)S(1)}, bf16[96,1024]{1,0:T(8,128)(2,1)S(1)}, u32[]{:S(2)}, u32[]{:S(2)}) collective-permute-start(bf16[96,1024]{1,0:T(8,128)(2,1)S(1)} %get-tuple-element.45), channel_id=1, source_target_pairs={{0,1},{1,2},{2,3},{3,4},{4,5},{5,6},{6,7},{7,8},{8,9},{9,10},{10,1... | collective-permute-start | bytes 589832 | tf_op jit(solution)/shard_map/ppermute | solution.py:282
  20.8 8.2 %collective-permute-start.3 = (bf16[112,1024]{1,0:T(8,128)(2,1)S(1)}, bf16[112,1024]{1,0:T(8,128)(2,1)S(1)}, u32[]{:S(2)}, u32[]{:S(2)}) collective-permute-start(bf16[112,1024]{1,0:T(8,128)(2,1)S(1)} %get-tuple-element.53), channel_id=1, source_target_pairs={{0,1},{1,2},{2,3},{3,4},{4,5},{5,6},{6,7},{7,8},{8,9},{9,10},{10,1... | collective-permute-start | bytes 688136 | tf_op jit(solution)/shard_map/ppermute | solution.py:282
  24.6 7.8 %collective-permute-start.2 = (bf16[96,1024]{1,0:T(8,128)(2,1)S(1)}, bf16[96,1024]{1,0:T(8,128)(2,1)S(1)}, u32[]{:S(2)}, u32[]{:S(2)}) collective-permute-start(bf16[96,1024]{1,0:T(8,128)(2,1)S(1)} %get-tuple-element.52), channel_id=1, source_target_pairs={{0,1},{1,2},{2,3},{3,4},{4,5},{5,6},{6,7},{7,8},{8,9},{9,10},{10,1... | collective-permute-start | bytes 589832 | tf_op jit(solution)/shard_map/ppermute | solution.py:282
  31.9 8.2 %collective-permute-start.5 = (bf16[112,1024]{1,0:T(8,128)(2,1)S(1)}, bf16[112,1024]{1,0:T(8,128)(2,1)S(1)}, u32[]{:S(2)}, u32[]{:S(2)}) collective-permute-start(bf16[112,1024]{1,0:T(8,128)(2,1)S(1)} %get-tuple-element.59), channel_id=1, source_target_pairs={{0,1},{1,2},{2,3},{3,4},{4,5},{5,6},{6,7},{7,8},{8,9},{9,10},{10,1... | collective-permute-start | bytes 688136 | tf_op jit(solution)/shard_map/ppermute | solution.py:282
  36.0 7.8 %collective-permute-start.4 = (bf16[96,1024]{1,0:T(8,128)(2,1)S(1)}, bf16[96,1024]{1,0:T(8,128)(2,1)S(1)}, u32[]{:S(2)}, u32[]{:S(2)}) collective-permute-start(bf16[96,1024]{1,0:T(8,128)(2,1)S(1)} %get-tuple-element.58), channel_id=1, source_target_pairs={{0,1},{1,2},{2,3},{3,4},{4,5},{5,6},{6,7},{7,8},{8,9},{9,10},{10,1... | collective-permute-start | bytes 589832 | tf_op jit(solution)/shard_map/ppermute | solution.py:282

commit v9 on v4

--- a/solution.py
+++ b/solution.py
@@ -35,6 +35,11 @@
     return np.concatenate([high, low], axis=0)
 
 
+def lower_triangle(rows, columns):
+    row_index = lax.broadcasted_iota(jnp.int32, (rows, columns), 0)
+    return lax.broadcasted_iota(jnp.int32, (rows, columns), 1) <= row_index
+
+
 def tables_of(ids_row, table):
     length = ids_row.shape[1]
     across = jnp.broadcast_to(ids_row, (length, length))
@@ -44,6 +49,10 @@
     matched = across == down
     places = jnp.sum(jnp.where(matched & (column < row_index), 1.0, 0.0), axis=1, keepdims=True)
     bias = jnp.where(matched & (column <= row_index), 0.0, HIDDEN)
+    own, earlier_keys = bias[MAX_LEN:, MAX_LEN:], bias[MAX_LEN:, :MAX_LEN]
+    merged = jnp.where(lower_triangle(MAX_LEN, MAX_LEN), own, earlier_keys)
+    merged = jnp.concatenate([merged, jnp.full((length - MAX_LEN, HD - MAX_LEN), HIDDEN, F32)], axis=1)
+    bias = jnp.concatenate([bias[:MAX_LEN, :HD], merged], axis=0)
     slots = lax.broadcasted_iota(jnp.int32, (length, 2 * MAX_LEN), 1)
     slots = jnp.where(slots >= MAX_LEN, slots - MAX_LEN, slots).astype(F32)
     one_hot = jnp.where(slots == places, 1.0, 0.0).astype(BF16)
@@ -84,23 +93,37 @@
         lower = rotated(got[:, HD:], cosine_q, sine_q)
         queries.append(jnp.concatenate([upper, lower], axis=0).astype(BF16))
 
-    count = bias_rows.shape[1]
-    ones = jnp.ones((count, HD), BF16)
     groups = range(KV_HEADS)
+    spare = jnp.zeros((HD - size, HD), BF16)
+    lower = lower_triangle(size, HD)
+    lower_share = jnp.where(lower, 1.0, 0.0).astype(BF16)
+
+    def rows_of(refs, group):
+        lanes = slice(group * HD, (group + 1) * HD)
+        if len(refs) == 1:
+            return refs[0][:, lanes]
+        return jnp.concatenate([part for ref in refs for part in (ref[:, lanes], spare)], axis=0)
+
+    key_refs, value_refs = [k_ref, *kept_keys], [v_ref, *kept_values]
     scores = []
     for group in groups:
-        lanes = slice(group * HD, (group + 1) * HD)
-        key_rows = jnp.concatenate([rows[:, lanes] for rows in kept_keys] + [k_ref[:, lanes]], axis=0)
+        key_rows = rows_of(key_refs, group)
         got = lax.dot_general(queries[group], key_rows, (((1,), (1,)), ((), ())), preferred_element_type=F32)
-        scores.append(got.reshape(2, size, count) + bias_rows[None])
+        got = got.reshape(2, size, key_rows.shape[0])
+        if kept_keys:
+            got = jnp.where(lower[None], got[:, :, :HD], got[:, :, HD:])
+        scores.append(got + bias_rows[None])
     most = [jnp.max(part, axis=2, keepdims=True) for part in scores]
-    expo = [jnp.exp2(scores[g] - most[g]).astype(BF16).reshape(2 * size, count) for g in groups]
+    expo = [jnp.exp2(scores[g] - most[g]).astype(BF16) for g in groups]
+    if kept_keys:
+        own = [part * lower_share[None] for part in expo]
+        expo = [jnp.concatenate([mine, part - mine], axis=2) for mine, part in zip(own, expo)]
     got = []
     for group in groups:
-        lanes = slice(group * HD, (group + 1) * HD)
-        value_rows = jnp.concatenate([rows[:, lanes] for rows in kept_values] + [v_ref[:, lanes]], axis=0)
-        value_rows = jnp.concatenate([value_rows, ones], axis=1)
-        got.append(jnp.dot(expo[group], value_rows, preferred_element_type=F32))
+        value_rows = rows_of(value_refs, group)
+        value_rows = jnp.concatenate([value_rows, jnp.ones((value_rows.shape[0], HD), BF16)], axis=1)
+        part = expo[group].reshape(2 * size, value_rows.shape[0])
+        got.append(jnp.dot(part, value_rows, preferred_element_type=F32))
     for group in groups:
         total = got[group][:, HD:]
         inverse = pl.reciprocal(total, approx=True)
@@ -112,15 +135,6 @@
         wait("o", start)
         update = jnp.dot(mixed_ref[...], wo_ref[:, start : start + PAIR], preferred_element_type=F32)
         write(start, x[:, start : start + PAIR] + update)
-
-
-def first_key(low):
-    return max(0, low - MAX_LEN + 1) // 16 * 16
-
-
-def kept_rows(index, size, refs):
-    least = first_key(index * size)
-    return [ref[max(0, least - place * size) :] for place, ref in enumerate(refs) if (place + 1) * size > least]
 
 
 def write_ids(ids_row, out_ref, size):
@@ -148,7 +162,7 @@
     made = []
 
     def batch(source, target, rows, lanes):
-        step = (rows.stop - rows.start) // 4
+        step = (rows.stop - rows.start) // 2
         copies = []
         for low in range(rows.start, rows.stop, step):
             part = (slice(low, low + step), lanes)
@@ -240,8 +254,8 @@
 
     layer(
         x_ref[:size, :].astype(F32), gain_ref[...], (wq_ref, wk_ref, wv_ref, wo_ref), lambda name, start: None,
-        cos_ref[low:high, :], bias_ref[low:high, first_key(low) : high],
-        kept_rows(index, size, keys), kept_rows(index, size, values), k_ref, v_ref, mixed_ref, write,
+        cos_ref[low:high, :], bias_ref[low:high, :] if index else bias_ref[:size, :size],
+        keys, values, k_ref, v_ref, mixed_ref, write,
     )
     if last and index == CHUNKS - 1:
         copy = pltpu.make_async_copy(out_ref, whole_ref.at[0, low:high], sems.at[index])
@@ -278,7 +292,7 @@
     table = jnp.asarray(rope_table())
     rows = [size + EXTRA] + [size] * (CHUNKS - 1)
     key_values = [kept((size, KV_WIDTH), BF16)] * 2
-    tables = [kept((length, PAIR), F32), kept((length, length), F32)]
+    tables = [kept((length, PAIR), F32), kept((length, HD), F32)]
     mixing = pltpu.VMEM((size, Q_WIDTH), BF16)
 
     got = pl.pallas_call(
@@ -304,7 +318,7 @@
             pltpu.VMEM(table.shape, F32),
             mixing,
             pltpu.SemaphoreType.DMA((3 + CHUNKS,)),
-            pltpu.SemaphoreType.DMA((24,)),
+            pltpu.SemaphoreType.DMA((12,)),
         ],
         compiler_params=limits,
         name="opening",

time: 45.7 us -> 45.3 us (level)
  Pallas kernels: 29.7 us -> 29.2 us
  transfers between devices with their start and end apart: 6 -> 6, of which waited for: 6 -> 3; matrix products, arithmetic and copies ran while one was open for 0% -> 0% of each run, Pallas kernels for 42% -> 42%
where the time goes in v9:
time: 45.3 us; the launch traced here: 45.1 us
  Pallas kernels  29.2 us (64%)
  waiting for transfers between devices  12.4 us (27%)
  starting transfers between devices  3.26 us (7%)
    pallas_call x7, Pallas kernels, body(): pl.pallas_call(functools.partial(chunk_kernel, index, last), out_shape=tu...  22.2 us
    ppermute x6, waiting for transfers between devices, passed_along(): lax.ppermute(array, 'section', [(i, (i + by) % length) for i in range(len...  12.4 us
    pallas_call x1, Pallas kernels, body(): pl.pallas_call(functools.partial(opening_kernel, size), out_shape=(kept((...  6.98 us
    ppermute x6, starting transfers between devices, passed_along(): lax.ppermute(array, 'section', [(i, (i + by) % length) for i in range(len...  3.26 us
  transfers between devices with their start and end apart: 6, of which 3 were waited for; matrix products, arithmetic and copies ran while one was open for 0% of the time, Pallas kernels for 42%

profile of v9, /device:TPU:0, one launch (start us, length us, event | category | flops | bytes accessed | tf_op | source)
XLA Modules:
  0.0 45.1 jit_solution(8957503067944686482)
XLA Ops:
  0.0 7.0 %opening.1 = (bf16[112,1024]{1,0:T(8,128)(2,1)S(1)}, bf16[96,1024]{1,0:T(8,128)(2,1)S(1)}, bf16[96,1024]{1,0:T(8,128)(2,1)S(1)}, f32[192,256]{1,0:T(8,128)S(1)},...) custom-call(bf16[1,192,1024]{2,1,0:T(8,128)(2,1)} %x_hbm.1, ...), custom_call_target="tpu_custom_call" | custom-call | tf_op jit(solution)/shard_map/opening/pallas_call | solution.py:298
  7.0 0.5 %collective-permute-start.1 = (bf16[112,1024]{1,0:T(8,128)(2,1)S(1)}, bf16[112,1024]{1,0:T(8,128)(2,1)S(1)}, u32[]{:S(2)}, u32[]{:S(2)}) collective-permute-start(bf16[112,1024]{1,0:T(8,128)(2,1)S(1)} %get-tuple-element.46), channel_id=1, source_target_pairs={{0,1},{1,2},{2,3},{3,4},{4,5},{5,6},{6,7},{7,8},{8,9},{9,10},{10,1... | collective-permute-start | bytes 688136 | tf_op jit(solution)/shard_map/ppermute | solution.py:285
  7.5 3.3 %chunk_0_1.1 = (bf16[96,1024]{1,0:T(8,128)(2,1)S(1)}, bf16[96,1024]{1,0:T(8,128)(2,1)}, bf16[96,1024]{1,0:T(8,128)(2,1)}) custom-call(bf16[96,1024]{1,0:T(8,128)(2,1)S(1)} %get-tuple-element.35.x_ref, f32[1,1024]{1,0:T(1,128)S(1)} %get-tuple-element.36.gain_ref, bf16[1024,2048]{1,0:T(8,128)(2,1)S(1)} %get-tuple-element.37.wq_ref, ...), custom_call_target="tpu_custom_call" | custom-call | tf_op jit(solution)/shard_map/chunk_0_1/pallas_call | solution.py:358
  10.8 2.6 %collective-permute-start = (bf16[96,1024]{1,0:T(8,128)(2,1)S(1)}, bf16[96,1024]{1,0:T(8,128)(2,1)S(1)}, u32[]{:S(2)}, u32[]{:S(2)}) collective-permute-start(bf16[96,1024]{1,0:T(8,128)(2,1)S(1)} %get-tuple-element.45), channel_id=1, source_target_pairs={{0,1},{1,2},{2,3},{3,4},{4,5},{5,6},{6,7},{7,8},{8,9},{9,10},{10,1... | collective-permute-start | bytes 589832 | tf_op jit(solution)/shard_map/ppermute | solution.py:285
  13.4 2.8 %collective-permute-done.1.x_ref = bf16[112,1024]{1,0:T(8,128)(2,1)S(1)} collective-permute-done((bf16[112,1024]{1,0:T(8,128)(2,1)S(1)}, bf16[112,1024]{1,0:T(8,128)(2,1)S(1)}, u32[]{:S(2)}, u32[]{:S(2)}) %collective-permute-start.1) | collective-permute-done | bytes 229408 | tf_op jit(solution)/shard_map/ppermute | solution.py:285
  16.2 3.0 %chunk_1_0.1 = (bf16[112,1024]{1,0:T(8,128)(2,1)S(1)}, bf16[96,1024]{1,0:T(8,128)(2,1)S(1)}, bf16[96,1024]{1,0:T(8,128)(2,1)S(1)}, f32[192,256]{1,0:T(8,128)S(1)}, f32[192,128]{1,0:T(8,128)S(1)}) custom-call(bf16[112,1024]{1,0:T(8,128)(2,1)S(1)} %collective-permute-done.1.x_ref, f32[1,1024]{1,0:T(1,128)S(1)} %get-tuple-element.36.gain_ref, ...), custom_call_target="tpu_custom_call" | custom-call | tf_op jit(solution)/shard_map/chunk_1_0/pallas_call | solution.py:358
  19.2 0.1 collective-permute-start.3
  19.2 0.0 collective-permute-done.x_ref
  19.2 3.3 %chunk_1_1.1 = (bf16[96,1024]{1,0:T(8,128)(2,1)S(1)}, bf16[96,1024]{1,0:T(8,128)(2,1)}, bf16[96,1024]{1,0:T(8,128)(2,1)}) custom-call(bf16[96,1024]{1,0:T(8,128)(2,1)S(1)} %collective-permute-done.x_ref, f32[1,1024]{1,0:T(1,128)S(1)} %get-tuple-element.36.gain_ref, bf16[1024,2048]{1,0:T(8,128)(2,1)S(1)} %get-tuple-element.37.wq_ref, ...), custom_call_target="tpu_custom_call" | custom-call | tf_op jit(solution)/shard_map/chunk_1_1/pallas_call | solution.py:358
  22.5 0.0 collective-permute-start.2
  22.5 4.8 %collective-permute-done.3.x_ref = bf16[112,1024]{1,0:T(8,128)(2,1)S(1)} collective-permute-done((bf16[112,1024]{1,0:T(8,128)(2,1)S(1)}, bf16[112,1024]{1,0:T(8,128)(2,1)S(1)}, u32[]{:S(2)}, u32[]{:S(2)}) %collective-permute-start.3) | collective-permute-done | bytes 229408 | tf_op jit(solution)/shard_map/ppermute | solution.py:285
  27.4 3.0 %chunk_2_0.1 = (bf16[112,1024]{1,0:T(8,128)(2,1)S(1)}, bf16[96,1024]{1,0:T(8,128)(2,1)S(1)}, bf16[96,1024]{1,0:T(8,128)(2,1)S(1)}, f32[192,256]{1,0:T(8,128)S(1)}, f32[192,128]{1,0:T(8,128)S(1)}) custom-call(bf16[112,1024]{1,0:T(8,128)(2,1)S(1)} %collective-permute-done.3.x_ref, f32[1,1024]{1,0:T(1,128)S(1)} %get-tuple-element.36.gain_ref, ...), custom_call_target="tpu_custom_call" | custom-call | tf_op jit(solution)/shard_map/chunk_2_0/pallas_call | solution.py:358
  30.3 0.1 collective-permute-start.5
  30.4 0.0 collective-permute-done.2.x_ref
  30.4 3.3 %chunk_2_1.1 = (bf16[96,1024]{1,0:T(8,128)(2,1)S(1)}, bf16[96,1024]{1,0:T(8,128)(2,1)}, bf16[96,1024]{1,0:T(8,128)(2,1)}) custom-call(bf16[96,1024]{1,0:T(8,128)(2,1)S(1)} %collective-permute-done.2.x_ref, f32[1,1024]{1,0:T(1,128)S(1)} %get-tuple-element.36.gain_ref, bf16[1024,2048]{1,0:T(8,128)(2,1)S(1)} %get-tuple-element.37.wq_ref, ...), custom_call_target="tpu_custom_call" | custom-call | tf_op jit(solution)/shard_map/chunk_2_1/pallas_call | solution.py:358
  33.7 0.0 collective-permute-start.4
  33.7 4.8 %collective-permute-done.5.x_ref = bf16[112,1024]{1,0:T(8,128)(2,1)S(1)} collective-permute-done((bf16[112,1024]{1,0:T(8,128)(2,1)S(1)}, bf16[112,1024]{1,0:T(8,128)(2,1)S(1)}, u32[]{:S(2)}, u32[]{:S(2)}) %collective-permute-start.5) | collective-permute-done | bytes 229408 | tf_op jit(solution)/shard_map/ppermute | solution.py:285
  38.5 2.9 %chunk_3_0.1 = (bf16[112,1024]{1,0:T(8,128)(2,1)S(1)}, bf16[96,1024]{1,0:T(8,128)(2,1)S(1)}, bf16[96,1024]{1,0:T(8,128)(2,1)S(1)}, f32[192,256]{1,0:T(8,128)S(1)}, f32[192,128]{1,0:T(8,128)S(1)}) custom-call(bf16[112,1024]{1,0:T(8,128)(2,1)S(1)} %collective-permute-done.5.x_ref, f32[1,1024]{1,0:T(1,128)S(1)} %get-tuple-element.36.gain_ref, ...), custom_call_target="tpu_custom_call" | custom-call | tf_op jit(solution)/shard_map/chunk_3_0/pallas_call | solution.py:358
  41.4 0.0 collective-permute-done.4.x_ref
  41.5 3.5 %chunk_3_1.1 = bf16[1,192,1024]{2,1,0:T(8,128)(2,1)} custom-call(bf16[96,1024]{1,0:T(8,128)(2,1)S(1)} %collective-permute-done.4.x_ref, f32[1,1024]{1,0:T(1,128)S(1)} %get-tuple-element.36.gain_ref, bf16[1024,2048]{1,0:T(8,128)(2,1)S(1)} %get-tuple-element.37.wq_ref, bf16[1024,1024]{1,0:T(8,128)(2,1)S(1)} %get-tuple-element.38.wk_ref, ...), custom_call_target="tpu_custom_call" | custom-call | tf_op jit(solution)/shard_map/chunk_3_1/pallas_call | solution.py:358
Async XLA Ops:
  7.0 9.2 %collective-permute-start.1 = (bf16[112,1024]{1,0:T(8,128)(2,1)S(1)}, bf16[112,1024]{1,0:T(8,128)(2,1)S(1)}, u32[]{:S(2)}, u32[]{:S(2)}) collective-permute-start(bf16[112,1024]{1,0:T(8,128)(2,1)S(1)} %get-tuple-element.46), channel_id=1, source_target_pairs={{0,1},{1,2},{2,3},{3,4},{4,5},{5,6},{6,7},{7,8},{8,9},{9,10},{10,1... | collective-permute-start | bytes 688136 | tf_op jit(solution)/shard_map/ppermute | solution.py:285
  10.8 8.4 %collective-permute-start = (bf16[96,1024]{1,0:T(8,128)(2,1)S(1)}, bf16[96,1024]{1,0:T(8,128)(2,1)S(1)}, u32[]{:S(2)}, u32[]{:S(2)}) collective-permute-start(bf16[96,1024]{1,0:T(8,128)(2,1)S(1)} %get-tuple-element.45), channel_id=1, source_target_pairs={{0,1},{1,2},{2,3},{3,4},{4,5},{5,6},{6,7},{7,8},{8,9},{9,10},{10,1... | collective-permute-start | bytes 589832 | tf_op jit(solution)/shard_map/ppermute | solution.py:285
  19.2 8.2 %collective-permute-start.3 = (bf16[112,1024]{1,0:T(8,128)(2,1)S(1)}, bf16[112,1024]{1,0:T(8,128)(2,1)S(1)}, u32[]{:S(2)}, u32[]{:S(2)}) collective-permute-start(bf16[112,1024]{1,0:T(8,128)(2,1)S(1)} %get-tuple-element.53), channel_id=1, source_target_pairs={{0,1},{1,2},{2,3},{3,4},{4,5},{5,6},{6,7},{7,8},{8,9},{9,10},{10,1... | collective-permute-start | bytes 688136 | tf_op jit(solution)/shard_map/ppermute | solution.py:285
  22.5 7.8 %collective-permute-start.2 = (bf16[96,1024]{1,0:T(8,128)(2,1)S(1)}, bf16[96,1024]{1,0:T(8,128)(2,1)S(1)}, u32[]{:S(2)}, u32[]{:S(2)}) collective-permute-start(bf16[96,1024]{1,0:T(8,128)(2,1)S(1)} %get-tuple-element.52), channel_id=1, source_target_pairs={{0,1},{1,2},{2,3},{3,4},{4,5},{5,6},{6,7},{7,8},{8,9},{9,10},{10,1... | collective-permute-start | bytes 589832 | tf_op jit(solution)/shard_map/ppermute | solution.py:285
  30.3 8.2 %collective-permute-start.5 = (bf16[112,1024]{1,0:T(8,128)(2,1)S(1)}, bf16[112,1024]{1,0:T(8,128)(2,1)S(1)}, u32[]{:S(2)}, u32[]{:S(2)}) collective-permute-start(bf16[112,1024]{1,0:T(8,128)(2,1)S(1)} %get-tuple-element.59), channel_id=1, source_target_pairs={{0,1},{1,2},{2,3},{3,4},{4,5},{5,6},{6,7},{7,8},{8,9},{9,10},{10,1... | collective-permute-start | bytes 688136 | tf_op jit(solution)/shard_map/ppermute | solution.py:285
  33.7 7.8 %collective-permute-start.4 = (bf16[96,1024]{1,0:T(8,128)(2,1)S(1)}, bf16[96,1024]{1,0:T(8,128)(2,1)S(1)}, u32[]{:S(2)}, u32[]{:S(2)}) collective-permute-start(bf16[96,1024]{1,0:T(8,128)(2,1)S(1)} %get-tuple-element.58), channel_id=1, source_target_pairs={{0,1},{1,2},{2,3},{3,4},{4,5},{5,6},{6,7},{7,8},{8,9},{9,10},{10,1... | collective-permute-start | bytes 589832 | tf_op jit(solution)/shard_map/ppermute | solution.py:285

commit v10 on v9

--- a/solution.py
+++ b/solution.py
@@ -64,27 +64,27 @@
     return values * cosine + pltpu.roll(values, HD // 2, 1) * sine
 
 
-def layer(x, gain, weights, wait, cos_rows, bias_rows, kept_keys, kept_values, k_ref, v_ref, mixed_ref, write):
+def layer(x, gain, weights, wait, prepare, kept_keys, kept_values, k_ref, v_ref, mixed_ref, write):
     size, model = x.shape
     wq_ref, wk_ref, wv_ref, wo_ref = weights
     scale = lax.rsqrt(jnp.mean(x * x, axis=1, keepdims=True) + 1e-05) * (1.0 / LIFT)
     lifted = (x * gain).astype(BF16)
+    for start in range(0, KV_WIDTH, PAIR):
+        wait("v", start)
+        got = jnp.dot(lifted, wv_ref[:, start : start + PAIR], preferred_element_type=F32)
+        v_ref[:, start : start + PAIR] = (got * scale).astype(BF16)
+    cos_rows, bias_rows = prepare()
     cosine = cos_rows[:, :HD] * scale
     sine = cos_rows[:, HD:] * scale
     factor = HD ** (-0.5) * np.log2(np.e)
     cosine_q = cosine * factor
     sine_q = sine * factor
-
     for start in range(0, KV_WIDTH, PAIR):
         wait("k", start)
         got = jnp.dot(lifted, wk_ref[:, start : start + PAIR], preferred_element_type=F32)
         for half in range(0, PAIR, HD):
             turned = rotated(got[:, half : half + HD], cosine, sine)
             k_ref[:, start + half : start + half + HD] = turned.astype(BF16)
-    for start in range(0, KV_WIDTH, PAIR):
-        wait("v", start)
-        got = jnp.dot(lifted, wv_ref[:, start : start + PAIR], preferred_element_type=F32)
-        v_ref[:, start : start + PAIR] = (got * scale).astype(BF16)
     queries = []
     for start in range(0, Q_WIDTH, PAIR):
         wait("q", start)
@@ -173,19 +173,19 @@
     model, half = wk_ref.shape[0], Q_WIDTH // 2
     narrow, wide = slice(0, KV_WIDTH), slice(0, Q_WIDTH)
     batches = [
+        batch(wv_hbm, wv_ref, slice(0, model), narrow),
         batch(wk_hbm, wk_ref, slice(0, model), narrow),
-        batch(wv_hbm, wv_ref, slice(0, model), narrow),
         batch(wq_hbm, wq_ref, slice(0, model // 2), wide),
         batch(wq_hbm, wq_ref, slice(model // 2, model), wide),
         batch(wo_hbm, wo_ref, slice(0, half), slice(0, model)),
         batch(wo_hbm, wo_ref, slice(half, Q_WIDTH), slice(0, model)),
     ]
-    arrivals = {("k", 0): (0,), ("v", 0): (1,), ("q", 0): (2, 3), ("o", 0): (4, 5)}
+    arrivals = {("v", 0): (0,), ("k", 0): (1,), ("q", 0): (2, 3), ("o", 0): (4, 5)}
 
     def begin(index):
         if index < len(batches):
-            for copy in batches[index]:
-                copy.start()
+            for place, copy in enumerate(batches[index]):
+                copy.start(priority=place % 2)
         if index == len(batches):
             for copy in late:
                 copy.start()
@@ -194,11 +194,11 @@
         for index in arrivals.get((name, start), ()):
             for copy in batches[index]:
                 copy.wait()
-            begin(index + 3)
+            begin(index + 4)
 
     for copy in small:
         copy.start()
-    for index in range(3):
+    for index in range(4):
         begin(index)
     for copy in small:
         copy.wait()
@@ -215,7 +215,7 @@
 
     layer(
         x_ref[...].astype(F32), gain_ref[...], (wq_ref, wk_ref, wv_ref, wo_ref), wait,
-        cos_ref[:size, :], bias_ref[:size, :size], [], [], k_ref, v_ref, mixed_ref, write,
+        lambda: (cos_ref[:size, :], bias_ref[:size, :size]), [], [], k_ref, v_ref, mixed_ref, write,
     )
     for copy in late:
         copy.wait()
@@ -229,9 +229,6 @@
     if index == 0:
         table_ref = refs.pop(0)
         out_ref, k_ref, v_ref, cos_ref, bias_ref = refs
-        factors, bias = tables_of(x_ref[size:, : CHUNKS * size].astype(F32)[:1], table_ref[...])
-        cos_ref[...] = factors
-        bias_ref[...] = bias
         if not last:
             out_ref[size:, :] = x_ref[size:, :]
         keys, values = [], []
@@ -249,13 +246,20 @@
         else:
             out_ref, k_ref, v_ref = refs
 
+    def prepare():
+        if index:
+            return cos_ref[low:high, :], bias_ref[low:high, :]
+        factors, bias = tables_of(x_ref[size:, : CHUNKS * size].astype(F32)[:1], table_ref[...])
+        cos_ref[...] = factors
+        bias_ref[...] = bias
+        return factors[:size], bias[:size, :size]
+
     def write(start, result):
         out_ref[:size, start : start + PAIR] = result.astype(BF16)
 
     layer(
         x_ref[:size, :].astype(F32), gain_ref[...], (wq_ref, wk_ref, wv_ref, wo_ref), lambda name, start: None,
-        cos_ref[low:high, :], bias_ref[low:high, :] if index else bias_ref[:size, :size],
-        keys, values, k_ref, v_ref, mixed_ref, write,
+        prepare, keys, values, k_ref, v_ref, mixed_ref, write,
     )
     if last and index == CHUNKS - 1:
         copy = pltpu.make_async_copy(out_ref, whole_ref.at[0, low:high], sems.at[index])

time: 45.3 us -> 44.5 us (0.982)
  Pallas kernels: 29.2 us -> 28.1 us
    pallas_call x1, Pallas kernels: 6.98 us -> 6.3 us  [body(): pl.pallas_call(functools.partial(opening_kernel, size), out_shape=(kept((...]
  transfers between devices with their start and end apart: 6 -> 6, of which waited for: 3 -> 6; matrix products, arithmetic and copies ran while one was open for 0% -> 0% of each run, Pallas kernels for 42% -> 41%
where the time goes in v10:
time: 44.5 us; the launch traced here: 44.3 us
  Pallas kernels  28.1 us (63%)
  waiting for transfers between devices  12.8 us (29%)
  starting transfers between devices  3.26 us (7%)
    pallas_call x7, Pallas kernels, body(): pl.pallas_call(functools.partial(chunk_kernel, index, last), out_shape=tu...  21.8 us
    ppermute x6, waiting for transfers between devices, passed_along(): lax.ppermute(array, 'section', [(i, (i + by) % length) for i in range(len...  12.8 us
    pallas_call x1, Pallas kernels, body(): pl.pallas_call(functools.partial(opening_kernel, size), out_shape=(kept((...  6.3 us
    ppermute x6, starting transfers between devices, passed_along(): lax.ppermute(array, 'section', [(i, (i + by) % length) for i in range(len...  3.26 us
  transfers between devices with their start and end apart: 6, of which 6 were waited for; matrix products, arithmetic and copies ran while one was open for 0% of the time, Pallas kernels for 41%

profile of v10, /device:TPU:0, one launch (start us, length us, event | category | flops | bytes accessed | tf_op | source)
XLA Modules:
  0.0 44.3 jit_solution(12946338939908543009)
XLA Ops:
  0.0 6.3 %opening.1 = (bf16[112,1024]{1,0:T(8,128)(2,1)S(1)}, bf16[96,1024]{1,0:T(8,128)(2,1)S(1)}, bf16[96,1024]{1,0:T(8,128)(2,1)S(1)}, f32[192,256]{1,0:T(8,128)S(1)},...) custom-call(bf16[1,192,1024]{2,1,0:T(8,128)(2,1)} %x_hbm.1, ...), custom_call_target="tpu_custom_call" | custom-call | tf_op jit(solution)/shard_map/opening/pallas_call | solution.py:302
  6.3 0.5 %collective-permute-start.1 = (bf16[112,1024]{1,0:T(8,128)(2,1)S(1)}, bf16[112,1024]{1,0:T(8,128)(2,1)S(1)}, u32[]{:S(2)}, u32[]{:S(2)}) collective-permute-start(bf16[112,1024]{1,0:T(8,128)(2,1)S(1)} %get-tuple-element.46), channel_id=1, source_target_pairs={{0,1},{1,2},{2,3},{3,4},{4,5},{5,6},{6,7},{7,8},{8,9},{9,10},{10,1... | collective-permute-start | bytes 688136 | tf_op jit(solution)/shard_map/ppermute | solution.py:289
  6.8 3.3 %chunk_0_1.1 = (bf16[96,1024]{1,0:T(8,128)(2,1)S(1)}, bf16[96,1024]{1,0:T(8,128)(2,1)}, bf16[96,1024]{1,0:T(8,128)(2,1)}) custom-call(bf16[96,1024]{1,0:T(8,128)(2,1)S(1)} %get-tuple-element.35.x_ref, f32[1,1024]{1,0:T(1,128)S(1)} %get-tuple-element.36.gain_ref, bf16[1024,2048]{1,0:T(8,128)(2,1)S(1)} %get-tuple-element.37.wq_ref, ...), custom_call_target="tpu_custom_call" | custom-call | tf_op jit(solution)/shard_map/chunk_0_1/pallas_call | solution.py:362
  10.1 2.6 %collective-permute-start = (bf16[96,1024]{1,0:T(8,128)(2,1)S(1)}, bf16[96,1024]{1,0:T(8,128)(2,1)S(1)}, u32[]{:S(2)}, u32[]{:S(2)}) collective-permute-start(bf16[96,1024]{1,0:T(8,128)(2,1)S(1)} %get-tuple-element.45), channel_id=1, source_target_pairs={{0,1},{1,2},{2,3},{3,4},{4,5},{5,6},{6,7},{7,8},{8,9},{9,10},{10,1... | collective-permute-start | bytes 589832 | tf_op jit(solution)/shard_map/ppermute | solution.py:289
  12.8 2.8 %collective-permute-done.1.x_ref = bf16[112,1024]{1,0:T(8,128)(2,1)S(1)} collective-permute-done((bf16[112,1024]{1,0:T(8,128)(2,1)S(1)}, bf16[112,1024]{1,0:T(8,128)(2,1)S(1)}, u32[]{:S(2)}, u32[]{:S(2)}) %collective-permute-start.1) | collective-permute-done | bytes 229408 | tf_op jit(solution)/shard_map/ppermute | solution.py:289
  15.5 2.8 %chunk_1_0.1 = (bf16[112,1024]{1,0:T(8,128)(2,1)S(1)}, bf16[96,1024]{1,0:T(8,128)(2,1)S(1)}, bf16[96,1024]{1,0:T(8,128)(2,1)S(1)}, f32[192,256]{1,0:T(8,128)S(1)}, f32[192,128]{1,0:T(8,128)S(1)}) custom-call(bf16[112,1024]{1,0:T(8,128)(2,1)S(1)} %collective-permute-done.1.x_ref, f32[1,1024]{1,0:T(1,128)S(1)} %get-tuple-element.36.gain_ref, ...), custom_call_target="tpu_custom_call" | custom-call | tf_op jit(solution)/shard_map/chunk_1_0/pallas_call | solution.py:362
  18.3 0.1 collective-permute-start.3
  18.4 0.1 collective-permute-done.x_ref
  18.5 3.3 %chunk_1_1.1 = (bf16[96,1024]{1,0:T(8,128)(2,1)S(1)}, bf16[96,1024]{1,0:T(8,128)(2,1)}, bf16[96,1024]{1,0:T(8,128)(2,1)}) custom-call(bf16[96,1024]{1,0:T(8,128)(2,1)S(1)} %collective-permute-done.x_ref, f32[1,1024]{1,0:T(1,128)S(1)} %get-tuple-element.36.gain_ref, bf16[1024,2048]{1,0:T(8,128)(2,1)S(1)} %get-tuple-element.37.wq_ref, ...), custom_call_target="tpu_custom_call" | custom-call | tf_op jit(solution)/shard_map/chunk_1_1/pallas_call | solution.py:362
  21.8 0.0 collective-permute-start.2
  21.8 4.7 %collective-permute-done.3.x_ref = bf16[112,1024]{1,0:T(8,128)(2,1)S(1)} collective-permute-done((bf16[112,1024]{1,0:T(8,128)(2,1)S(1)}, bf16[112,1024]{1,0:T(8,128)(2,1)S(1)}, u32[]{:S(2)}, u32[]{:S(2)}) %collective-permute-start.3) | collective-permute-done | bytes 229408 | tf_op jit(solution)/shard_map/ppermute | solution.py:289
  26.5 2.8 %chunk_2_0.1 = (bf16[112,1024]{1,0:T(8,128)(2,1)S(1)}, bf16[96,1024]{1,0:T(8,128)(2,1)S(1)}, bf16[96,1024]{1,0:T(8,128)(2,1)S(1)}, f32[192,256]{1,0:T(8,128)S(1)}, f32[192,128]{1,0:T(8,128)S(1)}) custom-call(bf16[112,1024]{1,0:T(8,128)(2,1)S(1)} %collective-permute-done.3.x_ref, f32[1,1024]{1,0:T(1,128)S(1)} %get-tuple-element.36.gain_ref, ...), custom_call_target="tpu_custom_call" | custom-call | tf_op jit(solution)/shard_map/chunk_2_0/pallas_call | solution.py:362
  29.3 0.1 collective-permute-start.5
  29.4 0.2 collective-permute-done.2.x_ref
  29.6 3.3 %chunk_2_1.1 = (bf16[96,1024]{1,0:T(8,128)(2,1)S(1)}, bf16[96,1024]{1,0:T(8,128)(2,1)}, bf16[96,1024]{1,0:T(8,128)(2,1)}) custom-call(bf16[96,1024]{1,0:T(8,128)(2,1)S(1)} %collective-permute-done.2.x_ref, f32[1,1024]{1,0:T(1,128)S(1)} %get-tuple-element.36.gain_ref, bf16[1024,2048]{1,0:T(8,128)(2,1)S(1)} %get-tuple-element.37.wq_ref, ...), custom_call_target="tpu_custom_call" | custom-call | tf_op jit(solution)/shard_map/chunk_2_1/pallas_call | solution.py:362
  32.9 0.0 collective-permute-start.4
  32.9 4.6 %collective-permute-done.5.x_ref = bf16[112,1024]{1,0:T(8,128)(2,1)S(1)} collective-permute-done((bf16[112,1024]{1,0:T(8,128)(2,1)S(1)}, bf16[112,1024]{1,0:T(8,128)(2,1)S(1)}, u32[]{:S(2)}, u32[]{:S(2)}) %collective-permute-start.5) | collective-permute-done | bytes 229408 | tf_op jit(solution)/shard_map/ppermute | solution.py:289
  37.5 2.8 %chunk_3_0.1 = (bf16[112,1024]{1,0:T(8,128)(2,1)S(1)}, bf16[96,1024]{1,0:T(8,128)(2,1)S(1)}, bf16[96,1024]{1,0:T(8,128)(2,1)S(1)}, f32[192,256]{1,0:T(8,128)S(1)}, f32[192,128]{1,0:T(8,128)S(1)}) custom-call(bf16[112,1024]{1,0:T(8,128)(2,1)S(1)} %collective-permute-done.5.x_ref, f32[1,1024]{1,0:T(1,128)S(1)} %get-tuple-element.36.gain_ref, ...), custom_call_target="tpu_custom_call" | custom-call | tf_op jit(solution)/shard_map/chunk_3_0/pallas_call | solution.py:362
  40.3 0.4 collective-permute-done.4.x_ref
  40.7 3.5 %chunk_3_1.1 = bf16[1,192,1024]{2,1,0:T(8,128)(2,1)} custom-call(bf16[96,1024]{1,0:T(8,128)(2,1)S(1)} %collective-permute-done.4.x_ref, f32[1,1024]{1,0:T(1,128)S(1)} %get-tuple-element.36.gain_ref, bf16[1024,2048]{1,0:T(8,128)(2,1)S(1)} %get-tuple-element.37.wq_ref, bf16[1024,1024]{1,0:T(8,128)(2,1)S(1)} %get-tuple-element.38.wk_ref, ...), custom_call_target="tpu_custom_call" | custom-call | tf_op jit(solution)/shard_map/chunk_3_1/pallas_call | solution.py:362
Async XLA Ops:
  6.3 9.2 %collective-permute-start.1 = (bf16[112,1024]{1,0:T(8,128)(2,1)S(1)}, bf16[112,1024]{1,0:T(8,128)(2,1)S(1)}, u32[]{:S(2)}, u32[]{:S(2)}) collective-permute-start(bf16[112,1024]{1,0:T(8,128)(2,1)S(1)} %get-tuple-element.46), channel_id=1, source_target_pairs={{0,1},{1,2},{2,3},{3,4},{4,5},{5,6},{6,7},{7,8},{8,9},{9,10},{10,1... | collective-permute-start | bytes 688136 | tf_op jit(solution)/shard_map/ppermute | solution.py:289
  10.1 8.4 %collective-permute-start = (bf16[96,1024]{1,0:T(8,128)(2,1)S(1)}, bf16[96,1024]{1,0:T(8,128)(2,1)S(1)}, u32[]{:S(2)}, u32[]{:S(2)}) collective-permute-start(bf16[96,1024]{1,0:T(8,128)(2,1)S(1)} %get-tuple-element.45), channel_id=1, source_target_pairs={{0,1},{1,2},{2,3},{3,4},{4,5},{5,6},{6,7},{7,8},{8,9},{9,10},{10,1... | collective-permute-start | bytes 589832 | tf_op jit(solution)/shard_map/ppermute | solution.py:289
  18.3 8.2 %collective-permute-start.3 = (bf16[112,1024]{1,0:T(8,128)(2,1)S(1)}, bf16[112,1024]{1,0:T(8,128)(2,1)S(1)}, u32[]{:S(2)}, u32[]{:S(2)}) collective-permute-start(bf16[112,1024]{1,0:T(8,128)(2,1)S(1)} %get-tuple-element.53), channel_id=1, source_target_pairs={{0,1},{1,2},{2,3},{3,4},{4,5},{5,6},{6,7},{7,8},{8,9},{9,10},{10,1... | collective-permute-start | bytes 688136 | tf_op jit(solution)/shard_map/ppermute | solution.py:289
  21.8 7.8 %collective-permute-start.2 = (bf16[96,1024]{1,0:T(8,128)(2,1)S(1)}, bf16[96,1024]{1,0:T(8,128)(2,1)S(1)}, u32[]{:S(2)}, u32[]{:S(2)}) collective-permute-start(bf16[96,1024]{1,0:T(8,128)(2,1)S(1)} %get-tuple-element.52), channel_id=1, source_target_pairs={{0,1},{1,2},{2,3},{3,4},{4,5},{5,6},{6,7},{7,8},{8,9},{9,10},{10,1... | collective-permute-start | bytes 589832 | tf_op jit(solution)/shard_map/ppermute | solution.py:289
  29.3 8.2 %collective-permute-start.5 = (bf16[112,1024]{1,0:T(8,128)(2,1)S(1)}, bf16[112,1024]{1,0:T(8,128)(2,1)S(1)}, u32[]{:S(2)}, u32[]{:S(2)}) collective-permute-start(bf16[112,1024]{1,0:T(8,128)(2,1)S(1)} %get-tuple-element.59), channel_id=1, source_target_pairs={{0,1},{1,2},{2,3},{3,4},{4,5},{5,6},{6,7},{7,8},{8,9},{9,10},{10,1... | collective-permute-start | bytes 688136 | tf_op jit(solution)/shard_map/ppermute | solution.py:289
  32.9 7.8 %collective-permute-start.4 = (bf16[96,1024]{1,0:T(8,128)(2,1)S(1)}, bf16[96,1024]{1,0:T(8,128)(2,1)S(1)}, u32[]{:S(2)}, u32[]{:S(2)}) collective-permute-start(bf16[96,1024]{1,0:T(8,128)(2,1)S(1)} %get-tuple-element.58), channel_id=1, source_target_pairs={{0,1},{1,2},{2,3},{3,4},{4,5},{5,6},{6,7},{7,8},{8,9},{9,10},{10,1... | collective-permute-start | bytes 589832 | tf_op jit(solution)/shard_map/ppermute | solution.py:289

commit v11 on v10

--- a/solution.py
+++ b/solution.py
@@ -85,18 +85,10 @@
         for half in range(0, PAIR, HD):
             turned = rotated(got[:, half : half + HD], cosine, sine)
             k_ref[:, start + half : start + half + HD] = turned.astype(BF16)
-    queries = []
-    for start in range(0, Q_WIDTH, PAIR):
-        wait("q", start)
-        got = jnp.dot(lifted, wq_ref[:, start : start + PAIR], preferred_element_type=F32)
-        upper = rotated(got[:, :HD], cosine_q, sine_q)
-        lower = rotated(got[:, HD:], cosine_q, sine_q)
-        queries.append(jnp.concatenate([upper, lower], axis=0).astype(BF16))
-
-    groups = range(KV_HEADS)
     spare = jnp.zeros((HD - size, HD), BF16)
     lower = lower_triangle(size, HD)
     lower_share = jnp.where(lower, 1.0, 0.0).astype(BF16)
+    key_refs, value_refs = [k_ref, *kept_keys], [v_ref, *kept_values]
 
     def rows_of(refs, group):
         lanes = slice(group * HD, (group + 1) * HD)
@@ -104,37 +96,64 @@
             return refs[0][:, lanes]
         return jnp.concatenate([part for ref in refs for part in (ref[:, lanes], spare)], axis=0)
 
-    key_refs, value_refs = [k_ref, *kept_keys], [v_ref, *kept_values]
-    scores = []
-    for group in groups:
+    def query(group):
+        lanes = slice(group * PAIR, (group + 1) * PAIR)
+        wait("q", group)
+        got = jnp.dot(lifted, wq_ref[:, lanes], preferred_element_type=F32)
+        turned = [rotated(got[:, half : half + HD], cosine_q, sine_q) for half in range(0, PAIR, HD)]
+        return jnp.concatenate(turned, axis=0).astype(BF16)
+
+    def score(group, queries):
         key_rows = rows_of(key_refs, group)
-        got = lax.dot_general(queries[group], key_rows, (((1,), (1,)), ((), ())), preferred_element_type=F32)
+        got = lax.dot_general(queries, key_rows, (((1,), (1,)), ((), ())), preferred_element_type=F32)
         got = got.reshape(2, size, key_rows.shape[0])
         if kept_keys:
             got = jnp.where(lower[None], got[:, :, :HD], got[:, :, HD:])
-        scores.append(got + bias_rows[None])
-    most = [jnp.max(part, axis=2, keepdims=True) for part in scores]
-    expo = [jnp.exp2(scores[g] - most[g]).astype(BF16) for g in groups]
-    if kept_keys:
-        own = [part * lower_share[None] for part in expo]
-        expo = [jnp.concatenate([mine, part - mine], axis=2) for mine, part in zip(own, expo)]
-    got = []
-    for group in groups:
-        value_rows = rows_of(value_refs, group)
-        value_rows = jnp.concatenate([value_rows, jnp.ones((value_rows.shape[0], HD), BF16)], axis=1)
-        part = expo[group].reshape(2 * size, value_rows.shape[0])
-        got.append(jnp.dot(part, value_rows, preferred_element_type=F32))
-    for group in groups:
-        total = got[group][:, HD:]
-        inverse = pl.reciprocal(total, approx=True)
-        inverse = inverse * (2.0 - total * inverse)
-        mixed = (got[group][:, :HD] * inverse).astype(BF16)
-        mixed_ref[:, group * PAIR : group * PAIR + HD] = mixed[:size]
-        mixed_ref[:, group * PAIR + HD : (group + 1) * PAIR] = mixed[size:]
-    for start in range(0, model, PAIR):
-        wait("o", start)
-        update = jnp.dot(mixed_ref[...], wo_ref[:, start : start + PAIR], preferred_element_type=F32)
-        write(start, x[:, start : start + PAIR] + update)
+        return got + bias_rows[None]
+
+    def exponents(scores):
+        most = [jnp.max(part, axis=2, keepdims=True) for part in scores]
+        expo = [jnp.exp2(part - peak).astype(BF16) for part, peak in zip(scores, most)]
+        if kept_keys:
+            own = [part * lower_share[None] for part in expo]
+            expo = [jnp.concatenate([mine, part - mine], axis=2) for mine, part in zip(own, expo)]
+        return expo
+
+    def mix(groups, expo):
+        got = []
+        for group, part in zip(groups, expo):
+            value_rows = rows_of(value_refs, group)
+            value_rows = jnp.concatenate([value_rows, jnp.ones((value_rows.shape[0], HD), BF16)], axis=1)
+            part = part.reshape(2 * size, value_rows.shape[0])
+            got.append(jnp.dot(part, value_rows, preferred_element_type=F32))
+        for group, part in zip(groups, got):
+            total = part[:, HD:]
+            inverse = pl.reciprocal(total, approx=True)
+            inverse = inverse * (2.0 - total * inverse)
+            mixed = (part[:, :HD] * inverse).astype(BF16)
+            mixed_ref[:, group * PAIR : group * PAIR + HD] = mixed[:size]
+            mixed_ref[:, group * PAIR + HD : (group + 1) * PAIR] = mixed[size:]
+
+    def products(half):
+        rows = slice(half * Q_WIDTH // 2, (half + 1) * Q_WIDTH // 2)
+        wait("o", half)
+        return [
+            jnp.dot(mixed_ref[:, rows], wo_ref[rows, start : start + PAIR], preferred_element_type=F32)
+            for start in range(0, model, PAIR)
+        ]
+
+    early, late = range(KV_HEADS // 2), range(KV_HEADS // 2, KV_HEADS)
+    queries = [query(group) for group in early]
+    scores = [score(group, part) for group, part in zip(early, queries)]
+    queries = [query(group) for group in late]
+    expo = exponents(scores)
+    scores = [score(group, part) for group, part in zip(late, queries)]
+    mix(early, expo)
+    updates = products(0)
+    expo = exponents(scores)
+    mix(late, expo)
+    for start, first, second in zip(range(0, model, PAIR), updates, products(1)):
+        write(start, x[:, start : start + PAIR] + (first + second))
 
 
 def write_ids(ids_row, out_ref, size):
@@ -180,7 +199,7 @@
         batch(wo_hbm, wo_ref, slice(0, half), slice(0, model)),
         batch(wo_hbm, wo_ref, slice(half, Q_WIDTH), slice(0, model)),
     ]
-    arrivals = {("v", 0): (0,), ("k", 0): (1,), ("q", 0): (2, 3), ("o", 0): (4, 5)}
+    arrivals = {("v", 0): (0,), ("k", 0): (1,), ("q", 0): (2, 3), ("o", 0): (4,), ("o", 1): (5,)}
 
     def begin(index):
         if index < len(batches):
@@ -194,11 +213,11 @@
         for index in arrivals.get((name, start), ()):
             for copy in batches[index]:
                 copy.wait()
-            begin(index + 4)
+            begin(index + 6)
 
     for copy in small:
         copy.start()
-    for index in range(4):
+    for index in range(6):
         begin(index)
     for copy in small:
         copy.wait()

time: 44.5 us -> 45.7 us (1.027)
  Pallas kernels: 28.1 us -> 29 us
    pallas_call x1, Pallas kernels: 6.3 us -> 7.26 us  [body(): pl.pallas_call(functools.partial(opening_kernel, size), out_shape=(kept((...]
  transfers between devices with their start and end apart: 6 -> 6, of which waited for: 6 -> 3; matrix products, arithmetic and copies ran while one was open for 0% -> 0% of each run, Pallas kernels for 41% -> 39%
where the time goes in v11:
time: 45.7 us; the launch traced here: 45.5 us
  Pallas kernels  29 us (63%)
  waiting for transfers between devices  12.7 us (28%)
  starting transfers between devices  3.61 us (8%)
    pallas_call x7, Pallas kernels, body(): pl.pallas_call(functools.partial(chunk_kernel, index, last), out_shape=tu...  21.7 us
    ppermute x6, waiting for transfers between devices, passed_along(): lax.ppermute(array, 'section', [(i, (i + by) % length) for i in range(len...  12.7 us
    pallas_call x1, Pallas kernels, body(): pl.pallas_call(functools.partial(opening_kernel, size), out_shape=(kept((...  7.26 us
    ppermute x6, starting transfers between devices, passed_along(): lax.ppermute(array, 'section', [(i, (i + by) % length) for i in range(len...  3.61 us
  transfers between devices with their start and end apart: 6, of which 3 were waited for; matrix products, arithmetic and copies ran while one was open for 0% of the time, Pallas kernels for 39%

profile of v11, /device:TPU:0, one launch (start us, length us, event | category | flops | bytes accessed | tf_op | source)
XLA Modules:
  0.0 45.5 jit_solution(609591365466561167)
XLA Ops:
  0.0 7.3 %opening.1 = (bf16[112,1024]{1,0:T(8,128)(2,1)S(1)}, bf16[96,1024]{1,0:T(8,128)(2,1)S(1)}, bf16[96,1024]{1,0:T(8,128)(2,1)S(1)}, f32[192,256]{1,0:T(8,128)S(1)},...) custom-call(bf16[1,192,1024]{2,1,0:T(8,128)(2,1)} %x_hbm.1, ...), custom_call_target="tpu_custom_call" | custom-call | tf_op jit(solution)/shard_map/opening/pallas_call | solution.py:321
  7.3 0.5 %collective-permute-start.1 = (bf16[112,1024]{1,0:T(8,128)(2,1)S(1)}, bf16[112,1024]{1,0:T(8,128)(2,1)S(1)}, u32[]{:S(2)}, u32[]{:S(2)}) collective-permute-start(bf16[112,1024]{1,0:T(8,128)(2,1)S(1)} %get-tuple-element.46), channel_id=1, source_target_pairs={{0,1},{1,2},{2,3},{3,4},{4,5},{5,6},{6,7},{7,8},{8,9},{9,10},{10,1... | collective-permute-start | bytes 688136 | tf_op jit(solution)/shard_map/ppermute | solution.py:308
  7.8 3.1 %chunk_0_1.1 = (bf16[96,1024]{1,0:T(8,128)(2,1)S(1)}, bf16[96,1024]{1,0:T(8,128)(2,1)}, bf16[96,1024]{1,0:T(8,128)(2,1)}) custom-call(bf16[96,1024]{1,0:T(8,128)(2,1)S(1)} %get-tuple-element.35.x_ref, f32[1,1024]{1,0:T(1,128)S(1)} %get-tuple-element.36.gain_ref, bf16[1024,2048]{1,0:T(8,128)(2,1)S(1)} %get-tuple-element.37.wq_ref, ...), custom_call_target="tpu_custom_call" | custom-call | tf_op jit(solution)/shard_map/chunk_0_1/pallas_call | solution.py:381
  10.9 2.7 %collective-permute-start = (bf16[96,1024]{1,0:T(8,128)(2,1)S(1)}, bf16[96,1024]{1,0:T(8,128)(2,1)S(1)}, u32[]{:S(2)}, u32[]{:S(2)}) collective-permute-start(bf16[96,1024]{1,0:T(8,128)(2,1)S(1)} %get-tuple-element.45), channel_id=1, source_target_pairs={{0,1},{1,2},{2,3},{3,4},{4,5},{5,6},{6,7},{7,8},{8,9},{9,10},{10,1... | collective-permute-start | bytes 589832 | tf_op jit(solution)/shard_map/ppermute | solution.py:308
  13.6 2.9 %collective-permute-done.1.x_ref = bf16[112,1024]{1,0:T(8,128)(2,1)S(1)} collective-permute-done((bf16[112,1024]{1,0:T(8,128)(2,1)S(1)}, bf16[112,1024]{1,0:T(8,128)(2,1)S(1)}, u32[]{:S(2)}, u32[]{:S(2)}) %collective-permute-start.1) | collective-permute-done | bytes 229408 | tf_op jit(solution)/shard_map/ppermute | solution.py:308
  16.5 2.9 %chunk_1_0.1 = (bf16[112,1024]{1,0:T(8,128)(2,1)S(1)}, bf16[96,1024]{1,0:T(8,128)(2,1)S(1)}, bf16[96,1024]{1,0:T(8,128)(2,1)S(1)}, f32[192,256]{1,0:T(8,128)S(1)}, f32[192,128]{1,0:T(8,128)S(1)}) custom-call(bf16[112,1024]{1,0:T(8,128)(2,1)S(1)} %collective-permute-done.1.x_ref, f32[1,1024]{1,0:T(1,128)S(1)} %get-tuple-element.36.gain_ref, ...), custom_call_target="tpu_custom_call" | custom-call | tf_op jit(solution)/shard_map/chunk_1_0/pallas_call | solution.py:381
  19.4 0.1 collective-permute-start.3
  19.4 0.0 collective-permute-done.x_ref
  19.4 3.1 %chunk_1_1.1 = (bf16[96,1024]{1,0:T(8,128)(2,1)S(1)}, bf16[96,1024]{1,0:T(8,128)(2,1)}, bf16[96,1024]{1,0:T(8,128)(2,1)}) custom-call(bf16[96,1024]{1,0:T(8,128)(2,1)S(1)} %collective-permute-done.x_ref, f32[1,1024]{1,0:T(1,128)S(1)} %get-tuple-element.36.gain_ref, bf16[1024,2048]{1,0:T(8,128)(2,1)S(1)} %get-tuple-element.37.wq_ref, ...), custom_call_target="tpu_custom_call" | custom-call | tf_op jit(solution)/shard_map/chunk_1_1/pallas_call | solution.py:381
  22.5 0.2 collective-permute-start.2
  22.8 4.8 %collective-permute-done.3.x_ref = bf16[112,1024]{1,0:T(8,128)(2,1)S(1)} collective-permute-done((bf16[112,1024]{1,0:T(8,128)(2,1)S(1)}, bf16[112,1024]{1,0:T(8,128)(2,1)S(1)}, u32[]{:S(2)}, u32[]{:S(2)}) %collective-permute-start.3) | collective-permute-done | bytes 229408 | tf_op jit(solution)/shard_map/ppermute | solution.py:308
  27.6 2.9 %chunk_2_0.1 = (bf16[112,1024]{1,0:T(8,128)(2,1)S(1)}, bf16[96,1024]{1,0:T(8,128)(2,1)S(1)}, bf16[96,1024]{1,0:T(8,128)(2,1)S(1)}, f32[192,256]{1,0:T(8,128)S(1)}, f32[192,128]{1,0:T(8,128)S(1)}) custom-call(bf16[112,1024]{1,0:T(8,128)(2,1)S(1)} %collective-permute-done.3.x_ref, f32[1,1024]{1,0:T(1,128)S(1)} %get-tuple-element.36.gain_ref, ...), custom_call_target="tpu_custom_call" | custom-call | tf_op jit(solution)/shard_map/chunk_2_0/pallas_call | solution.py:381
  30.5 0.1 collective-permute-start.5
  30.5 0.0 collective-permute-done.2.x_ref
  30.6 3.1 %chunk_2_1.1 = (bf16[96,1024]{1,0:T(8,128)(2,1)S(1)}, bf16[96,1024]{1,0:T(8,128)(2,1)}, bf16[96,1024]{1,0:T(8,128)(2,1)}) custom-call(bf16[96,1024]{1,0:T(8,128)(2,1)S(1)} %collective-permute-done.2.x_ref, f32[1,1024]{1,0:T(1,128)S(1)} %get-tuple-element.36.gain_ref, bf16[1024,2048]{1,0:T(8,128)(2,1)S(1)} %get-tuple-element.37.wq_ref, ...), custom_call_target="tpu_custom_call" | custom-call | tf_op jit(solution)/shard_map/chunk_2_1/pallas_call | solution.py:381
  33.6 0.1 collective-permute-start.4
  33.7 4.9 %collective-permute-done.5.x_ref = bf16[112,1024]{1,0:T(8,128)(2,1)S(1)} collective-permute-done((bf16[112,1024]{1,0:T(8,128)(2,1)S(1)}, bf16[112,1024]{1,0:T(8,128)(2,1)S(1)}, u32[]{:S(2)}, u32[]{:S(2)}) %collective-permute-start.5) | collective-permute-done | bytes 229408 | tf_op jit(solution)/shard_map/ppermute | solution.py:308
  38.7 2.9 %chunk_3_0.1 = (bf16[112,1024]{1,0:T(8,128)(2,1)S(1)}, bf16[96,1024]{1,0:T(8,128)(2,1)S(1)}, bf16[96,1024]{1,0:T(8,128)(2,1)S(1)}, f32[192,256]{1,0:T(8,128)S(1)}, f32[192,128]{1,0:T(8,128)S(1)}) custom-call(bf16[112,1024]{1,0:T(8,128)(2,1)S(1)} %collective-permute-done.5.x_ref, f32[1,1024]{1,0:T(1,128)S(1)} %get-tuple-element.36.gain_ref, ...), custom_call_target="tpu_custom_call" | custom-call | tf_op jit(solution)/shard_map/chunk_3_0/pallas_call | solution.py:381
  41.6 0.0 collective-permute-done.4.x_ref
  41.6 3.8 %chunk_3_1.1 = bf16[1,192,1024]{2,1,0:T(8,128)(2,1)} custom-call(bf16[96,1024]{1,0:T(8,128)(2,1)S(1)} %collective-permute-done.4.x_ref, f32[1,1024]{1,0:T(1,128)S(1)} %get-tuple-element.36.gain_ref, bf16[1024,2048]{1,0:T(8,128)(2,1)S(1)} %get-tuple-element.37.wq_ref, bf16[1024,1024]{1,0:T(8,128)(2,1)S(1)} %get-tuple-element.38.wk_ref, ...), custom_call_target="tpu_custom_call" | custom-call | tf_op jit(solution)/shard_map/chunk_3_1/pallas_call | solution.py:381
Async XLA Ops:
  7.3 9.2 %collective-permute-start.1 = (bf16[112,1024]{1,0:T(8,128)(2,1)S(1)}, bf16[112,1024]{1,0:T(8,128)(2,1)S(1)}, u32[]{:S(2)}, u32[]{:S(2)}) collective-permute-start(bf16[112,1024]{1,0:T(8,128)(2,1)S(1)} %get-tuple-element.46), channel_id=1, source_target_pairs={{0,1},{1,2},{2,3},{3,4},{4,5},{5,6},{6,7},{7,8},{8,9},{9,10},{10,1... | collective-permute-start | bytes 688136 | tf_op jit(solution)/shard_map/ppermute | solution.py:308
  10.9 8.6 %collective-permute-start = (bf16[96,1024]{1,0:T(8,128)(2,1)S(1)}, bf16[96,1024]{1,0:T(8,128)(2,1)S(1)}, u32[]{:S(2)}, u32[]{:S(2)}) collective-permute-start(bf16[96,1024]{1,0:T(8,128)(2,1)S(1)} %get-tuple-element.45), channel_id=1, source_target_pairs={{0,1},{1,2},{2,3},{3,4},{4,5},{5,6},{6,7},{7,8},{8,9},{9,10},{10,1... | collective-permute-start | bytes 589832 | tf_op jit(solution)/shard_map/ppermute | solution.py:308
  19.4 8.2 %collective-permute-start.3 = (bf16[112,1024]{1,0:T(8,128)(2,1)S(1)}, bf16[112,1024]{1,0:T(8,128)(2,1)S(1)}, u32[]{:S(2)}, u32[]{:S(2)}) collective-permute-start(bf16[112,1024]{1,0:T(8,128)(2,1)S(1)} %get-tuple-element.53), channel_id=1, source_target_pairs={{0,1},{1,2},{2,3},{3,4},{4,5},{5,6},{6,7},{7,8},{8,9},{9,10},{10,1... | collective-permute-start | bytes 688136 | tf_op jit(solution)/shard_map/ppermute | solution.py:308
  22.5 8.0 %collective-permute-start.2 = (bf16[96,1024]{1,0:T(8,128)(2,1)S(1)}, bf16[96,1024]{1,0:T(8,128)(2,1)S(1)}, u32[]{:S(2)}, u32[]{:S(2)}) collective-permute-start(bf16[96,1024]{1,0:T(8,128)(2,1)S(1)} %get-tuple-element.52), channel_id=1, source_target_pairs={{0,1},{1,2},{2,3},{3,4},{4,5},{5,6},{6,7},{7,8},{8,9},{9,10},{10,1... | collective-permute-start | bytes 589832 | tf_op jit(solution)/shard_map/ppermute | solution.py:308
  30.5 8.2 %collective-permute-start.5 = (bf16[112,1024]{1,0:T(8,128)(2,1)S(1)}, bf16[112,1024]{1,0:T(8,128)(2,1)S(1)}, u32[]{:S(2)}, u32[]{:S(2)}) collective-permute-start(bf16[112,1024]{1,0:T(8,128)(2,1)S(1)} %get-tuple-element.59), channel_id=1, source_target_pairs={{0,1},{1,2},{2,3},{3,4},{4,5},{5,6},{6,7},{7,8},{8,9},{9,10},{10,1... | collective-permute-start | bytes 688136 | tf_op jit(solution)/shard_map/ppermute | solution.py:308
  33.6 7.9 %collective-permute-start.4 = (bf16[96,1024]{1,0:T(8,128)(2,1)S(1)}, bf16[96,1024]{1,0:T(8,128)(2,1)S(1)}, u32[]{:S(2)}, u32[]{:S(2)}) collective-permute-start(bf16[96,1024]{1,0:T(8,128)(2,1)S(1)} %get-tuple-element.58), channel_id=1, source_target_pairs={{0,1},{1,2},{2,3},{3,4},{4,5},{5,6},{6,7},{7,8},{8,9},{9,10},{10,1... | collective-permute-start | bytes 589832 | tf_op jit(solution)/shard_map/ppermute | solution.py:308

commit v12 on v11

--- a/solution.py
+++ b/solution.py
@@ -64,7 +64,7 @@
     return values * cosine + pltpu.roll(values, HD // 2, 1) * sine
 
 
-def layer(x, gain, weights, wait, prepare, kept_keys, kept_values, k_ref, v_ref, mixed_ref, write):
+def layer(halves, x, gain, weights, wait, prepare, kept_keys, kept_values, k_ref, v_ref, mixed_ref, write):
     size, model = x.shape
     wq_ref, wk_ref, wv_ref, wo_ref = weights
     scale = lax.rsqrt(jnp.mean(x * x, axis=1, keepdims=True) + 1e-05) * (1.0 / LIFT)
@@ -136,13 +136,22 @@
 
     def products(half):
         rows = slice(half * Q_WIDTH // 2, (half + 1) * Q_WIDTH // 2)
-        wait("o", half)
         return [
             jnp.dot(mixed_ref[:, rows], wo_ref[rows, start : start + PAIR], preferred_element_type=F32)
             for start in range(0, model, PAIR)
         ]
 
-    early, late = range(KV_HEADS // 2), range(KV_HEADS // 2, KV_HEADS)
+    groups = range(KV_HEADS)
+    if not halves:
+        queries = [query(group) for group in groups]
+        expo = exponents([score(group, part) for group, part in zip(groups, queries)])
+        mix(groups, expo)
+        for start in range(0, model, PAIR):
+            wait("o", start)
+            update = jnp.dot(mixed_ref[...], wo_ref[:, start : start + PAIR], preferred_element_type=F32)
+            write(start, x[:, start : start + PAIR] + update)
+        return
+    early, late = groups[: KV_HEADS // 2], groups[KV_HEADS // 2 :]
     queries = [query(group) for group in early]
     scores = [score(group, part) for group, part in zip(early, queries)]
     queries = [query(group) for group in late]
@@ -190,34 +199,34 @@
         return copies
 
     model, half = wk_ref.shape[0], Q_WIDTH // 2
-    narrow, wide = slice(0, KV_WIDTH), slice(0, Q_WIDTH)
+    narrow = slice(0, KV_WIDTH)
     batches = [
         batch(wv_hbm, wv_ref, slice(0, model), narrow),
         batch(wk_hbm, wk_ref, slice(0, model), narrow),
-        batch(wq_hbm, wq_ref, slice(0, model // 2), wide),
-        batch(wq_hbm, wq_ref, slice(model // 2, model), wide),
+        batch(wq_hbm, wq_ref, slice(0, model), slice(0, half)),
+        batch(wq_hbm, wq_ref, slice(0, model), slice(half, Q_WIDTH)),
         batch(wo_hbm, wo_ref, slice(0, half), slice(0, model)),
         batch(wo_hbm, wo_ref, slice(half, Q_WIDTH), slice(0, model)),
     ]
-    arrivals = {("v", 0): (0,), ("k", 0): (1,), ("q", 0): (2, 3), ("o", 0): (4,), ("o", 1): (5,)}
+    arrivals = {("v", 0): (0,), ("k", 0): (1,), ("q", 0): (2,), ("q", KV_HEADS // 2): (3,), ("o", 0): (4, 5)}
 
     def begin(index):
-        if index < len(batches):
-            for place, copy in enumerate(batches[index]):
-                copy.start(priority=place % 2)
-        if index == len(batches):
-            for copy in late:
-                copy.start()
-
-    def wait(name, start):
-        for index in arrivals.get((name, start), ()):
+        for place, copy in enumerate(batches[index]):
+            copy.start(priority=place % 2)
+
+    def wait(name, place):
+        for index in arrivals.get((name, place), ()):
             for copy in batches[index]:
                 copy.wait()
-            begin(index + 6)
+            if index in (1, 2):
+                begin(index + 3)
+            if index == 3:
+                for copy in late:
+                    copy.start()
 
     for copy in small:
         copy.start()
-    for index in range(6):
+    for index in range(4):
         begin(index)
     for copy in small:
         copy.wait()
@@ -233,7 +242,7 @@
         out_ref[:size, start : start + PAIR] = values.astype(BF16)
 
     layer(
-        x_ref[...].astype(F32), gain_ref[...], (wq_ref, wk_ref, wv_ref, wo_ref), wait,
+        False, x_ref[...].astype(F32), gain_ref[...], (wq_ref, wk_ref, wv_ref, wo_ref), wait,
         lambda: (cos_ref[:size, :], bias_ref[:size, :size]), [], [], k_ref, v_ref, mixed_ref, write,
     )
     for copy in late:
@@ -277,7 +286,7 @@
         out_ref[:size, start : start + PAIR] = result.astype(BF16)
 
     layer(
-        x_ref[:size, :].astype(F32), gain_ref[...], (wq_ref, wk_ref, wv_ref, wo_ref), lambda name, start: None,
+        index > 0 and not last, x_ref[:size, :].astype(F32), gain_ref[...], (wq_ref, wk_ref, wv_ref, wo_ref), lambda name, start: None,
         prepare, keys, values, k_ref, v_ref, mixed_ref, write,
     )
     if last and index == CHUNKS - 1:

time: 45.7 us -> 44.3 us (0.969)
  Pallas kernels: 29 us -> 27.5 us
    pallas_call x1, Pallas kernels: 7.26 us -> 6.38 us  [body(): pl.pallas_call(functools.partial(opening_kernel, size), out_shape=(kept((...]
    pallas_call x7, Pallas kernels: 21.7 us -> 21.2 us  [body(): pl.pallas_call(functools.partial(chunk_kernel, index, last), out_shape=tu...]
  transfers between devices with their start and end apart: 6 -> 6, of which waited for: 3 -> 5; matrix products, arithmetic and copies ran while one was open for 0% -> 0% of each run, Pallas kernels for 39% -> 40%
where the time goes in v12:
time: 44.3 us; the launch traced here: 44.2 us
  Pallas kernels  27.5 us (62%)
  waiting for transfers between devices  12.8 us (29%)
  starting transfers between devices  3.6 us (8%)
    pallas_call x7, Pallas kernels, body(): pl.pallas_call(functools.partial(chunk_kernel, index, last), out_shape=tu...  21.2 us
    ppermute x6, waiting for transfers between devices, passed_along(): lax.ppermute(array, 'section', [(i, (i + by) % length) for i in range(len...  12.8 us
    pallas_call x1, Pallas kernels, body(): pl.pallas_call(functools.partial(opening_kernel, size), out_shape=(kept((...  6.38 us
    ppermute x6, starting transfers between devices, passed_along(): lax.ppermute(array, 'section', [(i, (i + by) % length) for i in range(len...  3.6 us
  transfers between devices with their start and end apart: 6, of which 5 were waited for; matrix products, arithmetic and copies ran while one was open for 0% of the time, Pallas kernels for 40%

profile of v12, /device:TPU:0, one launch (start us, length us, event | category | flops | bytes accessed | tf_op | source)
XLA Modules:
  0.0 44.2 jit_solution(9404776493794957768)
XLA Ops:
  0.0 6.4 %opening.1 = (bf16[112,1024]{1,0:T(8,128)(2,1)S(1)}, bf16[96,1024]{1,0:T(8,128)(2,1)S(1)}, bf16[96,1024]{1,0:T(8,128)(2,1)S(1)}, f32[192,256]{1,0:T(8,128)S(1)},...) custom-call(bf16[1,192,1024]{2,1,0:T(8,128)(2,1)} %x_hbm.1, ...), custom_call_target="tpu_custom_call" | custom-call | tf_op jit(solution)/shard_map/opening/pallas_call | solution.py:330
  6.4 0.5 %collective-permute-start.1 = (bf16[112,1024]{1,0:T(8,128)(2,1)S(1)}, bf16[112,1024]{1,0:T(8,128)(2,1)S(1)}, u32[]{:S(2)}, u32[]{:S(2)}) collective-permute-start(bf16[112,1024]{1,0:T(8,128)(2,1)S(1)} %get-tuple-element.46), channel_id=1, source_target_pairs={{0,1},{1,2},{2,3},{3,4},{4,5},{5,6},{6,7},{7,8},{8,9},{9,10},{10,1... | collective-permute-start | bytes 688136 | tf_op jit(solution)/shard_map/ppermute | solution.py:317
  6.9 3.1 %chunk_0_1.1 = (bf16[96,1024]{1,0:T(8,128)(2,1)S(1)}, bf16[96,1024]{1,0:T(8,128)(2,1)}, bf16[96,1024]{1,0:T(8,128)(2,1)}) custom-call(bf16[96,1024]{1,0:T(8,128)(2,1)S(1)} %get-tuple-element.35.x_ref, f32[1,1024]{1,0:T(1,128)S(1)} %get-tuple-element.36.gain_ref, bf16[1024,2048]{1,0:T(8,128)(2,1)S(1)} %get-tuple-element.37.wq_ref, ...), custom_call_target="tpu_custom_call" | custom-call | tf_op jit(solution)/shard_map/chunk_0_1/pallas_call | solution.py:390
  10.0 2.7 %collective-permute-start = (bf16[96,1024]{1,0:T(8,128)(2,1)S(1)}, bf16[96,1024]{1,0:T(8,128)(2,1)S(1)}, u32[]{:S(2)}, u32[]{:S(2)}) collective-permute-start(bf16[96,1024]{1,0:T(8,128)(2,1)S(1)} %get-tuple-element.45), channel_id=1, source_target_pairs={{0,1},{1,2},{2,3},{3,4},{4,5},{5,6},{6,7},{7,8},{8,9},{9,10},{10,1... | collective-permute-start | bytes 589832 | tf_op jit(solution)/shard_map/ppermute | solution.py:317
  12.7 2.9 %collective-permute-done.1.x_ref = bf16[112,1024]{1,0:T(8,128)(2,1)S(1)} collective-permute-done((bf16[112,1024]{1,0:T(8,128)(2,1)S(1)}, bf16[112,1024]{1,0:T(8,128)(2,1)S(1)}, u32[]{:S(2)}, u32[]{:S(2)}) %collective-permute-start.1) | collective-permute-done | bytes 229408 | tf_op jit(solution)/shard_map/ppermute | solution.py:317
  15.6 2.8 %chunk_1_0.1 = (bf16[112,1024]{1,0:T(8,128)(2,1)S(1)}, bf16[96,1024]{1,0:T(8,128)(2,1)S(1)}, bf16[96,1024]{1,0:T(8,128)(2,1)S(1)}, f32[192,256]{1,0:T(8,128)S(1)}, f32[192,128]{1,0:T(8,128)S(1)}) custom-call(bf16[112,1024]{1,0:T(8,128)(2,1)S(1)} %collective-permute-done.1.x_ref, f32[1,1024]{1,0:T(1,128)S(1)} %get-tuple-element.36.gain_ref, ...), custom_call_target="tpu_custom_call" | custom-call | tf_op jit(solution)/shard_map/chunk_1_0/pallas_call | solution.py:390
  18.4 0.1 collective-permute-start.3
  18.5 0.0 collective-permute-done.x_ref
  18.5 3.1 %chunk_1_1.1 = (bf16[96,1024]{1,0:T(8,128)(2,1)S(1)}, bf16[96,1024]{1,0:T(8,128)(2,1)}, bf16[96,1024]{1,0:T(8,128)(2,1)}) custom-call(bf16[96,1024]{1,0:T(8,128)(2,1)S(1)} %collective-permute-done.x_ref, f32[1,1024]{1,0:T(1,128)S(1)} %get-tuple-element.36.gain_ref, bf16[1024,2048]{1,0:T(8,128)(2,1)S(1)} %get-tuple-element.37.wq_ref, ...), custom_call_target="tpu_custom_call" | custom-call | tf_op jit(solution)/shard_map/chunk_1_1/pallas_call | solution.py:390
  21.6 0.2 collective-permute-start.2
  21.8 4.8 %collective-permute-done.3.x_ref = bf16[112,1024]{1,0:T(8,128)(2,1)S(1)} collective-permute-done((bf16[112,1024]{1,0:T(8,128)(2,1)S(1)}, bf16[112,1024]{1,0:T(8,128)(2,1)S(1)}, u32[]{:S(2)}, u32[]{:S(2)}) %collective-permute-start.3) | collective-permute-done | bytes 229408 | tf_op jit(solution)/shard_map/ppermute | solution.py:317
  26.6 2.8 %chunk_2_0.1 = (bf16[112,1024]{1,0:T(8,128)(2,1)S(1)}, bf16[96,1024]{1,0:T(8,128)(2,1)S(1)}, bf16[96,1024]{1,0:T(8,128)(2,1)S(1)}, f32[192,256]{1,0:T(8,128)S(1)}, f32[192,128]{1,0:T(8,128)S(1)}) custom-call(bf16[112,1024]{1,0:T(8,128)(2,1)S(1)} %collective-permute-done.3.x_ref, f32[1,1024]{1,0:T(1,128)S(1)} %get-tuple-element.36.gain_ref, ...), custom_call_target="tpu_custom_call" | custom-call | tf_op jit(solution)/shard_map/chunk_2_0/pallas_call | solution.py:390
  29.4 0.1 collective-permute-start.5
  29.5 0.1 collective-permute-done.2.x_ref
  29.6 3.1 %chunk_2_1.1 = (bf16[96,1024]{1,0:T(8,128)(2,1)S(1)}, bf16[96,1024]{1,0:T(8,128)(2,1)}, bf16[96,1024]{1,0:T(8,128)(2,1)}) custom-call(bf16[96,1024]{1,0:T(8,128)(2,1)S(1)} %collective-permute-done.2.x_ref, f32[1,1024]{1,0:T(1,128)S(1)} %get-tuple-element.36.gain_ref, bf16[1024,2048]{1,0:T(8,128)(2,1)S(1)} %get-tuple-element.37.wq_ref, ...), custom_call_target="tpu_custom_call" | custom-call | tf_op jit(solution)/shard_map/chunk_2_1/pallas_call | solution.py:390
  32.7 0.1 collective-permute-start.4
  32.7 4.9 %collective-permute-done.5.x_ref = bf16[112,1024]{1,0:T(8,128)(2,1)S(1)} collective-permute-done((bf16[112,1024]{1,0:T(8,128)(2,1)S(1)}, bf16[112,1024]{1,0:T(8,128)(2,1)S(1)}, u32[]{:S(2)}, u32[]{:S(2)}) %collective-permute-start.5) | collective-permute-done | bytes 229408 | tf_op jit(solution)/shard_map/ppermute | solution.py:317
  37.6 2.8 %chunk_3_0.1 = (bf16[112,1024]{1,0:T(8,128)(2,1)S(1)}, bf16[96,1024]{1,0:T(8,128)(2,1)S(1)}, bf16[96,1024]{1,0:T(8,128)(2,1)S(1)}, f32[192,256]{1,0:T(8,128)S(1)}, f32[192,128]{1,0:T(8,128)S(1)}) custom-call(bf16[112,1024]{1,0:T(8,128)(2,1)S(1)} %collective-permute-done.5.x_ref, f32[1,1024]{1,0:T(1,128)S(1)} %get-tuple-element.36.gain_ref, ...), custom_call_target="tpu_custom_call" | custom-call | tf_op jit(solution)/shard_map/chunk_3_0/pallas_call | solution.py:390
  40.4 0.1 collective-permute-done.4.x_ref
  40.5 3.5 %chunk_3_1.1 = bf16[1,192,1024]{2,1,0:T(8,128)(2,1)} custom-call(bf16[96,1024]{1,0:T(8,128)(2,1)S(1)} %collective-permute-done.4.x_ref, f32[1,1024]{1,0:T(1,128)S(1)} %get-tuple-element.36.gain_ref, bf16[1024,2048]{1,0:T(8,128)(2,1)S(1)} %get-tuple-element.37.wq_ref, bf16[1024,1024]{1,0:T(8,128)(2,1)S(1)} %get-tuple-element.38.wk_ref, ...), custom_call_target="tpu_custom_call" | custom-call | tf_op jit(solution)/shard_map/chunk_3_1/pallas_call | solution.py:390
Async XLA Ops:
  6.4 9.2 %collective-permute-start.1 = (bf16[112,1024]{1,0:T(8,128)(2,1)S(1)}, bf16[112,1024]{1,0:T(8,128)(2,1)S(1)}, u32[]{:S(2)}, u32[]{:S(2)}) collective-permute-start(bf16[112,1024]{1,0:T(8,128)(2,1)S(1)} %get-tuple-element.46), channel_id=1, source_target_pairs={{0,1},{1,2},{2,3},{3,4},{4,5},{5,6},{6,7},{7,8},{8,9},{9,10},{10,1... | collective-permute-start | bytes 688136 | tf_op jit(solution)/shard_map/ppermute | solution.py:317
  10.0 8.5 %collective-permute-start = (bf16[96,1024]{1,0:T(8,128)(2,1)S(1)}, bf16[96,1024]{1,0:T(8,128)(2,1)S(1)}, u32[]{:S(2)}, u32[]{:S(2)}) collective-permute-start(bf16[96,1024]{1,0:T(8,128)(2,1)S(1)} %get-tuple-element.45), channel_id=1, source_target_pairs={{0,1},{1,2},{2,3},{3,4},{4,5},{5,6},{6,7},{7,8},{8,9},{9,10},{10,1... | collective-permute-start | bytes 589832 | tf_op jit(solution)/shard_map/ppermute | solution.py:317
  18.4 8.2 %collective-permute-start.3 = (bf16[112,1024]{1,0:T(8,128)(2,1)S(1)}, bf16[112,1024]{1,0:T(8,128)(2,1)S(1)}, u32[]{:S(2)}, u32[]{:S(2)}) collective-permute-start(bf16[112,1024]{1,0:T(8,128)(2,1)S(1)} %get-tuple-element.53), channel_id=1, source_target_pairs={{0,1},{1,2},{2,3},{3,4},{4,5},{5,6},{6,7},{7,8},{8,9},{9,10},{10,1... | collective-permute-start | bytes 688136 | tf_op jit(solution)/shard_map/ppermute | solution.py:317
  21.6 8.0 %collective-permute-start.2 = (bf16[96,1024]{1,0:T(8,128)(2,1)S(1)}, bf16[96,1024]{1,0:T(8,128)(2,1)S(1)}, u32[]{:S(2)}, u32[]{:S(2)}) collective-permute-start(bf16[96,1024]{1,0:T(8,128)(2,1)S(1)} %get-tuple-element.52), channel_id=1, source_target_pairs={{0,1},{1,2},{2,3},{3,4},{4,5},{5,6},{6,7},{7,8},{8,9},{9,10},{10,1... | collective-permute-start | bytes 589832 | tf_op jit(solution)/shard_map/ppermute | solution.py:317
  29.4 8.2 %collective-permute-start.5 = (bf16[112,1024]{1,0:T(8,128)(2,1)S(1)}, bf16[112,1024]{1,0:T(8,128)(2,1)S(1)}, u32[]{:S(2)}, u32[]{:S(2)}) collective-permute-start(bf16[112,1024]{1,0:T(8,128)(2,1)S(1)} %get-tuple-element.59), channel_id=1, source_target_pairs={{0,1},{1,2},{2,3},{3,4},{4,5},{5,6},{6,7},{7,8},{8,9},{9,10},{10,1... | collective-permute-start | bytes 688136 | tf_op jit(solution)/shard_map/ppermute | solution.py:317
  32.7 7.8 %collective-permute-start.4 = (bf16[96,1024]{1,0:T(8,128)(2,1)S(1)}, bf16[96,1024]{1,0:T(8,128)(2,1)S(1)}, u32[]{:S(2)}, u32[]{:S(2)}) collective-permute-start(bf16[96,1024]{1,0:T(8,128)(2,1)S(1)} %get-tuple-element.58), channel_id=1, source_target_pairs={{0,1},{1,2},{2,3},{3,4},{4,5},{5,6},{6,7},{7,8},{8,9},{9,10},{10,1... | collective-permute-start | bytes 589832 | tf_op jit(solution)/shard_map/ppermute | solution.py:317

commit v13 on v12

--- a/solution.py
+++ b/solution.py
@@ -165,15 +165,14 @@
         write(start, x[:, start : start + PAIR] + (first + second))
 
 
-def write_ids(ids_row, out_ref, size):
-    length = ids_row.shape[1]
-    out_ref[size:, :] = jnp.zeros((EXTRA, out_ref.shape[1]), BF16)
-    out_ref[size:, :length] = jnp.broadcast_to(ids_row, (EXTRA, length)).astype(BF16)
+def write_ids(ids_row, ids_out):
+    ids_out[...] = jnp.zeros(ids_out.shape, BF16)
+    ids_out[:, : ids_row.shape[1]] = jnp.broadcast_to(ids_row, (EXTRA, ids_row.shape[1])).astype(BF16)
 
 
 def opening_kernel(
     size, x_hbm, ids_hbm, gain_hbm, table_hbm, wq_hbm, wk_hbm, wv_hbm, wo_hbm,
-    out_ref, k_ref, v_ref, cos_ref, bias_ref, wq_ref, wk_ref, wv_ref, wo_ref, gain_ref, table_ref, *refs,
+    out_ref, ids_out, k_ref, v_ref, cos_ref, bias_ref, wq_ref, wk_ref, wv_ref, wo_ref, gain_ref, table_ref, *refs,
 ):
     rest_refs, refs = refs[: CHUNKS - 1], refs[CHUNKS - 1 :]
     x_ref, ids_ref, raw_gain, raw_table, mixed_ref, small_sems, sems = refs
@@ -236,7 +235,7 @@
     factors, bias = tables_of(ids_row, table_ref[...])
     cos_ref[...] = factors
     bias_ref[...] = bias
-    write_ids(ids_row, out_ref, size)
+    write_ids(ids_row, ids_out)
 
     def write(start, values):
         out_ref[:size, start : start + PAIR] = values.astype(BF16)
@@ -255,10 +254,9 @@
     size = mixed_ref.shape[0]
     low, high = index * size, (index + 1) * size
     if index == 0:
-        table_ref = refs.pop(0)
-        out_ref, k_ref, v_ref, cos_ref, bias_ref = refs
-        if not last:
-            out_ref[size:, :] = x_ref[size:, :]
+        ids_ref, table_ref, out_ref, k_ref, v_ref, cos_ref, bias_ref, *ids_out = refs
+        for ref in ids_out:
+            ref[...] = ids_ref[...]
         keys, values = [], []
     else:
         cos_ref, bias_ref = refs[:2]
@@ -277,7 +275,7 @@
     def prepare():
         if index:
             return cos_ref[low:high, :], bias_ref[low:high, :]
-        factors, bias = tables_of(x_ref[size:, : CHUNKS * size].astype(F32)[:1], table_ref[...])
+        factors, bias = tables_of(ids_ref[:, : CHUNKS * size].astype(F32)[:1], table_ref[...])
         cos_ref[...] = factors
         bias_ref[...] = bias
         return factors[:size], bias[:size, :size]
@@ -322,7 +320,8 @@
     size = length // CHUNKS
     limits = pltpu.CompilerParams(vmem_limit_bytes=32 * 1024 * 1024)
     table = jnp.asarray(rope_table())
-    rows = [size + EXTRA] + [size] * (CHUNKS - 1)
+    costs = [pl.CostEstimate(flops=flops, bytes_accessed=1024, transcendentals=0) for flops in (20 * 10**9, 1024)]
+    ids_shape = kept((EXTRA, PAIR), BF16)
     key_values = [kept((size, KV_WIDTH), BF16)] * 2
     tables = [kept((length, PAIR), F32), kept((length, HD), F32)]
     mixing = pltpu.VMEM((size, Q_WIDTH), BF16)
@@ -330,7 +329,8 @@
     got = pl.pallas_call(
         functools.partial(opening_kernel, size),
         out_shape=(
-            kept((rows[0], model), BF16),
+            kept((size, model), BF16),
+            ids_shape,
             *key_values,
             *tables,
             kept((model, Q_WIDTH), BF16),
@@ -342,7 +342,7 @@
             *[kept((size, model), BF16)] * (CHUNKS - 1),
         ),
         in_specs=[HBM] * 8,
-        out_specs=(VMEM,) * (10 + CHUNKS),
+        out_specs=(VMEM,) * (11 + CHUNKS),
         scratch_shapes=[
             pltpu.VMEM((size, model), BF16),
             pltpu.VMEM(segment.shape, jnp.int32),
@@ -355,10 +355,10 @@
         compiler_params=limits,
         name="opening",
     )(*(left(array) for array in (micro, segment, gain, table, w_query, w_key, w_value, w_out)))
-    out, k_rows, v_rows, cosines, bias = got[:5]
-    weights = (got[9], *got[5:9])
-    table = got[10]
-    streams = [out, *got[11:]]
+    out, ids, k_rows, v_rows, cosines, bias = got[:6]
+    weights = (got[10], *got[6:10])
+    table = got[11]
+    streams = [out, *got[12:]]
 
     for tick_index in range(TICKS):
         last = tick_index == TICKS - 1
@@ -366,15 +366,16 @@
         for index in range(CHUNKS):
             if tick_index == 0 and index == 0:
                 outs.append(passed_along(streams[0], 1))
+                ids = passed_along(ids, 1)
                 keys.append(k_rows)
                 values.append(v_rows)
                 continue
             args = [streams[index], *weights]
-            shapes = [kept((rows[index], model), BF16), *key_values]
+            shapes = [kept((size, model), BF16), *key_values]
             scratch = [mixing]
             if index == 0:
-                args.append(table)
-                shapes += tables
+                args += [ids, table]
+                shapes += tables + [ids_shape] * (not last)
             else:
                 args += [cosines, bias, *keys, *values]
             specs = [VMEM] * len(shapes)
@@ -390,12 +391,14 @@
             got = pl.pallas_call(
                 functools.partial(chunk_kernel, index, last),
                 out_shape=tuple(shapes), in_specs=[VMEM] * len(args), out_specs=tuple(specs),
-                scratch_shapes=scratch, compiler_params=limits, name="chunk_%d_%d" % (tick_index, index),
+                scratch_shapes=scratch, compiler_params=limits, cost_estimate=costs[index > 0], name="chunk_%d_%d" % (tick_index, index),
             )(*map(held, args))
             if ending:
                 return got[0]
             if index == 0:
-                cosines, bias = got[3:]
+                cosines, bias = got[3:5]
+                if not last:
+                    ids = passed_along(got[5], 1)
             keys.append(got[1])
             values.append(got[2])
             outs.append(got[0] if last else passed_along(got[0], 1))

time: 44.3 us -> 46.4 us (1.047)
  waiting for transfers between devices: 12.8 us -> 14.5 us
    ppermute x6 -> x9, waiting for transfers between devices: 12.8 us -> 14.5 us  [passed_along(): lax.ppermute(array, 'section', [(i, (i + by) % length) for i in range(len...]
    ppermute x6 -> x9, starting transfers between devices: 3.6 us -> 3.78 us  [passed_along(): lax.ppermute(array, 'section', [(i, (i + by) % length) for i in range(len...]
  transfers between devices with their start and end apart: 6 -> 9, of which waited for: 5 -> 6; matrix products, arithmetic and copies ran while one was open for 0% -> 0% of each run, Pallas kernels for 40% -> 39%
where the time goes in v13:
time: 46.4 us; the launch traced here: 46.3 us
  Pallas kernels  27.8 us (60%)
  waiting for transfers between devices  14.5 us (31%)
  starting transfers between devices  3.78 us (8%)
    pallas_call x7, Pallas kernels, body(): pl.pallas_call(functools.partial(chunk_kernel, index, last), out_shape=tu...  21.4 us
    ppermute x9, waiting for transfers between devices, passed_along(): lax.ppermute(array, 'section', [(i, (i + by) % length) for i in range(len...  14.5 us
    pallas_call x1, Pallas kernels, body(): pl.pallas_call(functools.partial(opening_kernel, size), out_shape=(kept((...  6.38 us
    ppermute x9, starting transfers between devices, passed_along(): lax.ppermute(array, 'section', [(i, (i + by) % length) for i in range(len...  3.78 us
  transfers between devices with their start and end apart: 9, of which 6 were waited for; matrix products, arithmetic and copies ran while one was open for 0% of the time, Pallas kernels for 39%

profile of v13, /device:TPU:0, one launch (start us, length us, event | category | flops | bytes accessed | tf_op | source)
XLA Modules:
  0.0 46.3 jit_solution(7478868131829355976)
XLA Ops:
  0.0 6.4 %opening.1 = (bf16[96,1024]{1,0:T(8,128)(2,1)S(1)}, bf16[16,256]{1,0:T(8,128)(2,1)S(1)}, bf16[96,1024]{1,0:T(8,128)(2,1)S(1)}, bf16[96,1024]{1,0:T(8,128)(2,1)S(...) custom-call(bf16[1,192,1024]{2,1,0:T(8,128)(2,1)} %x_hbm.1, ...), custom_call_target="tpu_custom_call" | custom-call | tf_op jit(solution)/shard_map/opening/pallas_call | solution.py:329
  6.4 0.5 %collective-permute-start.1 = (bf16[96,1024]{1,0:T(8,128)(2,1)S(1)}, bf16[96,1024]{1,0:T(8,128)(2,1)S(1)}, u32[]{:S(2)}, u32[]{:S(2)}) collective-permute-start(bf16[96,1024]{1,0:T(8,128)(2,1)S(1)} %get-tuple-element.49), channel_id=1, source_target_pairs={{0,1},{1,2},{2,3},{3,4},{4,5},{5,6},{6,7},{7,8},{8,9},{9,10},{10,1... | collective-permute-start | bytes 589832 | tf_op jit(solution)/shard_map/ppermute | solution.py:315
  6.9 2.6 %collective-permute-start.2 = (bf16[16,256]{1,0:T(8,128)(2,1)S(1)}, bf16[16,256]{1,0:T(8,128)(2,1)S(1)}, u32[]{:S(2)}, u32[]{:S(2)}) collective-permute-start(bf16[16,256]{1,0:T(8,128)(2,1)S(1)} %get-tuple-element.50), channel_id=1, source_target_pairs={{0,1},{1,2},{2,3},{3,4},{4,5},{5,6},{6,7},{7,8},{8,9},{9,10},{10,1... | collective-permute-start | bytes 24584 | tf_op jit(solution)/shard_map/ppermute | solution.py:315
  9.5 3.1 %chunk_0_1.1 = (bf16[96,1024]{1,0:T(8,128)(2,1)S(1)}, bf16[96,1024]{1,0:T(8,128)(2,1)}, bf16[96,1024]{1,0:T(8,128)(2,1)}) custom-call(bf16[96,1024]{1,0:T(8,128)(2,1)S(1)} %get-tuple-element.38.x_ref, f32[1,1024]{1,0:T(1,128)S(1)} %get-tuple-element.39.gain_ref, bf16[1024,2048]{1,0:T(8,128)(2,1)S(1)} %get-tuple-element.40.wq_ref, ...), custom_call_target="tpu_custom_call" | custom-call | flops 1024 | bytes 1024 | tf_op jit(solution)/shard_map/chunk_0_1/pallas_call | solution.py:391
  12.7 0.1 collective-permute-start
  12.8 2.6 %collective-permute-done.2.refs_0_ = bf16[16,256]{1,0:T(8,128)(2,1)S(1)} collective-permute-done((bf16[16,256]{1,0:T(8,128)(2,1)S(1)}, bf16[16,256]{1,0:T(8,128)(2,1)S(1)}, u32[]{:S(2)}, u32[]{:S(2)}) %collective-permute-start.2) | collective-permute-done | bytes 8224 | tf_op jit(solution)/shard_map/ppermute | solution.py:315
  15.3 0.0 collective-permute-done.1.x_ref
  15.3 2.8 %chunk_1_0.1 = (bf16[96,1024]{1,0:T(8,128)(2,1)S(1)}, bf16[96,1024]{1,0:T(8,128)(2,1)S(1)}, bf16[96,1024]{1,0:T(8,128)(2,1)S(1)}, f32[192,256]{1,0:T(8,128)S(1)}...) custom-call(bf16[96,1024]{1,0:T(8,128)(2,1)S(1)} %collective-permute-done.1.x_ref, ...), custom_call_target="tpu_custom_call" | custom-call | flops 20000000000 | bytes 1024 | tf_op jit(solution)/shard_map/chunk_1_0/pallas_call | solution.py:391
  18.2 0.1 collective-permute-start.4
  18.2 0.1 collective-permute-start.5
  18.3 2.2 %collective-permute-done.x_ref = bf16[96,1024]{1,0:T(8,128)(2,1)S(1)} collective-permute-done((bf16[96,1024]{1,0:T(8,128)(2,1)S(1)}, bf16[96,1024]{1,0:T(8,128)(2,1)S(1)}, u32[]{:S(2)}, u32[]{:S(2)}) %collective-permute-start) | collective-permute-done | bytes 196640 | tf_op jit(solution)/shard_map/ppermute | solution.py:315
  20.5 3.1 %chunk_1_1.1 = (bf16[96,1024]{1,0:T(8,128)(2,1)S(1)}, bf16[96,1024]{1,0:T(8,128)(2,1)}, bf16[96,1024]{1,0:T(8,128)(2,1)}) custom-call(bf16[96,1024]{1,0:T(8,128)(2,1)S(1)} %collective-permute-done.x_ref, f32[1,1024]{1,0:T(1,128)S(1)} %get-tuple-element.39.gain_ref, bf16[1024,2048]{1,0:T(8,128)(2,1)S(1)} %get-tuple-element.40.wq_ref, ...), custom_call_target="tpu_custom_call" | custom-call | flops 1024 | bytes 1024 | tf_op jit(solution)/shard_map/chunk_1_1/pallas_call | solution.py:391
  23.6 0.2 collective-permute-start.3
  23.9 2.2 %collective-permute-done.5.refs_0_ = bf16[16,256]{1,0:T(8,128)(2,1)S(1)} collective-permute-done((bf16[16,256]{1,0:T(8,128)(2,1)S(1)}, bf16[16,256]{1,0:T(8,128)(2,1)S(1)}, u32[]{:S(2)}, u32[]{:S(2)}) %collective-permute-start.5) | collective-permute-done | bytes 8224 | tf_op jit(solution)/shard_map/ppermute | solution.py:315
  26.1 0.0 collective-permute-done.4.x_ref
  26.1 2.8 %chunk_2_0.1 = (bf16[96,1024]{1,0:T(8,128)(2,1)S(1)}, bf16[96,1024]{1,0:T(8,128)(2,1)S(1)}, bf16[96,1024]{1,0:T(8,128)(2,1)S(1)}, f32[192,256]{1,0:T(8,128)S(1)}...) custom-call(bf16[96,1024]{1,0:T(8,128)(2,1)S(1)} %collective-permute-done.4.x_ref, ...), custom_call_target="tpu_custom_call" | custom-call | flops 20000000000 | bytes 1024 | tf_op jit(solution)/shard_map/chunk_2_0/pallas_call | solution.py:391
  28.9 0.1 collective-permute-start.7
  29.0 0.1 collective-permute-start.8
  29.1 2.6 %collective-permute-done.3.x_ref = bf16[96,1024]{1,0:T(8,128)(2,1)S(1)} collective-permute-done((bf16[96,1024]{1,0:T(8,128)(2,1)S(1)}, bf16[96,1024]{1,0:T(8,128)(2,1)S(1)}, u32[]{:S(2)}, u32[]{:S(2)}) %collective-permute-start.3) | collective-permute-done | bytes 196640 | tf_op jit(solution)/shard_map/ppermute | solution.py:315
  31.6 3.1 %chunk_2_1.1 = (bf16[96,1024]{1,0:T(8,128)(2,1)S(1)}, bf16[96,1024]{1,0:T(8,128)(2,1)}, bf16[96,1024]{1,0:T(8,128)(2,1)}) custom-call(bf16[96,1024]{1,0:T(8,128)(2,1)S(1)} %collective-permute-done.3.x_ref, f32[1,1024]{1,0:T(1,128)S(1)} %get-tuple-element.39.gain_ref, bf16[1024,2048]{1,0:T(8,128)(2,1)S(1)} %get-tuple-element.40.wq_ref, ...), custom_call_target="tpu_custom_call" | custom-call | flops 1024 | bytes 1024 | tf_op jit(solution)/shard_map/chunk_2_1/pallas_call | solution.py:391
  34.8 0.1 collective-permute-start.6
  34.8 2.1 %collective-permute-done.8.refs_0_ = bf16[16,256]{1,0:T(8,128)(2,1)S(1)} collective-permute-done((bf16[16,256]{1,0:T(8,128)(2,1)S(1)}, bf16[16,256]{1,0:T(8,128)(2,1)S(1)}, u32[]{:S(2)}, u32[]{:S(2)}) %collective-permute-start.8) | collective-permute-done | bytes 8224 | tf_op jit(solution)/shard_map/ppermute | solution.py:315
  36.9 0.0 collective-permute-done.7.x_ref
  36.9 2.8 %chunk_3_0.1 = (bf16[96,1024]{1,0:T(8,128)(2,1)S(1)}, bf16[96,1024]{1,0:T(8,128)(2,1)S(1)}, bf16[96,1024]{1,0:T(8,128)(2,1)S(1)}, f32[192,256]{1,0:T(8,128)S(1)}, f32[192,128]{1,0:T(8,128)S(1)}) custom-call(bf16[96,1024]{1,0:T(8,128)(2,1)S(1)} %collective-permute-done.7.x_ref, f32[1,1024]{1,0:T(1,128)S(1)} %get-tuple-element.39.gain_ref, ...), custom_call_target="tpu_custom_call" | custom-call | flops 20000000000 | bytes 1024 | tf_op jit(solution)/shard_map/chunk_3_0/pallas_call | solution.py:391
  39.7 2.9 %collective-permute-done.6.x_ref = bf16[96,1024]{1,0:T(8,128)(2,1)S(1)} collective-permute-done((bf16[96,1024]{1,0:T(8,128)(2,1)S(1)}, bf16[96,1024]{1,0:T(8,128)(2,1)S(1)}, u32[]{:S(2)}, u32[]{:S(2)}) %collective-permute-start.6) | collective-permute-done | bytes 196640 | tf_op jit(solution)/shard_map/ppermute | solution.py:315
  42.6 3.5 %chunk_3_1.1 = bf16[1,192,1024]{2,1,0:T(8,128)(2,1)} custom-call(bf16[96,1024]{1,0:T(8,128)(2,1)S(1)} %collective-permute-done.6.x_ref, f32[1,1024]{1,0:T(1,128)S(1)} %get-tuple-element.39.gain_ref, bf16[1024,2048]{1,0:T(8,128)(2,1)S(1)} %get-tuple-element.40.wq_ref, bf16[1024,1024]{1,0:T(8,128)(2,1)S(1)} %get-tuple-element.41.wk_ref, ...), custom_call_target="tpu_custom_call" | custom-call | flops 1024 | bytes 1024 | tf_op jit(solution)/shard_map/chunk_3_1/pallas_call | solution.py:391
Async XLA Ops:
  6.4 8.9 %collective-permute-start.1 = (bf16[96,1024]{1,0:T(8,128)(2,1)S(1)}, bf16[96,1024]{1,0:T(8,128)(2,1)S(1)}, u32[]{:S(2)}, u32[]{:S(2)}) collective-permute-start(bf16[96,1024]{1,0:T(8,128)(2,1)S(1)} %get-tuple-element.49), channel_id=1, source_target_pairs={{0,1},{1,2},{2,3},{3,4},{4,5},{5,6},{6,7},{7,8},{8,9},{9,10},{10,1... | collective-permute-start | bytes 589832 | tf_op jit(solution)/shard_map/ppermute | solution.py:315
  6.9 8.4 %collective-permute-start.2 = (bf16[16,256]{1,0:T(8,128)(2,1)S(1)}, bf16[16,256]{1,0:T(8,128)(2,1)S(1)}, u32[]{:S(2)}, u32[]{:S(2)}) collective-permute-start(bf16[16,256]{1,0:T(8,128)(2,1)S(1)} %get-tuple-element.50), channel_id=1, source_target_pairs={{0,1},{1,2},{2,3},{3,4},{4,5},{5,6},{6,7},{7,8},{8,9},{9,10},{10,1... | collective-permute-start | bytes 24584 | tf_op jit(solution)/shard_map/ppermute | solution.py:315
  12.7 7.8 %collective-permute-start = (bf16[96,1024]{1,0:T(8,128)(2,1)S(1)}, bf16[96,1024]{1,0:T(8,128)(2,1)S(1)}, u32[]{:S(2)}, u32[]{:S(2)}) collective-permute-start(bf16[96,1024]{1,0:T(8,128)(2,1)S(1)} %get-tuple-element.48), channel_id=1, source_target_pairs={{0,1},{1,2},{2,3},{3,4},{4,5},{5,6},{6,7},{7,8},{8,9},{9,10},{10,1... | collective-permute-start | bytes 589832 | tf_op jit(solution)/shard_map/ppermute | solution.py:315
  18.2 7.9 %collective-permute-start.4 = (bf16[96,1024]{1,0:T(8,128)(2,1)S(1)}, bf16[96,1024]{1,0:T(8,128)(2,1)S(1)}, u32[]{:S(2)}, u32[]{:S(2)}) collective-permute-start(bf16[96,1024]{1,0:T(8,128)(2,1)S(1)} %get-tuple-element.57), channel_id=1, source_target_pairs={{0,1},{1,2},{2,3},{3,4},{4,5},{5,6},{6,7},{7,8},{8,9},{9,10},{10,1... | collective-permute-start | bytes 589832 | tf_op jit(solution)/shard_map/ppermute | solution.py:315
  18.2 7.9 %collective-permute-start.5 = (bf16[16,256]{1,0:T(8,128)(2,1)S(1)}, bf16[16,256]{1,0:T(8,128)(2,1)S(1)}, u32[]{:S(2)}, u32[]{:S(2)}) collective-permute-start(bf16[16,256]{1,0:T(8,128)(2,1)S(1)} %get-tuple-element.58), channel_id=1, source_target_pairs={{0,1},{1,2},{2,3},{3,4},{4,5},{5,6},{6,7},{7,8},{8,9},{9,10},{10,1... | collective-permute-start | bytes 24584 | tf_op jit(solution)/shard_map/ppermute | solution.py:315
  23.6 8.0 %collective-permute-start.3 = (bf16[96,1024]{1,0:T(8,128)(2,1)S(1)}, bf16[96,1024]{1,0:T(8,128)(2,1)S(1)}, u32[]{:S(2)}, u32[]{:S(2)}) collective-permute-start(bf16[96,1024]{1,0:T(8,128)(2,1)S(1)} %get-tuple-element.56), channel_id=1, source_target_pairs={{0,1},{1,2},{2,3},{3,4},{4,5},{5,6},{6,7},{7,8},{8,9},{9,10},{10,1... | collective-permute-start | bytes 589832 | tf_op jit(solution)/shard_map/ppermute | solution.py:315
  28.9 7.9 %collective-permute-start.7 = (bf16[96,1024]{1,0:T(8,128)(2,1)S(1)}, bf16[96,1024]{1,0:T(8,128)(2,1)S(1)}, u32[]{:S(2)}, u32[]{:S(2)}) collective-permute-start(bf16[96,1024]{1,0:T(8,128)(2,1)S(1)} %get-tuple-element.64), channel_id=1, source_target_pairs={{0,1},{1,2},{2,3},{3,4},{4,5},{5,6},{6,7},{7,8},{8,9},{9,10},{10,1... | collective-permute-start | bytes 589832 | tf_op jit(solution)/shard_map/ppermute | solution.py:315
  29.0 7.9 %collective-permute-start.8 = (bf16[16,256]{1,0:T(8,128)(2,1)S(1)}, bf16[16,256]{1,0:T(8,128)(2,1)S(1)}, u32[]{:S(2)}, u32[]{:S(2)}) collective-permute-start(bf16[16,256]{1,0:T(8,128)(2,1)S(1)} %get-tuple-element.65), channel_id=1, source_target_pairs={{0,1},{1,2},{2,3},{3,4},{4,5},{5,6},{6,7},{7,8},{8,9},{9,10},{10,1... | collective-permute-start | bytes 24584 | tf_op jit(solution)/shard_map/ppermute | solution.py:315
  34.8 7.8 %collective-permute-start.6 = (bf16[96,1024]{1,0:T(8,128)(2,1)S(1)}, bf16[96,1024]{1,0:T(8,128)(2,1)S(1)}, u32[]{:S(2)}, u32[]{:S(2)}) collective-permute-start(bf16[96,1024]{1,0:T(8,128)(2,1)S(1)} %get-tuple-element.63), channel_id=1, source_target_pairs={{0,1},{1,2},{2,3},{3,4},{4,5},{5,6},{6,7},{7,8},{8,9},{9,10},{10,1... | collective-permute-start | bytes 589832 | tf_op jit(solution)/shard_map/ppermute | solution.py:315

commit v14 on v13

--- a/solution.py
+++ b/solution.py
@@ -172,7 +172,7 @@
 
 def opening_kernel(
     size, x_hbm, ids_hbm, gain_hbm, table_hbm, wq_hbm, wk_hbm, wv_hbm, wo_hbm,
-    out_ref, ids_out, k_ref, v_ref, cos_ref, bias_ref, wq_ref, wk_ref, wv_ref, wo_ref, gain_ref, table_ref, *refs,
+    out_ref, k_ref, v_ref, cos_ref, bias_ref, wq_ref, wk_ref, wv_ref, wo_ref, gain_ref, table_ref, *refs,
 ):
     rest_refs, refs = refs[: CHUNKS - 1], refs[CHUNKS - 1 :]
     x_ref, ids_ref, raw_gain, raw_table, mixed_ref, small_sems, sems = refs
@@ -235,7 +235,7 @@
     factors, bias = tables_of(ids_row, table_ref[...])
     cos_ref[...] = factors
     bias_ref[...] = bias
-    write_ids(ids_row, ids_out)
+    write_ids(ids_row, out_ref.at[x_ref.shape[0] :])
 
     def write(start, values):
         out_ref[:size, start : start + PAIR] = values.astype(BF16)
@@ -255,6 +255,8 @@
     low, high = index * size, (index + 1) * size
     if index == 0:
         ids_ref, table_ref, out_ref, k_ref, v_ref, cos_ref, bias_ref, *ids_out = refs
+        if ids_ref.shape[0] > EXTRA:
+            ids_ref = ids_ref.at[size:, :PAIR]
         for ref in ids_out:
             ref[...] = ids_ref[...]
         keys, values = [], []
@@ -329,8 +331,7 @@
     got = pl.pallas_call(
         functools.partial(opening_kernel, size),
         out_shape=(
-            kept((size, model), BF16),
-            ids_shape,
+            kept((size + EXTRA, model), BF16),
             *key_values,
             *tables,
             kept((model, Q_WIDTH), BF16),
@@ -342,7 +343,7 @@
             *[kept((size, model), BF16)] * (CHUNKS - 1),
         ),
         in_specs=[HBM] * 8,
-        out_specs=(VMEM,) * (11 + CHUNKS),
+        out_specs=(VMEM,) * (10 + CHUNKS),
         scratch_shapes=[
             pltpu.VMEM((size, model), BF16),
             pltpu.VMEM(segment.shape, jnp.int32),
@@ -355,10 +356,10 @@
         compiler_params=limits,
         name="opening",
     )(*(left(array) for array in (micro, segment, gain, table, w_query, w_key, w_value, w_out)))
-    out, ids, k_rows, v_rows, cosines, bias = got[:6]
-    weights = (got[10], *got[6:10])
-    table = got[11]
-    streams = [out, *got[12:]]
+    out, k_rows, v_rows, cosines, bias = got[:5]
+    weights = (got[9], *got[5:9])
+    table = got[10]
+    streams = [out, *got[11:]]
 
     for tick_index in range(TICKS):
         last = tick_index == TICKS - 1
@@ -366,7 +367,7 @@
         for index in range(CHUNKS):
             if tick_index == 0 and index == 0:
                 outs.append(passed_along(streams[0], 1))
-                ids = passed_along(ids, 1)
+                ids = outs[0]
                 keys.append(k_rows)
                 values.append(v_rows)
                 continue

time: 46.4 us -> 44.4 us (0.957)
  waiting for transfers between devices: 14.5 us -> 12.8 us
    ppermute x9 -> x8, waiting for transfers between devices: 14.5 us -> 12.8 us  [passed_along(): lax.ppermute(array, 'section', [(i, (i + by) % length) for i in range(len...]
    ppermute x9 -> x8, starting transfers between devices: 3.78 us -> 3.71 us  [passed_along(): lax.ppermute(array, 'section', [(i, (i + by) % length) for i in range(len...]
  transfers between devices with their start and end apart: 9 -> 8, of which waited for: 6 -> 5; matrix products, arithmetic and copies ran while one was open for 0% -> 0% of each run, Pallas kernels for 39% -> 40%
where the time goes in v14:
time: 44.4 us; the launch traced here: 44.3 us
  Pallas kernels  27.6 us (62%)
  waiting for transfers between devices  12.8 us (29%)
  starting transfers between devices  3.71 us (8%)
    pallas_call x7, Pallas kernels, body(): pl.pallas_call(functools.partial(chunk_kernel, index, last), out_shape=tu...  21.2 us
    ppermute x8, waiting for transfers between devices, passed_along(): lax.ppermute(array, 'section', [(i, (i + by) % length) for i in range(len...  12.8 us
    pallas_call x1, Pallas kernels, body(): pl.pallas_call(functools.partial(opening_kernel, size), out_shape=(kept((...  6.38 us
    ppermute x8, starting transfers between devices, passed_along(): lax.ppermute(array, 'section', [(i, (i + by) % length) for i in range(len...  3.71 us
  transfers between devices with their start and end apart: 8, of which 5 were waited for; matrix products, arithmetic and copies ran while one was open for 0% of the time, Pallas kernels for 40%

profile of v14, /device:TPU:0, one launch (start us, length us, event | category | flops | bytes accessed | tf_op | source)
XLA Modules:
  0.0 44.3 jit_solution(12182751383001532794)
XLA Ops:
  0.0 6.4 %opening.1 = (bf16[112,1024]{1,0:T(8,128)(2,1)S(1)}, bf16[96,1024]{1,0:T(8,128)(2,1)S(1)}, bf16[96,1024]{1,0:T(8,128)(2,1)S(1)}, f32[192,256]{1,0:T(8,128)S(1)},...) custom-call(bf16[1,192,1024]{2,1,0:T(8,128)(2,1)} %x_hbm.1, ...), custom_call_target="tpu_custom_call" | custom-call | tf_op jit(solution)/shard_map/opening/pallas_call | solution.py:331
  6.4 0.5 %collective-permute-start.1 = (bf16[112,1024]{1,0:T(8,128)(2,1)S(1)}, bf16[112,1024]{1,0:T(8,128)(2,1)S(1)}, u32[]{:S(2)}, u32[]{:S(2)}) collective-permute-start(bf16[112,1024]{1,0:T(8,128)(2,1)S(1)} %get-tuple-element.48), channel_id=1, source_target_pairs={{0,1},{1,2},{2,3},{3,4},{4,5},{5,6},{6,7},{7,8},{8,9},{9,10},{10,1... | collective-permute-start | bytes 688136 | tf_op jit(solution)/shard_map/ppermute | solution.py:317
  6.9 3.1 %chunk_0_1.1 = (bf16[96,1024]{1,0:T(8,128)(2,1)S(1)}, bf16[96,1024]{1,0:T(8,128)(2,1)}, bf16[96,1024]{1,0:T(8,128)(2,1)}) custom-call(bf16[96,1024]{1,0:T(8,128)(2,1)S(1)} %get-tuple-element.37.x_ref, f32[1,1024]{1,0:T(1,128)S(1)} %get-tuple-element.38.gain_ref, bf16[1024,2048]{1,0:T(8,128)(2,1)S(1)} %get-tuple-element.39.wq_ref, ...), custom_call_target="tpu_custom_call" | custom-call | flops 1024 | bytes 1024 | tf_op jit(solution)/shard_map/chunk_0_1/pallas_call | solution.py:392
  10.0 2.7 %collective-permute-start = (bf16[96,1024]{1,0:T(8,128)(2,1)S(1)}, bf16[96,1024]{1,0:T(8,128)(2,1)S(1)}, u32[]{:S(2)}, u32[]{:S(2)}) collective-permute-start(bf16[96,1024]{1,0:T(8,128)(2,1)S(1)} %get-tuple-element.47), channel_id=1, source_target_pairs={{0,1},{1,2},{2,3},{3,4},{4,5},{5,6},{6,7},{7,8},{8,9},{9,10},{10,1... | collective-permute-start | bytes 589832 | tf_op jit(solution)/shard_map/ppermute | solution.py:317
  12.7 2.9 %collective-permute-done.1.x_ref.refs_0_ = bf16[112,1024]{1,0:T(8,128)(2,1)S(1)} collective-permute-done((bf16[112,1024]{1,0:T(8,128)(2,1)S(1)}, bf16[112,1024]{1,0:T(8,128)(2,1)S(1)}, u32[]{:S(2)}, u32[]{:S(2)}) %collective-permute-start.1) | collective-permute-done | bytes 229408 | tf_op jit(solution)/shard_map/ppermute | solution.py:317
  15.6 2.8 %chunk_1_0.1 = (bf16[96,1024]{1,0:T(8,128)(2,1)S(1)}, bf16[96,1024]{1,0:T(8,128)(2,1)S(1)}, bf16[96,1024]{1,0:T(8,128)(2,1)S(1)}, f32[192,256]{1,0:T(8,128)S(1)}...) custom-call(bf16[112,1024]{1,0:T(8,128)(2,1)S(1)} %collective-permute-done.1.x_ref.refs_0_, ...), custom_call_target="tpu_custom_call" | custom-call | flops 20000000000 | bytes 1024 | tf_op jit(solution)/shard_map/chunk_1_0/pallas_call | solution.py:392
  18.4 0.1 collective-permute-start.3
  18.4 0.1 collective-permute-start.4
  18.5 0.0 collective-permute-done.x_ref
  18.5 3.1 %chunk_1_1.1 = (bf16[96,1024]{1,0:T(8,128)(2,1)S(1)}, bf16[96,1024]{1,0:T(8,128)(2,1)}, bf16[96,1024]{1,0:T(8,128)(2,1)}) custom-call(bf16[96,1024]{1,0:T(8,128)(2,1)S(1)} %collective-permute-done.x_ref, f32[1,1024]{1,0:T(1,128)S(1)} %get-tuple-element.38.gain_ref, bf16[1024,2048]{1,0:T(8,128)(2,1)S(1)} %get-tuple-element.39.wq_ref, ...), custom_call_target="tpu_custom_call" | custom-call | flops 1024 | bytes 1024 | tf_op jit(solution)/shard_map/chunk_1_1/pallas_call | solution.py:392
  21.6 0.2 collective-permute-start.2
  21.9 4.4 %collective-permute-done.4.refs_0_ = bf16[16,256]{1,0:T(8,128)(2,1)S(1)} collective-permute-done((bf16[16,256]{1,0:T(8,128)(2,1)S(1)}, bf16[16,256]{1,0:T(8,128)(2,1)S(1)}, u32[]{:S(2)}, u32[]{:S(2)}) %collective-permute-start.4) | collective-permute-done | bytes 8224 | tf_op jit(solution)/shard_map/ppermute | solution.py:317
  26.3 0.0 collective-permute-done.3.x_ref
  26.3 2.8 %chunk_2_0.1 = (bf16[96,1024]{1,0:T(8,128)(2,1)S(1)}, bf16[96,1024]{1,0:T(8,128)(2,1)S(1)}, bf16[96,1024]{1,0:T(8,128)(2,1)S(1)}, f32[192,256]{1,0:T(8,128)S(1)}...) custom-call(bf16[96,1024]{1,0:T(8,128)(2,1)S(1)} %collective-permute-done.3.x_ref, ...), custom_call_target="tpu_custom_call" | custom-call | flops 20000000000 | bytes 1024 | tf_op jit(solution)/shard_map/chunk_2_0/pallas_call | solution.py:392
  29.1 0.1 collective-permute-start.6
  29.2 0.1 collective-permute-start.7
  29.2 0.4 collective-permute-done.2.x_ref
  29.7 3.1 %chunk_2_1.1 = (bf16[96,1024]{1,0:T(8,128)(2,1)S(1)}, bf16[96,1024]{1,0:T(8,128)(2,1)}, bf16[96,1024]{1,0:T(8,128)(2,1)}) custom-call(bf16[96,1024]{1,0:T(8,128)(2,1)S(1)} %collective-permute-done.2.x_ref, f32[1,1024]{1,0:T(1,128)S(1)} %get-tuple-element.38.gain_ref, bf16[1024,2048]{1,0:T(8,128)(2,1)S(1)} %get-tuple-element.39.wq_ref, ...), custom_call_target="tpu_custom_call" | custom-call | flops 1024 | bytes 1024 | tf_op jit(solution)/shard_map/chunk_2_1/pallas_call | solution.py:392
  32.8 0.1 collective-permute-start.5
  32.8 4.2 %collective-permute-done.7.refs_0_ = bf16[16,256]{1,0:T(8,128)(2,1)S(1)} collective-permute-done((bf16[16,256]{1,0:T(8,128)(2,1)S(1)}, bf16[16,256]{1,0:T(8,128)(2,1)S(1)}, u32[]{:S(2)}, u32[]{:S(2)}) %collective-permute-start.7) | collective-permute-done | bytes 8224 | tf_op jit(solution)/shard_map/ppermute | solution.py:317
  37.0 0.0 collective-permute-done.6.x_ref
  37.1 2.8 %chunk_3_0.1 = (bf16[96,1024]{1,0:T(8,128)(2,1)S(1)}, bf16[96,1024]{1,0:T(8,128)(2,1)S(1)}, bf16[96,1024]{1,0:T(8,128)(2,1)S(1)}, f32[192,256]{1,0:T(8,128)S(1)}, f32[192,128]{1,0:T(8,128)S(1)}) custom-call(bf16[96,1024]{1,0:T(8,128)(2,1)S(1)} %collective-permute-done.6.x_ref, f32[1,1024]{1,0:T(1,128)S(1)} %get-tuple-element.38.gain_ref, ...), custom_call_target="tpu_custom_call" | custom-call | flops 20000000000 | bytes 1024 | tf_op jit(solution)/shard_map/chunk_3_0/pallas_call | solution.py:392
  39.9 0.7 %collective-permute-done.5.x_ref = bf16[96,1024]{1,0:T(8,128)(2,1)S(1)} collective-permute-done((bf16[96,1024]{1,0:T(8,128)(2,1)S(1)}, bf16[96,1024]{1,0:T(8,128)(2,1)S(1)}, u32[]{:S(2)}, u32[]{:S(2)}) %collective-permute-start.5) | collective-permute-done | bytes 196640 | tf_op jit(solution)/shard_map/ppermute | solution.py:317
  40.6 3.5 %chunk_3_1.1 = bf16[1,192,1024]{2,1,0:T(8,128)(2,1)} custom-call(bf16[96,1024]{1,0:T(8,128)(2,1)S(1)} %collective-permute-done.5.x_ref, f32[1,1024]{1,0:T(1,128)S(1)} %get-tuple-element.38.gain_ref, bf16[1024,2048]{1,0:T(8,128)(2,1)S(1)} %get-tuple-element.39.wq_ref, bf16[1024,1024]{1,0:T(8,128)(2,1)S(1)} %get-tuple-element.40.wk_ref, ...), custom_call_target="tpu_custom_call" | custom-call | flops 1024 | bytes 1024 | tf_op jit(solution)/shard_map/chunk_3_1/pallas_call | solution.py:392
Async XLA Ops:
  6.4 9.2 %collective-permute-start.1 = (bf16[112,1024]{1,0:T(8,128)(2,1)S(1)}, bf16[112,1024]{1,0:T(8,128)(2,1)S(1)}, u32[]{:S(2)}, u32[]{:S(2)}) collective-permute-start(bf16[112,1024]{1,0:T(8,128)(2,1)S(1)} %get-tuple-element.48), channel_id=1, source_target_pairs={{0,1},{1,2},{2,3},{3,4},{4,5},{5,6},{6,7},{7,8},{8,9},{9,10},{10,1... | collective-permute-start | bytes 688136 | tf_op jit(solution)/shard_map/ppermute | solution.py:317
  10.0 8.5 %collective-permute-start = (bf16[96,1024]{1,0:T(8,128)(2,1)S(1)}, bf16[96,1024]{1,0:T(8,128)(2,1)S(1)}, u32[]{:S(2)}, u32[]{:S(2)}) collective-permute-start(bf16[96,1024]{1,0:T(8,128)(2,1)S(1)} %get-tuple-element.47), channel_id=1, source_target_pairs={{0,1},{1,2},{2,3},{3,4},{4,5},{5,6},{6,7},{7,8},{8,9},{9,10},{10,1... | collective-permute-start | bytes 589832 | tf_op jit(solution)/shard_map/ppermute | solution.py:317
  18.4 7.9 %collective-permute-start.3 = (bf16[96,1024]{1,0:T(8,128)(2,1)S(1)}, bf16[96,1024]{1,0:T(8,128)(2,1)S(1)}, u32[]{:S(2)}, u32[]{:S(2)}) collective-permute-start(bf16[96,1024]{1,0:T(8,128)(2,1)S(1)} %get-tuple-element.55), channel_id=1, source_target_pairs={{0,1},{1,2},{2,3},{3,4},{4,5},{5,6},{6,7},{7,8},{8,9},{9,10},{10,1... | collective-permute-start | bytes 589832 | tf_op jit(solution)/shard_map/ppermute | solution.py:317
  18.4 7.9 %collective-permute-start.4 = (bf16[16,256]{1,0:T(8,128)(2,1)S(1)}, bf16[16,256]{1,0:T(8,128)(2,1)S(1)}, u32[]{:S(2)}, u32[]{:S(2)}) collective-permute-start(bf16[16,256]{1,0:T(8,128)(2,1)S(1)} %get-tuple-element.56), channel_id=1, source_target_pairs={{0,1},{1,2},{2,3},{3,4},{4,5},{5,6},{6,7},{7,8},{8,9},{9,10},{10,1... | collective-permute-start | bytes 24584 | tf_op jit(solution)/shard_map/ppermute | solution.py:317
  21.6 8.0 %collective-permute-start.2 = (bf16[96,1024]{1,0:T(8,128)(2,1)S(1)}, bf16[96,1024]{1,0:T(8,128)(2,1)S(1)}, u32[]{:S(2)}, u32[]{:S(2)}) collective-permute-start(bf16[96,1024]{1,0:T(8,128)(2,1)S(1)} %get-tuple-element.54), channel_id=1, source_target_pairs={{0,1},{1,2},{2,3},{3,4},{4,5},{5,6},{6,7},{7,8},{8,9},{9,10},{10,1... | collective-permute-start | bytes 589832 | tf_op jit(solution)/shard_map/ppermute | solution.py:317
  29.1 7.9 %collective-permute-start.6 = (bf16[96,1024]{1,0:T(8,128)(2,1)S(1)}, bf16[96,1024]{1,0:T(8,128)(2,1)S(1)}, u32[]{:S(2)}, u32[]{:S(2)}) collective-permute-start(bf16[96,1024]{1,0:T(8,128)(2,1)S(1)} %get-tuple-element.62), channel_id=1, source_target_pairs={{0,1},{1,2},{2,3},{3,4},{4,5},{5,6},{6,7},{7,8},{8,9},{9,10},{10,1... | collective-permute-start | bytes 589832 | tf_op jit(solution)/shard_map/ppermute | solution.py:317
  29.2 7.9 %collective-permute-start.7 = (bf16[16,256]{1,0:T(8,128)(2,1)S(1)}, bf16[16,256]{1,0:T(8,128)(2,1)S(1)}, u32[]{:S(2)}, u32[]{:S(2)}) collective-permute-start(bf16[16,256]{1,0:T(8,128)(2,1)S(1)} %get-tuple-element.63), channel_id=1, source_target_pairs={{0,1},{1,2},{2,3},{3,4},{4,5},{5,6},{6,7},{7,8},{8,9},{9,10},{10,1... | collective-permute-start | bytes 24584 | tf_op jit(solution)/shard_map/ppermute | solution.py:317
  32.8 7.8 %collective-permute-start.5 = (bf16[96,1024]{1,0:T(8,128)(2,1)S(1)}, bf16[96,1024]{1,0:T(8,128)(2,1)S(1)}, u32[]{:S(2)}, u32[]{:S(2)}) collective-permute-start(bf16[96,1024]{1,0:T(8,128)(2,1)S(1)} %get-tuple-element.61), channel_id=1, source_target_pairs={{0,1},{1,2},{2,3},{3,4},{4,5},{5,6},{6,7},{7,8},{8,9},{9,10},{10,1... | collective-permute-start | bytes 589832 | tf_op jit(solution)/shard_map/ppermute | solution.py:317

commit v15 on v10

--- a/solution.py
+++ b/solution.py
@@ -256,15 +256,19 @@
 
     def write(start, result):
         out_ref[:size, start : start + PAIR] = result.astype(BF16)
+        if last and index == CHUNKS - 1 and start % (2 * PAIR):
+            lanes = slice(start - PAIR, start + PAIR)
+            copies.append(
+                pltpu.make_async_copy(out_ref.at[:, lanes], whole_ref.at[0, low:high, lanes], sems.at[len(copies)])
+            )
+            copies[-1].start()
 
     layer(
         x_ref[:size, :].astype(F32), gain_ref[...], (wq_ref, wk_ref, wv_ref, wo_ref), lambda name, start: None,
         prepare, keys, values, k_ref, v_ref, mixed_ref, write,
     )
     if last and index == CHUNKS - 1:
-        copy = pltpu.make_async_copy(out_ref, whole_ref.at[0, low:high], sems.at[index])
-        copy.start()
-        for each in copies + [copy]:
+        for each in copies:
             each.wait()
 
 
@@ -357,7 +361,7 @@
                 specs = [pl.BlockSpec(memory_space=pl.ANY)]
                 scratch = [
                     pltpu.VMEM((size, model), BF16), *[pltpu.VMEM((size, KV_WIDTH), BF16)] * 2,
-                    pltpu.SemaphoreType.DMA((CHUNKS,)), mixing,
+                    pltpu.SemaphoreType.DMA((CHUNKS + 1,)), mixing,
                 ]
             got = pl.pallas_call(
                 functools.partial(chunk_kernel, index, last),

time: 44.5 us -> 44.5 us (level)
  no operation moved by 1% of the time
where the time goes in v15:
time: 44.5 us; the launch traced here: 44.3 us
  Pallas kernels  28.1 us (63%)
  waiting for transfers between devices  12.8 us (29%)
  starting transfers between devices  3.26 us (7%)
    pallas_call x7, Pallas kernels, body(): pl.pallas_call(functools.partial(chunk_kernel, index, last), out_shape=tu...  21.8 us
    ppermute x6, waiting for transfers between devices, passed_along(): lax.ppermute(array, 'section', [(i, (i + by) % length) for i in range(len...  12.8 us
    pallas_call x1, Pallas kernels, body(): pl.pallas_call(functools.partial(opening_kernel, size), out_shape=(kept((...  6.3 us
    ppermute x6, starting transfers between devices, passed_along(): lax.ppermute(array, 'section', [(i, (i + by) % length) for i in range(len...  3.26 us
  transfers between devices with their start and end apart: 6, of which 6 were waited for; matrix products, arithmetic and copies ran while one was open for 0% of the time, Pallas kernels for 41%

profile of v15, /device:TPU:0, one launch (start us, length us, event | category | flops | bytes accessed | tf_op | source)
XLA Modules:
  0.0 44.3 jit_solution(226777903958235132)
XLA Ops:
  0.0 6.3 %opening.1 = (bf16[112,1024]{1,0:T(8,128)(2,1)S(1)}, bf16[96,1024]{1,0:T(8,128)(2,1)S(1)}, bf16[96,1024]{1,0:T(8,128)(2,1)S(1)}, f32[192,256]{1,0:T(8,128)S(1)},...) custom-call(bf16[1,192,1024]{2,1,0:T(8,128)(2,1)} %x_hbm.1, ...), custom_call_target="tpu_custom_call" | custom-call | tf_op jit(solution)/shard_map/opening/pallas_call | solution.py:306
  6.3 0.5 %collective-permute-start.1 = (bf16[112,1024]{1,0:T(8,128)(2,1)S(1)}, bf16[112,1024]{1,0:T(8,128)(2,1)S(1)}, u32[]{:S(2)}, u32[]{:S(2)}) collective-permute-start(bf16[112,1024]{1,0:T(8,128)(2,1)S(1)} %get-tuple-element.46), channel_id=1, source_target_pairs={{0,1},{1,2},{2,3},{3,4},{4,5},{5,6},{6,7},{7,8},{8,9},{9,10},{10,1... | collective-permute-start | bytes 688136 | tf_op jit(solution)/shard_map/ppermute | solution.py:293
  6.8 3.3 %chunk_0_1.1 = (bf16[96,1024]{1,0:T(8,128)(2,1)S(1)}, bf16[96,1024]{1,0:T(8,128)(2,1)}, bf16[96,1024]{1,0:T(8,128)(2,1)}) custom-call(bf16[96,1024]{1,0:T(8,128)(2,1)S(1)} %get-tuple-element.35.x_ref, f32[1,1024]{1,0:T(1,128)S(1)} %get-tuple-element.36.gain_ref, bf16[1024,2048]{1,0:T(8,128)(2,1)S(1)} %get-tuple-element.37.wq_ref, ...), custom_call_target="tpu_custom_call" | custom-call | tf_op jit(solution)/shard_map/chunk_0_1/pallas_call | solution.py:366
  10.1 2.6 %collective-permute-start = (bf16[96,1024]{1,0:T(8,128)(2,1)S(1)}, bf16[96,1024]{1,0:T(8,128)(2,1)S(1)}, u32[]{:S(2)}, u32[]{:S(2)}) collective-permute-start(bf16[96,1024]{1,0:T(8,128)(2,1)S(1)} %get-tuple-element.45), channel_id=1, source_target_pairs={{0,1},{1,2},{2,3},{3,4},{4,5},{5,6},{6,7},{7,8},{8,9},{9,10},{10,1... | collective-permute-start | bytes 589832 | tf_op jit(solution)/shard_map/ppermute | solution.py:293
  12.8 2.8 %collective-permute-done.1.x_ref = bf16[112,1024]{1,0:T(8,128)(2,1)S(1)} collective-permute-done((bf16[112,1024]{1,0:T(8,128)(2,1)S(1)}, bf16[112,1024]{1,0:T(8,128)(2,1)S(1)}, u32[]{:S(2)}, u32[]{:S(2)}) %collective-permute-start.1) | collective-permute-done | bytes 229408 | tf_op jit(solution)/shard_map/ppermute | solution.py:293
  15.5 2.8 %chunk_1_0.1 = (bf16[112,1024]{1,0:T(8,128)(2,1)S(1)}, bf16[96,1024]{1,0:T(8,128)(2,1)S(1)}, bf16[96,1024]{1,0:T(8,128)(2,1)S(1)}, f32[192,256]{1,0:T(8,128)S(1)}, f32[192,128]{1,0:T(8,128)S(1)}) custom-call(bf16[112,1024]{1,0:T(8,128)(2,1)S(1)} %collective-permute-done.1.x_ref, f32[1,1024]{1,0:T(1,128)S(1)} %get-tuple-element.36.gain_ref, ...), custom_call_target="tpu_custom_call" | custom-call | tf_op jit(solution)/shard_map/chunk_1_0/pallas_call | solution.py:366
  18.3 0.1 collective-permute-start.3
  18.4 0.1 collective-permute-done.x_ref
  18.5 3.3 %chunk_1_1.1 = (bf16[96,1024]{1,0:T(8,128)(2,1)S(1)}, bf16[96,1024]{1,0:T(8,128)(2,1)}, bf16[96,1024]{1,0:T(8,128)(2,1)}) custom-call(bf16[96,1024]{1,0:T(8,128)(2,1)S(1)} %collective-permute-done.x_ref, f32[1,1024]{1,0:T(1,128)S(1)} %get-tuple-element.36.gain_ref, bf16[1024,2048]{1,0:T(8,128)(2,1)S(1)} %get-tuple-element.37.wq_ref, ...), custom_call_target="tpu_custom_call" | custom-call | tf_op jit(solution)/shard_map/chunk_1_1/pallas_call | solution.py:366
  21.8 0.0 collective-permute-start.2
  21.8 4.7 %collective-permute-done.3.x_ref = bf16[112,1024]{1,0:T(8,128)(2,1)S(1)} collective-permute-done((bf16[112,1024]{1,0:T(8,128)(2,1)S(1)}, bf16[112,1024]{1,0:T(8,128)(2,1)S(1)}, u32[]{:S(2)}, u32[]{:S(2)}) %collective-permute-start.3) | collective-permute-done | bytes 229408 | tf_op jit(solution)/shard_map/ppermute | solution.py:293
  26.5 2.8 %chunk_2_0.1 = (bf16[112,1024]{1,0:T(8,128)(2,1)S(1)}, bf16[96,1024]{1,0:T(8,128)(2,1)S(1)}, bf16[96,1024]{1,0:T(8,128)(2,1)S(1)}, f32[192,256]{1,0:T(8,128)S(1)}, f32[192,128]{1,0:T(8,128)S(1)}) custom-call(bf16[112,1024]{1,0:T(8,128)(2,1)S(1)} %collective-permute-done.3.x_ref, f32[1,1024]{1,0:T(1,128)S(1)} %get-tuple-element.36.gain_ref, ...), custom_call_target="tpu_custom_call" | custom-call | tf_op jit(solution)/shard_map/chunk_2_0/pallas_call | solution.py:366
  29.3 0.1 collective-permute-start.5
  29.4 0.2 collective-permute-done.2.x_ref
  29.6 3.3 %chunk_2_1.1 = (bf16[96,1024]{1,0:T(8,128)(2,1)S(1)}, bf16[96,1024]{1,0:T(8,128)(2,1)}, bf16[96,1024]{1,0:T(8,128)(2,1)}) custom-call(bf16[96,1024]{1,0:T(8,128)(2,1)S(1)} %collective-permute-done.2.x_ref, f32[1,1024]{1,0:T(1,128)S(1)} %get-tuple-element.36.gain_ref, bf16[1024,2048]{1,0:T(8,128)(2,1)S(1)} %get-tuple-element.37.wq_ref, ...), custom_call_target="tpu_custom_call" | custom-call | tf_op jit(solution)/shard_map/chunk_2_1/pallas_call | solution.py:366
  32.9 0.0 collective-permute-start.4
  32.9 4.6 %collective-permute-done.5.x_ref = bf16[112,1024]{1,0:T(8,128)(2,1)S(1)} collective-permute-done((bf16[112,1024]{1,0:T(8,128)(2,1)S(1)}, bf16[112,1024]{1,0:T(8,128)(2,1)S(1)}, u32[]{:S(2)}, u32[]{:S(2)}) %collective-permute-start.5) | collective-permute-done | bytes 229408 | tf_op jit(solution)/shard_map/ppermute | solution.py:293
  37.5 2.8 %chunk_3_0.1 = (bf16[112,1024]{1,0:T(8,128)(2,1)S(1)}, bf16[96,1024]{1,0:T(8,128)(2,1)S(1)}, bf16[96,1024]{1,0:T(8,128)(2,1)S(1)}, f32[192,256]{1,0:T(8,128)S(1)}, f32[192,128]{1,0:T(8,128)S(1)}) custom-call(bf16[112,1024]{1,0:T(8,128)(2,1)S(1)} %collective-permute-done.5.x_ref, f32[1,1024]{1,0:T(1,128)S(1)} %get-tuple-element.36.gain_ref, ...), custom_call_target="tpu_custom_call" | custom-call | tf_op jit(solution)/shard_map/chunk_3_0/pallas_call | solution.py:366
  40.3 0.4 collective-permute-done.4.x_ref
  40.7 3.5 %chunk_3_1.1 = bf16[1,192,1024]{2,1,0:T(8,128)(2,1)} custom-call(bf16[96,1024]{1,0:T(8,128)(2,1)S(1)} %collective-permute-done.4.x_ref, f32[1,1024]{1,0:T(1,128)S(1)} %get-tuple-element.36.gain_ref, bf16[1024,2048]{1,0:T(8,128)(2,1)S(1)} %get-tuple-element.37.wq_ref, bf16[1024,1024]{1,0:T(8,128)(2,1)S(1)} %get-tuple-element.38.wk_ref, ...), custom_call_target="tpu_custom_call" | custom-call | tf_op jit(solution)/shard_map/chunk_3_1/pallas_call | solution.py:366
Async XLA Ops:
  6.3 9.2 %collective-permute-start.1 = (bf16[112,1024]{1,0:T(8,128)(2,1)S(1)}, bf16[112,1024]{1,0:T(8,128)(2,1)S(1)}, u32[]{:S(2)}, u32[]{:S(2)}) collective-permute-start(bf16[112,1024]{1,0:T(8,128)(2,1)S(1)} %get-tuple-element.46), channel_id=1, source_target_pairs={{0,1},{1,2},{2,3},{3,4},{4,5},{5,6},{6,7},{7,8},{8,9},{9,10},{10,1... | collective-permute-start | bytes 688136 | tf_op jit(solution)/shard_map/ppermute | solution.py:293
  10.1 8.4 %collective-permute-start = (bf16[96,1024]{1,0:T(8,128)(2,1)S(1)}, bf16[96,1024]{1,0:T(8,128)(2,1)S(1)}, u32[]{:S(2)}, u32[]{:S(2)}) collective-permute-start(bf16[96,1024]{1,0:T(8,128)(2,1)S(1)} %get-tuple-element.45), channel_id=1, source_target_pairs={{0,1},{1,2},{2,3},{3,4},{4,5},{5,6},{6,7},{7,8},{8,9},{9,10},{10,1... | collective-permute-start | bytes 589832 | tf_op jit(solution)/shard_map/ppermute | solution.py:293
  18.3 8.2 %collective-permute-start.3 = (bf16[112,1024]{1,0:T(8,128)(2,1)S(1)}, bf16[112,1024]{1,0:T(8,128)(2,1)S(1)}, u32[]{:S(2)}, u32[]{:S(2)}) collective-permute-start(bf16[112,1024]{1,0:T(8,128)(2,1)S(1)} %get-tuple-element.53), channel_id=1, source_target_pairs={{0,1},{1,2},{2,3},{3,4},{4,5},{5,6},{6,7},{7,8},{8,9},{9,10},{10,1... | collective-permute-start | bytes 688136 | tf_op jit(solution)/shard_map/ppermute | solution.py:293
  21.8 7.8 %collective-permute-start.2 = (bf16[96,1024]{1,0:T(8,128)(2,1)S(1)}, bf16[96,1024]{1,0:T(8,128)(2,1)S(1)}, u32[]{:S(2)}, u32[]{:S(2)}) collective-permute-start(bf16[96,1024]{1,0:T(8,128)(2,1)S(1)} %get-tuple-element.52), channel_id=1, source_target_pairs={{0,1},{1,2},{2,3},{3,4},{4,5},{5,6},{6,7},{7,8},{8,9},{9,10},{10,1... | collective-permute-start | bytes 589832 | tf_op jit(solution)/shard_map/ppermute | solution.py:293
  29.3 8.2 %collective-permute-start.5 = (bf16[112,1024]{1,0:T(8,128)(2,1)S(1)}, bf16[112,1024]{1,0:T(8,128)(2,1)S(1)}, u32[]{:S(2)}, u32[]{:S(2)}) collective-permute-start(bf16[112,1024]{1,0:T(8,128)(2,1)S(1)} %get-tuple-element.59), channel_id=1, source_target_pairs={{0,1},{1,2},{2,3},{3,4},{4,5},{5,6},{6,7},{7,8},{8,9},{9,10},{10,1... | collective-permute-start | bytes 688136 | tf_op jit(solution)/shard_map/ppermute | solution.py:293
  32.9 7.8 %collective-permute-start.4 = (bf16[96,1024]{1,0:T(8,128)(2,1)S(1)}, bf16[96,1024]{1,0:T(8,128)(2,1)S(1)}, u32[]{:S(2)}, u32[]{:S(2)}) collective-permute-start(bf16[96,1024]{1,0:T(8,128)(2,1)S(1)} %get-tuple-element.58), channel_id=1, source_target_pairs={{0,1},{1,2},{2,3},{3,4},{4,5},{5,6},{6,7},{7,8},{8,9},{9,10},{10,1... | collective-permute-start | bytes 589832 | tf_op jit(solution)/shard_map/ppermute | solution.py:293
